TPU v7x, 32 devices: a whole 2x2x4 slice. The times are simulated.
32 devices in a mesh: aa: 4 (over y, x), ba: 4 (over z), col: 2 (over core).
Axes of the slice: x: 2, y: 2, z: 4, core: 2. Of those that a mesh axis runs over, the one named last changes fastest.
Arguments:
- tensor: bfloat16 [1024, 512, 256], P('aa', 'ba', 'col'), may hold values from -6 to 6
- factor_two: bfloat16 [512, 64], P('ba'), may hold values from -0.25 to 0.25
- factor_three: bfloat16 [256, 64], P('col'), may hold values from -0.375 to 0.375
Outputs:
- gram: float32 [1024, 1024], P('aa', ('ba', 'col'))
All inputs are finite; a program needn't handle non-finite values.
Results may differ from a plain program's by a relative error of at most 0.008.
Values sent between devices are 32-bit elements; how exact they have to be, the bound alone decides.
No kernel may reach another device: no remote copies, remote signals or barrier semaphores. Data moves between devices by JAX's collectives and lax.ppermute only.
A program may use at most 64 MiB of HBM per device.

v0:
```python
import jax
import jax.numpy as jnp
from jax import lax
from jax.sharding import PartitionSpec as P


def body(tensor, factor_two, factor_three):
    rank = factor_three.shape[1]
    local_rows = tensor.shape[0]
    local_two = tensor.shape[1]
    partial_value = jnp.einsum(
        "ijk,ks->jsi", tensor, factor_three, preferred_element_type=jnp.float32
    ).astype(jnp.bfloat16)
    flat_partial = partial_value.reshape(local_two, rank * local_rows)
    n_mid = lax.axis_size("ba")
    n_last = lax.axis_size("col")
    width = min(
        rank,
        (rank * rank // (n_mid * n_last) * lax.axis_size(("ba", "col")) + rank - 1) // rank + 1,
    )
    product = jnp.dot(factor_two.T, flat_partial, preferred_element_type=jnp.float32)
    product = product.reshape(width * rank, local_rows)
    columns_here = lax.psum_scatter(product, ("ba", "col"), scatter_dimension=0, tiled=True)
    scale = 1.0 / (rank * rank)
    gram_terms = jnp.dot(
        columns_here.T,
        lax.all_gather(columns_here, "aa", axis=1, tiled=True),
        precision=lax.Precision.HIGHEST,
        preferred_element_type=jnp.float32,
    )
    gram = lax.psum_scatter(gram_terms, ("ba", "col"), scatter_dimension=1, tiled=True) * scale
    return gram


def solution(mesh):
    return jax.shard_map(
        body,
        mesh=mesh,
        in_specs=(P("aa", "ba", "col"), P("ba", None), P("col", None)),
        out_specs=P("aa", ("ba", "col")),
        check_vma=False,
    )
```

profile of v0, /device:TPU:0, one launch (start us, length us, event | category | flops | bytes accessed | tf_op | source)
XLA Modules:
  0.0 158.2 jit_solution(10736559623507158199)
XLA Ops:
  6.5 0.0 copy-start
  6.5 0.0 reduce-scatter.3.cloned.1.call-start
  6.5 0.7 copy-done
  7.3 6.4 %convert_bitcast_fusion = bf16[128,64,256]{0,1,2:T(8,128)(2,1)S(1)} fusion(bf16[256,128,128]{2,1,0:T(8,128)(2,1)} %param.3, bf16[128,64]{0,1:T(8,128)(2,1)S(1)} %copy-done), kind=kOutput, calls=%fused_computation.1 | convolution fusion | flops 538968064 | bytes 12599296 | tf_op jit(solution)/shard_map/ijk,ks->jsi/dot_general | solution.py:11
  13.7 0.0 copy-start.1
  13.7 2.7 %copy.4 = bf16[128,64,256]{0,2,1:T(8,128)(2,1)S(1)} copy(bf16[128,64,256]{0,1,2:T(8,128)(2,1)S(1)} %convert_bitcast_fusion) | data formatting | bytes 8388608 | tf_op jit(solution)/shard_map/convert_element_type | solution.py:13
  16.4 0.0 copy-done.1
  16.4 3.6 %convolution_bitcast_fusion = f32[64,16384]{1,0:T(8,128)} fusion(bf16[128,16384]{0,1:T(8,128)(2,1)S(1)} %bitcast.13, bf16[128,64]{0,1:T(8,128)(2,1)S(1)} %copy-done.1), kind=kOutput, calls=%fused_computation | convolution fusion | flops 268435456 | bytes 8404992 | tf_op jit(solution)/shard_map/dot_general | solution.py:21
  19.9 4.9 %reshape.7 = f32[4096,256]{1,0:T(8,128)} reshape(f32[64,16384]{1,0:T(8,128)} %convolution_bitcast_fusion) | data formatting | bytes 8388608 | tf_op jit(solution)/shard_map/reshape | solution.py:22
  24.8 0.0 reduce-scatter.3.cloned.1.call-update
  24.8 0.0 all-gather.2.cloned.1.call-start
  24.9 52.8 %reduce-scatter.3.cloned.1.call-done = f32[512,256]{1,0:T(8,128)} async-done(((f32[4096,256]{1,0:T(8,128)}), f32[512,256]{1,0:T(8,128)}) %reduce-scatter.3.cloned.1.call-update) | async-done | bytes 524304 | tf_op jit(solution)/shard_map/reduce_scatter | solution.py:23
  77.7 0.0 all-gather.2.cloned.1.call-update
  77.7 0.0 reduce-scatter.5.cloned.1.call-start
  77.8 35.1 %all-gather.2.cloned.1.call-done = f32[512,1024]{1,0:T(8,128)} async-done(((f32[512,256]{1,0:T(8,128)}), f32[512,1024]{1,0:T(8,128)}) %all-gather.2.cloned.1.call-update) | async-done | bytes 2097168 | tf_op jit(solution)/shard_map/all_gather | solution.py:27
  112.9 4.6 %fusion.1 = f32[256,1024]{1,0:T(8,128)} fusion(f32[512,256]{1,0:T(8,128)} %reduce-scatter.3.cloned.1.call-done, f32[512,1024]{1,0:T(8,128)} %all-gather.2.cloned.1.call-done), kind=kOutput, calls=%fused_computation.4 | convolution fusion | flops 1610612736 | bytes 3670016 | tf_op jit(solution)/shard_map/dot_general | solution.py:25
  117.5 0.0 reduce-scatter.5.cloned.1.call-update
  117.5 32.6 %reduce-scatter.5.cloned.1.call-done = f32[256,128]{1,0:T(8,128)} async-done(((f32[256,1024]{1,0:T(8,128)}), f32[256,128]{1,0:T(8,128)}) %reduce-scatter.5.cloned.1.call-update) | async-done | bytes 131088 | tf_op jit(solution)/shard_map/reduce_scatter | solution.py:31
  150.1 1.6 broadcast_multiply_fusion
Async XLA Ops:
  6.5 0.7 copy-start
  6.5 71.2 %reduce-scatter.3.cloned.1.call-start = ((), (), s32[]{:S(2)}) async-start(), calls=%async_computation.2 | async-start | bytes 4718592 | tf_op jit(solution)/shard_map/reduce_scatter | solution.py:23
  13.7 2.7 %copy-start.1 = (bf16[128,64]{0,1:T(8,128)(2,1)S(1)}, bf16[128,64]{0,1:T(8,128)(2,1)}, u32[]{:S(2)}) copy-start(bf16[128,64]{0,1:T(8,128)(2,1)} %param.4) | copy-start | bytes 49156
  24.8 88.0 %all-gather.2.cloned.1.call-start = ((), (), s32[]{:S(2)}) async-start(), calls=%async_computation.3 | async-start | bytes 2621440 | tf_op jit(solution)/shard_map/all_gather | solution.py:27
  77.7 72.4 %reduce-scatter.5.cloned.1.call-start = ((), (), s32[]{:S(2)}) async-start(), calls=%async_computation.4 | async-start | bytes 1179648 | tf_op jit(solution)/shard_map/reduce_scatter | solution.py:31
Sparse Core Ops, SparseCore 0:
  25.0 52.6 reduce-scatter.2
  79.5 33.2 all-gather.1
  117.6 32.4 reduce-scatter.4
where the time goes:
time: 159 us; the launch traced here: 158 us
  waiting for transfers between devices  121 us (76%)
  matrix products  14.6 us (9%)
  between operations  13.1 us (8%)
  local copies, waits for them, and re-layouts  8.29 us (5%)
    reduce_scatter x1, waiting for transfers between devices, body(): lax.psum_scatter(product, ('ba', 'col'), scatter_dimension=0, tiled=True)  52.8 us
    all_gather x1, waiting for transfers between devices, body(): lax.all_gather(columns_here, 'aa', axis=1, tiled=True)  35.1 us
    reduce_scatter x1, waiting for transfers between devices, body(): lax.psum_scatter(gram_terms, ('ba', 'col'), scatter_dimension=1, tiled=True)  32.6 us
    dot_general x1, matrix products, body(): jnp.einsum('ijk,ks->jsi', tensor, factor_three, preferred_element_type=jn...  6.39 us
    reshape x1, local copies, waits for them, and re-layouts, body(): product = product.reshape(width * rank, local_rows)  4.87 us
    dot_general x1, matrix products, body(): jnp.dot(columns_here.T, lax.all_gather(columns_here, 'aa', axis=1, tiled=...  4.62 us
    dot_general x1, matrix products, body(): jnp.dot(factor_two.T, flat_partial, preferred_element_type=jnp.float32)  3.55 us
  transfers between devices with their start and end apart: 3, of which 3 were waited for; matrix products, arithmetic and copies ran while one was open for 0% of the time, Pallas kernels for 0%

commit v1 on v0

v1 whole, which is shorter than its diff:
```python
import functools

import jax
import jax.numpy as jnp
from jax import lax
from jax.experimental import pallas as pl
from jax.experimental.pallas import tpu as pltpu
from jax.sharding import PartitionSpec as P

UNIT = 16
HALF = UNIT // 2
CHUNKS = (3, 3, 2)


def reversed_bits(value, count):
    return sum(((value >> k) & 1) << (count - 1 - k) for k in range(count))


def bits_of(n):
    return n.bit_length() - 1


def exchange(x, axis, distance):
    n = lax.axis_size(axis)
    return lax.ppermute(x, axis, [(i, i ^ distance) for i in range(n)])


def project_kernel(place, n_col, n_mid, tensor_ref, two_ref, three_ref, out_ref, two_s, three_s):
    rank = three_ref.shape[0]
    block = rank // n_mid

    @pl.when((pl.program_id(0) == 0) & (pl.program_id(1) == 0))
    def _():
        wide = two_ref[...].astype(jnp.float32)
        out_ref[0, :, : wide.shape[1]] = wide
        rows = []
        for position in range(n_mid):
            at = place[1] ^ reversed_bits(n_mid - 1 - position, bits_of(n_mid))
            rows.append(out_ref[0, pl.ds(pl.multiple_of(at * block, block), block), : wide.shape[1]])
        two_s[...] = jnp.concatenate(rows, axis=0).astype(jnp.bfloat16)
        three = three_ref[...]
        zero = jnp.zeros_like(three)
        three_s[...] = jnp.concatenate(
            [jnp.concatenate([three, zero], axis=1), jnp.concatenate([zero, three], axis=1)], axis=0
        )

    values = tensor_ref[...]
    _, n_two, n_three = values.shape
    pairs = jnp.concatenate([values[:HALF], values[HALF:]], axis=2).reshape(HALF * n_two, 2 * n_three)
    partial_value = lax.dot_general(
        pairs, three_s[...], (((1,), (1,)), ((), ())), preferred_element_type=jnp.float32
    ).astype(jnp.bfloat16)
    partial_value = partial_value.reshape(HALF, n_two, 2 * rank)
    wide = jnp.concatenate([partial_value[p] for p in range(HALF)], axis=1)
    out_ref[0] = jnp.dot(two_s[...], wide, preferred_element_type=jnp.float32)


def project(place, tensor, two_t, three_t, first, count, n_col, n_mid, per_core):
    rows, n_two, n_three = tensor.shape
    rank = two_t.shape[0]
    width = UNIT * rank

    def block_at(position, unit, place):
        core = place[0]
        for p in range(n_col):
            flip = reversed_bits(n_col - 1 - p, bits_of(n_col))
            core = jnp.where(position == p, place[0] ^ flip, core)
        at = (first + unit) * UNIT
        h, t = at // per_core, at % per_core
        return (h * n_col * per_core + core * per_core + t) // UNIT

    return pl.pallas_call(
        lambda place, *refs: project_kernel(place, n_col, n_mid, *refs),
        out_shape=jax.ShapeDtypeStruct((n_col, rank, count * width), jnp.float32),
        grid_spec=pltpu.PrefetchScalarGridSpec(
            num_scalar_prefetch=1,
            grid=(n_col, count),
            in_specs=[
                pl.BlockSpec((UNIT, n_two, n_three), lambda p, u, place: (block_at(p, u, place), 0, 0)),
                pl.BlockSpec((rank, n_two), lambda p, u, place: (0, 0)),
                pl.BlockSpec((rank, n_three), lambda p, u, place: (0, 0)),
            ],
            out_specs=pl.BlockSpec((1, rank, width), lambda p, u, place: (p, 0, u)),
            scratch_shapes=[
                pltpu.VMEM((rank, n_two), jnp.bfloat16),
                pltpu.VMEM((2 * rank, 2 * n_three), jnp.bfloat16),
            ],
        ),
        name="project",
    )(place, tensor, two_t, three_t)


def turn_kernel(n_terms, *refs):
    terms, (out_ref, turned) = refs[:n_terms], refs[n_terms:]
    total = terms[0][0] if len(terms[0].shape) == 3 else terms[0][...]
    for term in terms[1:]:
        total = total + (term[0] if len(term.shape) == 3 else term[...])
    block, width = total.shape
    lanes = out_ref.shape[1] // (block // 2)
    for unit in range(width // (HALF * lanes)):
        for p in range(HALF):
            at = (unit * HALF + p) * lanes
            for g in range(block // 8):
                turned[pl.ds(g * 8 * HALF + p, 8, stride=HALF), :] = total[g * 8 : g * 8 + 8, at : at + lanes]
        low = lax.broadcasted_iota(jnp.int32, (HALF, lanes), 1) < lanes // 2
        for pair in range(block // 2):
            even = turned[2 * pair * HALF : (2 * pair + 1) * HALF, :]
            odd = turned[(2 * pair + 1) * HALF : (2 * pair + 2) * HALF, :]
            columns = slice(pair * lanes, (pair + 1) * lanes)
            out_ref[unit * UNIT : unit * UNIT + HALF, columns] = jnp.where(low, even, pltpu.roll(odd, lanes // 2, 1))
            out_ref[unit * UNIT + HALF : (unit + 1) * UNIT, columns] = jnp.where(low, pltpu.roll(even, lanes // 2, 1), odd)


def turn(terms, block, rank):
    width = terms[0].shape[-1]
    specs = []
    for term in terms:
        at = term.shape[-2] // block - 1
        if term.ndim == 3:
            specs.append(pl.BlockSpec((1, block, width), lambda i, last=term.shape[0] - 1, at=at: (last, at, 0)))
        else:
            specs.append(pl.BlockSpec((block, width), lambda i, at=at: (at, 0)))
    return pl.pallas_call(
        functools.partial(turn_kernel, len(terms)),
        out_shape=jax.ShapeDtypeStruct((width // rank, block * rank), jnp.float32),
        grid=(1,),
        in_specs=specs,
        out_specs=pl.BlockSpec((width // rank, block * rank), lambda i: (0, 0)),
        scratch_shapes=[pltpu.VMEM((block * HALF, 2 * rank), jnp.float32)],
        name="turn",
    )(*terms)


def split(value):
    high = value.astype(jnp.bfloat16)
    return high, (value - high.astype(jnp.float32)).astype(jnp.bfloat16)


def gram_kernel(place, starts, n_aa, n_col, n_mid, per_core, *refs):
    n_chunks = len(starts)
    rows_in = refs[: n_chunks * n_col]
    others_in = refs[n_chunks * n_col : n_chunks * (n_col + n_aa - 1)]
    out_ref, left, left_low, right, right_low = refs[n_chunks * (n_col + n_aa - 1) :]
    for distance in range(n_col):
        core = place[0] ^ distance
        for k, start in enumerate(starts):
            ref = rows_in[k * n_col + distance]
            for unit in range(ref.shape[0] // UNIT):
                high, low = split(ref[unit * UNIT : (unit + 1) * UNIT, :])
                at = (start + unit) * UNIT
                row = (at // per_core) * n_col * per_core + core * per_core + at % per_core
                where = pl.ds(pl.multiple_of(row, UNIT), UNIT)
                left[where, :], left_low[where, :] = high, low
                if distance == 0:
                    right[0, at : at + UNIT, :], right_low[0, at : at + UNIT, :] = high, low
    for distance in range(1, n_aa):
        for k, start in enumerate(starts):
            ref = others_in[k * (n_aa - 1) + distance - 1]
            where = slice(start * UNIT, start * UNIT + ref.shape[0])
            right[distance, where, :], right_low[distance, where, :] = split(ref[...])
    scale = 1.0 / (n_mid * left.shape[1])
    share = n_mid // n_aa
    dot = functools.partial(
        lax.dot_general, dimension_numbers=(((1,), (1,)), ((), ())), preferred_element_type=jnp.float32
    )
    for distance in range(n_mid):
        goal = place[1] ^ distance
        block = (goal // share) ^ place[2]
        rows = pl.ds(pl.multiple_of((goal % share) * per_core, UNIT), per_core)
        high, low = right[block, rows, :], right_low[block, rows, :]
        value = dot(left[...], high) + (dot(left[...], low) + dot(left_low[...], high))
        out_ref[distance] = value * scale


def gram_terms(place, own, others, starts, n_aa, n_col, n_mid, per_core, local_rows):
    depth = own[0].shape[1]
    held = n_mid // n_aa * per_core
    n_in = len(own) + len(others)
    return pl.pallas_call(
        lambda place, *refs: gram_kernel(place, starts, n_aa, n_col, n_mid, per_core, *refs),
        out_shape=jax.ShapeDtypeStruct((n_mid, local_rows, per_core), jnp.float32),
        in_specs=[pl.BlockSpec(memory_space=pltpu.SMEM)] + [pl.BlockSpec(memory_space=pltpu.VMEM)] * n_in,
        out_specs=pl.BlockSpec(memory_space=pltpu.VMEM),
        scratch_shapes=[pltpu.VMEM((local_rows, depth), jnp.bfloat16)] * 2
        + [pltpu.VMEM((n_aa, held, depth), jnp.bfloat16)] * 2,
        compiler_params=pltpu.CompilerParams(vmem_limit_bytes=40 * 1024 * 1024),
        name="gram_terms",
    )(place, *own, *others)


def body(tensor, factor_two, factor_three):
    n_aa, n_mid, n_col = (lax.axis_size(name) for name in ("aa", "ba", "col"))
    rank = factor_three.shape[1]
    local_rows = tensor.shape[0]
    per_core = local_rows * n_aa // (n_mid * n_col)
    units = local_rows // n_col // UNIT
    bounds = [0]
    for k in range(len(CHUNKS)):
        bounds.append(round(units * sum(CHUNKS[: k + 1]) / sum(CHUNKS)))
    spans = [(a, b) for a, b in zip(bounds, bounds[1:]) if b > a]
    block = rank // n_mid
    place = jnp.stack([lax.axis_index("col"), lax.axis_index("ba"), lax.axis_index("aa")]).astype(jnp.int32)
    two_t, three_t = factor_two.T, factor_three.T

    own, others = [], []
    for first, end in spans:
        product = project(place, tensor, two_t, three_t, first, end - first, n_col, n_mid, per_core)
        terms = [product]
        size = n_col
        for k in range(bits_of(n_col)):
            size //= 2
            send = sum(term[-2 * size : -size] for term in terms)
            terms.append(exchange(send, "col", 1 << k))
        terms = [term[-1] for term in terms]
        size = rank
        for k in range(bits_of(n_mid)):
            size //= 2
            send = sum(term[-2 * size :][:size] for term in terms)
            terms.append(exchange(send, "ba", 1 << k))
        mine = turn(terms, block, rank)
        own += [mine] + [exchange(mine, "col", d) for d in range(1, n_col)]
        others += [exchange(mine, "aa", d) for d in range(1, n_aa)]

    starts = [first for first, _ in spans]
    sums = gram_terms(place, own, others, starts, n_aa, n_col, n_mid, per_core, local_rows)
    gram = sums[0]
    for d in range(1, n_mid):
        gram = gram + exchange(sums[d], "ba", d)
    return gram


def solution(mesh):
    return jax.shard_map(
        body,
        mesh=mesh,
        in_specs=(P("aa", "ba", "col"), P("ba", None), P("col", None)),
        out_specs=P("aa", ("ba", "col")),
        check_vma=False,
    )
```

time: 159 us -> 124 us (0.78)
  waiting for transfers between devices: 121 us -> 50.4 us
  Pallas kernels: 0 us -> 27.9 us
  starting transfers between devices: 0.08 us -> 26.7 us
  matrix products: 14.6 us -> 0 us
  between operations: 13.1 us -> 0.11 us
  other arithmetic: 1.57 us -> 8.29 us
  local copies, waits for them, and re-layouts: 8.29 us -> 9.91 us
    reduce_scatter x2 -> x0, waiting for transfers between devices: 85.4 us -> none  [the longest x1 52.8 us: body(): lax.psum_scatter(product, ('ba', 'col'), scatter_dimension=0, tiled=True)]
    ppermute x0 -> x24, waiting for transfers between devices: none -> 50.4 us  [exchange(): return lax.ppermute(x, axis, [(i, i ^ distance) for i in range(n)])]
    all_gather x1 -> x0, waiting for transfers between devices: 35.1 us -> none  [body(): lax.all_gather(columns_here, 'aa', axis=1, tiled=True)]
    pallas_call x0 -> x7, Pallas kernels: none -> 27.9 us  [the longest x3 19.2 us: project(): pl.pallas_call(lambda place, *refs: project_kernel(place, n_col, n_mid, *...]
    ppermute x0 -> x24, starting transfers between devices: none -> 26.7 us  [exchange(): return lax.ppermute(x, axis, [(i, i ^ distance) for i in range(n)])]
    dot_general x3 -> x0, matrix products: 14.6 us -> none  [the longest x1 6.39 us: body(): jnp.einsum('ijk,ks->jsi', tensor, factor_three, preferred_element_type=jn...]
    add x0 -> x7, other arithmetic: none -> 7.65 us  [the longest x6 6.96 us: body(): send = sum((term[-2 * size:][:size] for term in terms))]
    slice x0 -> x3, local copies, waits for them, and re-layouts: none -> 6.89 us  [body(): send = sum((term[-2 * size:-size] for term in terms))]
  transfers between devices with their start and end apart: 3 -> 24, of which waited for: 3 -> 12; matrix products, arithmetic and copies ran while one was open for 0% -> 10% of each run, Pallas kernels for 0% -> 16%
where the time goes in v1:
time: 124 us; the launch traced here: 123 us
  waiting for transfers between devices  50.4 us (41%)
  Pallas kernels  27.9 us (22%)
  starting transfers between devices  26.7 us (22%)
  local copies, waits for them, and re-layouts  9.91 us (8%)
  other arithmetic  8.29 us (7%)
    ppermute x24, waiting for transfers between devices, exchange(): return lax.ppermute(x, axis, [(i, i ^ distance) for i in range(n)])  50.4 us
    ppermute x24, starting transfers between devices, exchange(): return lax.ppermute(x, axis, [(i, i ^ distance) for i in range(n)])  26.7 us
    pallas_call x3, Pallas kernels, project(): pl.pallas_call(lambda place, *refs: project_kernel(place, n_col, n_mid, *...  19.2 us
    add x6, other arithmetic, body(): send = sum((term[-2 * size:][:size] for term in terms))  6.96 us
    slice x3, local copies, waits for them, and re-layouts, body(): send = sum((term[-2 * size:-size] for term in terms))  6.89 us
    pallas_call x3, Pallas kernels, turn(): pl.pallas_call(functools.partial(turn_kernel, len(terms)), out_shape=jax....  5.99 us
    unnamed x26, local copies, waits for them, and re-layouts  2.99 us
    pallas_call x1, Pallas kernels, gram_terms(): pl.pallas_call(lambda place, *refs: gram_kernel(place, starts, n_aa, n_co...  2.71 us
  transfers between devices with their start and end apart: 24, of which 12 were waited for; matrix products, arithmetic and copies ran while one was open for 10% of the time, Pallas kernels for 16%

profile of v1, /device:TPU:0, one launch (start us, length us, event | category | flops | bytes accessed | tf_op | source)
XLA Modules:
  0.0 123.3 jit_solution(645132988251860707)
XLA Ops:
  0.6 5.3 %project.5 = f32[2,64,2048]{2,1,0:T(8,128)} custom-call(s32[3]{0:T(128)} %pad_add_fusion.place, bf16[256,128,128]{2,1,0:T(8,128)(2,1)} %refs_0_.5, bf16[64,128]{1,0:T(8,128)(2,1)} %bitcast.49, bf16[64,128]{1,0:T(8,128)(2,1)} %bitcast.52), custom_call_target="tpu_custom_call" | custom-call | tf_op jit(solution)/shard_map/project/pallas_call | solution.py:72
  5.9 2.1 %fusion.11 = (f32[1,64,2048]{2,1,0:T(8,128)S(1)}, f32[64,2048]{1,0:T(8,128)}) fusion(f32[2,64,2048]{2,1,0:T(8,128)} %project.5), kind=kLoop, calls=%fused_computation.28 | loop fusion | bytes 2097152 | tf_op jit(solution)/shard_map/slice | solution.py:212
  8.5 7.0 %project.3 = f32[2,64,3072]{2,1,0:T(8,128)} custom-call(s32[3]{0:T(128)} %pad_add_fusion.place, bf16[256,128,128]{2,1,0:T(8,128)(2,1)} %refs_0_.5, bf16[64,128]{1,0:T(8,128)(2,1)} %bitcast.50, bf16[64,128]{1,0:T(8,128)(2,1)} %bitcast.53), custom_call_target="tpu_custom_call" | custom-call | tf_op jit(solution)/shard_map/project/pallas_call | solution.py:72
  15.4 2.4 %fusion.10 = (f32[1,64,3072]{2,1,0:T(8,128)S(1)}, f32[64,3072]{1,0:T(8,128)}) fusion(f32[2,64,3072]{2,1,0:T(8,128)} %project.3), kind=kLoop, calls=%fused_computation.27 | loop fusion | bytes 3145728 | tf_op jit(solution)/shard_map/slice | solution.py:212
  17.9 6.9 %project.4 = f32[2,64,3072]{2,1,0:T(8,128)} custom-call(s32[3]{0:T(128)} %pad_add_fusion.place, bf16[256,128,128]{2,1,0:T(8,128)(2,1)} %refs_0_.5, bf16[64,128]{1,0:T(8,128)(2,1)} %bitcast.51, bf16[64,128]{1,0:T(8,128)(2,1)} %bitcast.54), custom_call_target="tpu_custom_call" | custom-call | tf_op jit(solution)/shard_map/project/pallas_call | solution.py:72
  26.0 3.1 %collective-permute-start.9 = (f32[32,2048]{1,0:T(8,128)S(1)}, f32[32,2048]{1,0:T(8,128)S(1)}, u32[]{:S(2)}, u32[]{:S(2)}) collective-permute-start(f32[32,2048]{1,0:T(8,128)S(1)} %fusion.2), channel_id=1, source_target_pairs={{0,2},{2,0},{4,6},{6,4},{1,3},{3,1},{5,7},{7,5},{8,10},{10,8},{12,... | collective-permute-start | bytes 786440 | tf_op jit(solution)/shard_map/ppermute | solution.py:25
  29.0 2.4 %fusion.9 = (f32[1,64,3072]{2,1,0:T(8,128)S(1)}, f32[64,3072]{1,0:T(8,128)}) fusion(f32[2,64,3072]{2,1,0:T(8,128)} %project.4), kind=kLoop, calls=%fused_computation.26 | loop fusion | bytes 3145728 | tf_op jit(solution)/shard_map/slice | solution.py:212
  31.5 4.0 %collective-permute-done.9.refs_2_ = f32[32,2048]{1,0:T(8,128)S(1)} collective-permute-done((f32[32,2048]{1,0:T(8,128)S(1)}, f32[32,2048]{1,0:T(8,128)S(1)}, u32[]{:S(2)}, u32[]{:S(2)}) %collective-permute-start.9) | collective-permute-done | bytes 262176 | tf_op jit(solution)/shard_map/ppermute | solution.py:25
  36.5 2.8 %collective-permute-start.10 = (f32[16,2048]{1,0:T(8,128)S(1)}, f32[16,2048]{1,0:T(8,128)S(1)}, u32[]{:S(2)}, u32[]{:S(2)}) collective-permute-start(f32[16,2048]{1,0:T(8,128)S(1)} %slice_add_fusion.7), channel_id=1, source_target_pairs={{0,4},{2,6},{4,0},{6,2},{1,5},{3,7},{5,1},{7,3},{8,12},{10,14},{12... | collective-permute-start | bytes 393224 | tf_op jit(solution)/shard_map/ppermute | solution.py:25
  44.1 9.2 %collective-permute-done.1.refs_2_ = f32[32,3072]{1,0:T(8,128)S(1)} collective-permute-done((f32[32,3072]{1,0:T(8,128)S(1)}, f32[32,3072]{1,0:T(8,128)S(1)}, u32[]{:S(2)}, u32[]{:S(2)}) %collective-permute-start.1) | collective-permute-done | bytes 393248 | tf_op jit(solution)/shard_map/ppermute | solution.py:25
  55.8 8.5 %collective-permute-done.5.refs_2_ = f32[32,3072]{1,0:T(8,128)S(1)} collective-permute-done((f32[32,3072]{1,0:T(8,128)S(1)}, f32[32,3072]{1,0:T(8,128)S(1)}, u32[]{:S(2)}, u32[]{:S(2)}) %collective-permute-start.5) | collective-permute-done | bytes 393248 | tf_op jit(solution)/shard_map/ppermute | solution.py:25
  70.7 2.1 %turn.3.refs_0_ = f32[48,1024]{1,0:T(8,128)} custom-call(f32[64,3072]{1,0:T(8,128)} %get-tuple-element.8.refs_0_, f32[64,3072]{1,0:T(8,128)} %bitcast.46, f32[32,3072]{1,0:T(8,128)} %copy-done.8, f32[16,3072]{1,0:T(8,128)} %copy-done.11), custom_call_target="tpu_custom_call" | custom-call | tf_op jit(solution)/shard_map/turn/pallas_call | solution.py:123
  73.0 2.5 %collective-permute-done.6.refs_3_ = f32[16,3072]{1,0:T(8,128)S(1)} collective-permute-done((f32[16,3072]{1,0:T(8,128)S(1)}, f32[16,3072]{1,0:T(8,128)S(1)}, u32[]{:S(2)}, u32[]{:S(2)}) %collective-permute-start.6) | collective-permute-done | bytes 196640 | tf_op jit(solution)/shard_map/ppermute | solution.py:25
  76.1 2.0 %turn.4.refs_2_ = f32[48,1024]{1,0:T(8,128)} custom-call(f32[64,3072]{1,0:T(8,128)} %get-tuple-element.6.refs_0_, f32[64,3072]{1,0:T(8,128)} %bitcast.47, f32[32,3072]{1,0:T(8,128)} %copy-done.7, f32[16,3072]{1,0:T(8,128)} %copy-done.10), custom_call_target="tpu_custom_call" | custom-call | tf_op jit(solution)/shard_map/turn/pallas_call | solution.py:123
  81.7 3.6 %collective-permute-done.19.refs_13_ = f32[32,1024]{1,0:T(8,128)S(1)} collective-permute-done((f32[32,1024]{1,0:T(8,128)S(1)}, f32[32,1024]{1,0:T(8,128)S(1)}, u32[]{:S(2)}, u32[]{:S(2)}) %collective-permute-start.19) | collective-permute-done | bytes 131104 | tf_op jit(solution)/shard_map/ppermute | solution.py:25
  86.9 2.3 %collective-permute-done.20.refs_14_ = f32[32,1024]{1,0:T(8,128)S(1)} collective-permute-done((f32[32,1024]{1,0:T(8,128)S(1)}, f32[32,1024]{1,0:T(8,128)S(1)}, u32[]{:S(2)}, u32[]{:S(2)}) %collective-permute-start.20) | collective-permute-done | bytes 131104 | tf_op jit(solution)/shard_map/ppermute | solution.py:25
  94.2 3.2 %collective-permute-done.13.refs_7_ = f32[48,1024]{1,0:T(8,128)S(1)} collective-permute-done((f32[48,1024]{1,0:T(8,128)S(1)}, f32[48,1024]{1,0:T(8,128)S(1)}, u32[]{:S(2)}, u32[]{:S(2)}) %collective-permute-start.13) | collective-permute-done | bytes 196640 | tf_op jit(solution)/shard_map/ppermute | solution.py:25
  98.0 3.3 %collective-permute-done.15.refs_9_ = f32[48,1024]{1,0:T(8,128)S(1)} collective-permute-done((f32[48,1024]{1,0:T(8,128)}, f32[48,1024]{1,0:T(8,128)S(1)}, u32[]{:S(2)}, u32[]{:S(2)}) %collective-permute-start.15) | collective-permute-done | bytes 196640 | tf_op jit(solution)/shard_map/ppermute | solution.py:25
  101.3 4.7 %collective-permute-done.16.refs_10_ = f32[48,1024]{1,0:T(8,128)S(1)} collective-permute-done((f32[48,1024]{1,0:T(8,128)}, f32[48,1024]{1,0:T(8,128)S(1)}, u32[]{:S(2)}, u32[]{:S(2)}) %collective-permute-start.16) | collective-permute-done | bytes 196640 | tf_op jit(solution)/shard_map/ppermute | solution.py:25
  107.0 2.7 %gram_terms.1 = f32[4,256,128]{2,1,0:T(8,128)S(1)} custom-call(s32[3]{0:T(128)S(1)} %copy-done.3, f32[48,1024]{1,0:T(8,128)S(1)} %copy-done, f32[48,1024]{1,0:T(8,128)S(1)} %collective-permute-done.3.refs_1_, f32[48,1024]{1,0:T(8,128)S(1)} %copy-done.1, f32[48,1024]{1,0:T(8,128)S(1)} %collective-permute-done.7.refs_3_, f32[32,1024]{1,0:T(8,128)S(1)} %copy-done.2, ...), custom_call_target="tpu_custom_call" | custom-call | tf_op jit(solution)/shard_map/gram_terms/pallas_call | solution.py:179
  109.7 2.3 %collective-permute-start.23 = (f32[256,128]{1,0:T(8,128)S(1)}, f32[256,128]{1,0:T(8,128)S(1)}, u32[]{:S(2)}, u32[]{:S(2)}) collective-permute-start(f32[256,128]{1,0:T(8,128)S(1)} %get-tuple-element.12), channel_id=1, source_target_pairs={{0,6},{2,4},{4,2},{6,0},{1,7},{3,5},{5,3},{7,1},{8,14},{10,12},{12... | collective-permute-start | bytes 393224 | tf_op jit(solution)/shard_map/ppermute | solution.py:25
  112.0 2.2 %collective-permute-start.21 = (f32[256,128]{1,0:T(8,128)S(1)}, f32[256,128]{1,0:T(8,128)S(1)}, u32[]{:S(2)}, u32[]{:S(2)}) collective-permute-start(f32[256,128]{1,0:T(8,128)S(1)} %get-tuple-element.11), channel_id=1, source_target_pairs={{0,2},{2,0},{4,6},{6,4},{1,3},{3,1},{5,7},{7,5},{8,10},{10,8},{12,... | collective-permute-start | bytes 393224 | tf_op jit(solution)/shard_map/ppermute | solution.py:25
  114.2 3.9 %collective-permute-done.23 = f32[256,128]{1,0:T(8,128)S(1)} collective-permute-done((f32[256,128]{1,0:T(8,128)S(1)}, f32[256,128]{1,0:T(8,128)S(1)}, u32[]{:S(2)}, u32[]{:S(2)}) %collective-permute-start.23) | collective-permute-done | bytes 131104 | tf_op jit(solution)/shard_map/ppermute | solution.py:25
  118.1 4.6 %collective-permute-done.22 = f32[256,128]{1,0:T(8,128)S(1)} collective-permute-done((f32[256,128]{1,0:T(8,128)S(1)}, f32[256,128]{1,0:T(8,128)S(1)}, u32[]{:S(2)}, u32[]{:S(2)}) %collective-permute-start.22) | collective-permute-done | bytes 131104 | tf_op jit(solution)/shard_map/ppermute | solution.py:25
  (69 shorter events, 30.2 us)
Async XLA Ops:
  8.0 16.8 %collective-permute-start.8 = (f32[1,64,2048]{2,1,0:T(8,128)S(1)}, f32[1,64,2048]{2,1,0:T(8,128)S(1)}, u32[]{:S(2)}, u32[]{:S(2)}) collective-permute-start(f32[1,64,2048]{2,1,0:T(8,128)S(1)} %get-tuple-element.9), channel_id=1, source_target_pairs={{0,1},{1,0},{2,3},{3,2},{4,5},{5,4},{6,7},{7,6},{8,9},{9,8},{10,11... | collective-permute-start | bytes 1572872 | tf_op jit(solution)/shard_map/ppermute | solution.py:25
  17.8 21.5 %collective-permute-start = (f32[1,64,3072]{2,1,0:T(8,128)S(1)}, f32[1,64,3072]{2,1,0:T(8,128)S(1)}, u32[]{:S(2)}, u32[]{:S(2)}) collective-permute-start(f32[1,64,3072]{2,1,0:T(8,128)S(1)} %get-tuple-element.7), channel_id=1, source_target_pairs={{0,1},{1,0},{2,3},{3,2},{4,5},{5,4},{6,7},{7,6},{8,9},{9,8},{10,11... | collective-permute-start | bytes 2359304 | tf_op jit(solution)/shard_map/ppermute | solution.py:25
  26.0 9.6 %collective-permute-start.9 = (f32[32,2048]{1,0:T(8,128)S(1)}, f32[32,2048]{1,0:T(8,128)S(1)}, u32[]{:S(2)}, u32[]{:S(2)}) collective-permute-start(f32[32,2048]{1,0:T(8,128)S(1)} %fusion.2), channel_id=1, source_target_pairs={{0,2},{2,0},{4,6},{6,4},{1,3},{3,1},{5,7},{7,5},{8,10},{10,8},{12,... | collective-permute-start | bytes 786440 | tf_op jit(solution)/shard_map/ppermute | solution.py:25
  31.5 10.9 %collective-permute-start.4 = (f32[1,64,3072]{2,1,0:T(8,128)S(1)}, f32[1,64,3072]{2,1,0:T(8,128)S(1)}, u32[]{:S(2)}, u32[]{:S(2)}) collective-permute-start(f32[1,64,3072]{2,1,0:T(8,128)S(1)} %get-tuple-element.5), channel_id=1, source_target_pairs={{0,1},{1,0},{2,3},{3,2},{4,5},{5,4},{6,7},{7,6},{8,9},{9,8},{10,11... | collective-permute-start | bytes 2359304 | tf_op jit(solution)/shard_map/ppermute | solution.py:25
  36.5 29.3 %collective-permute-start.10 = (f32[16,2048]{1,0:T(8,128)S(1)}, f32[16,2048]{1,0:T(8,128)S(1)}, u32[]{:S(2)}, u32[]{:S(2)}) collective-permute-start(f32[16,2048]{1,0:T(8,128)S(1)} %slice_add_fusion.7), channel_id=1, source_target_pairs={{0,4},{2,6},{4,0},{6,2},{1,5},{3,7},{5,1},{7,3},{8,12},{10,14},{12... | collective-permute-start | bytes 393224 | tf_op jit(solution)/shard_map/ppermute | solution.py:25
  40.7 12.6 %collective-permute-start.1 = (f32[32,3072]{1,0:T(8,128)S(1)}, f32[32,3072]{1,0:T(8,128)S(1)}, u32[]{:S(2)}, u32[]{:S(2)}) collective-permute-start(f32[32,3072]{1,0:T(8,128)S(1)} %fusion.1), channel_id=1, source_target_pairs={{0,2},{2,0},{4,6},{6,4},{1,3},{3,1},{5,7},{7,5},{8,10},{10,8},{12,... | collective-permute-start | bytes 1179656 | tf_op jit(solution)/shard_map/ppermute | solution.py:25
  43.6 20.7 %collective-permute-start.5 = (f32[32,3072]{1,0:T(8,128)S(1)}, f32[32,3072]{1,0:T(8,128)S(1)}, u32[]{:S(2)}, u32[]{:S(2)}) collective-permute-start(f32[32,3072]{1,0:T(8,128)S(1)} %fusion), channel_id=1, source_target_pairs={{0,2},{2,0},{4,6},{6,4},{1,3},{3,1},{5,7},{7,5},{8,10},{10,8},{12,... | collective-permute-start | bytes 1179656 | tf_op jit(solution)/shard_map/ppermute | solution.py:25
  54.4 15.5 %collective-permute-start.2 = (f32[16,3072]{1,0:T(8,128)S(1)}, f32[16,3072]{1,0:T(8,128)S(1)}, u32[]{:S(2)}, u32[]{:S(2)}) collective-permute-start(f32[16,3072]{1,0:T(8,128)S(1)} %slice_add_fusion.5), channel_id=1, source_target_pairs={{0,4},{2,6},{4,0},{6,2},{1,5},{3,7},{5,1},{7,3},{8,12},{10,14},{12... | collective-permute-start | bytes 589832 | tf_op jit(solution)/shard_map/ppermute | solution.py:25
  65.4 10.0 %collective-permute-start.6 = (f32[16,3072]{1,0:T(8,128)S(1)}, f32[16,3072]{1,0:T(8,128)S(1)}, u32[]{:S(2)}, u32[]{:S(2)}) collective-permute-start(f32[16,3072]{1,0:T(8,128)S(1)} %slice_add_fusion.3), channel_id=1, source_target_pairs={{0,4},{2,6},{4,0},{6,2},{1,5},{3,7},{5,1},{7,3},{8,12},{10,14},{12... | collective-permute-start | bytes 589832 | tf_op jit(solution)/shard_map/ppermute | solution.py:25
  68.4 11.2 %collective-permute-start.11 = (f32[32,1024]{1,0:T(8,128)}, f32[32,1024]{1,0:T(8,128)S(1)}, u32[]{:S(2)}, u32[]{:S(2)}) collective-permute-start(f32[32,1024]{1,0:T(8,128)} %turn.5.refs_4_), channel_id=1, source_target_pairs={{0,1},{1,0},{2,3},{3,2},{4,5},{5,4},{6,7},{7,6},{8,9},{9,8},{10,11... | collective-permute-start | bytes 393224 | tf_op jit(solution)/shard_map/ppermute | solution.py:25
  68.4 12.7 %collective-permute-start.18 = (f32[32,1024]{1,0:T(8,128)}, f32[32,1024]{1,0:T(8,128)S(1)}, u32[]{:S(2)}, u32[]{:S(2)}) collective-permute-start(f32[32,1024]{1,0:T(8,128)} %turn.5.refs_4_), channel_id=1, source_target_pairs={{0,8},{8,0},{16,24},{24,16},{1,9},{9,1},{17,25},{25,17},{2,10},{10... | collective-permute-start | bytes 393224 | tf_op jit(solution)/shard_map/ppermute | solution.py:25
  72.7 18.0 %collective-permute-start.3 = (f32[48,1024]{1,0:T(8,128)}, f32[48,1024]{1,0:T(8,128)S(1)}, u32[]{:S(2)}, u32[]{:S(2)}) collective-permute-start(f32[48,1024]{1,0:T(8,128)} %turn.3.refs_0_), channel_id=1, source_target_pairs={{0,1},{1,0},{2,3},{3,2},{4,5},{5,4},{6,7},{7,6},{8,9},{9,8},{10,11... | collective-permute-start | bytes 589832 | tf_op jit(solution)/shard_map/ppermute | solution.py:25
  78.2 13.2 %collective-permute-start.7 = (f32[48,1024]{1,0:T(8,128)}, f32[48,1024]{1,0:T(8,128)S(1)}, u32[]{:S(2)}, u32[]{:S(2)}) collective-permute-start(f32[48,1024]{1,0:T(8,128)} %turn.4.refs_2_), channel_id=1, source_target_pairs={{0,1},{1,0},{2,3},{3,2},{4,5},{5,4},{6,7},{7,6},{8,9},{9,8},{10,11... | collective-permute-start | bytes 589832 | tf_op jit(solution)/shard_map/ppermute | solution.py:25
  78.2 14.6 %collective-permute-start.12 = (f32[48,1024]{1,0:T(8,128)S(1)}, f32[48,1024]{1,0:T(8,128)S(1)}, u32[]{:S(2)}, u32[]{:S(2)}) collective-permute-start(f32[48,1024]{1,0:T(8,128)S(1)} %copy-done), channel_id=1, source_target_pairs={{0,8},{8,0},{16,24},{24,16},{1,9},{9,1},{17,25},{25,17},{2,10},{10... | collective-permute-start | bytes 589832 | tf_op jit(solution)/shard_map/ppermute | solution.py:25
  79.6 5.6 %collective-permute-start.19 = (f32[32,1024]{1,0:T(8,128)S(1)}, f32[32,1024]{1,0:T(8,128)S(1)}, u32[]{:S(2)}, u32[]{:S(2)}) collective-permute-start(f32[32,1024]{1,0:T(8,128)S(1)} %copy-done.2), channel_id=1, source_target_pairs={{0,16},{8,24},{16,0},{24,8},{1,17},{9,25},{17,1},{25,9},{2,18},{10... | collective-permute-start | bytes 393224 | tf_op jit(solution)/shard_map/ppermute | solution.py:25
  81.1 8.2 %collective-permute-start.20 = (f32[32,1024]{1,0:T(8,128)S(1)}, f32[32,1024]{1,0:T(8,128)S(1)}, u32[]{:S(2)}, u32[]{:S(2)}) collective-permute-start(f32[32,1024]{1,0:T(8,128)S(1)} %copy-done.2), channel_id=1, source_target_pairs={{0,24},{8,16},{16,8},{24,0},{1,25},{9,17},{17,9},{25,1},{2,26},{10... | collective-permute-start | bytes 393224 | tf_op jit(solution)/shard_map/ppermute | solution.py:25
  85.2 12.2 %collective-permute-start.13 = (f32[48,1024]{1,0:T(8,128)S(1)}, f32[48,1024]{1,0:T(8,128)S(1)}, u32[]{:S(2)}, u32[]{:S(2)}) collective-permute-start(f32[48,1024]{1,0:T(8,128)S(1)} %copy-done), channel_id=1, source_target_pairs={{0,16},{8,24},{16,0},{24,8},{1,17},{9,25},{17,1},{25,9},{2,18},{10... | collective-permute-start | bytes 589832 | tf_op jit(solution)/shard_map/ppermute | solution.py:25
  89.3 8.7 %collective-permute-start.14 = (f32[48,1024]{1,0:T(8,128)S(1)}, f32[48,1024]{1,0:T(8,128)S(1)}, u32[]{:S(2)}, u32[]{:S(2)}) collective-permute-start(f32[48,1024]{1,0:T(8,128)S(1)} %copy-done), channel_id=1, source_target_pairs={{0,24},{8,16},{16,8},{24,0},{1,25},{9,17},{17,9},{25,1},{2,26},{10... | collective-permute-start | bytes 589832 | tf_op jit(solution)/shard_map/ppermute | solution.py:25
  90.7 10.6 %collective-permute-start.15 = (f32[48,1024]{1,0:T(8,128)}, f32[48,1024]{1,0:T(8,128)S(1)}, u32[]{:S(2)}, u32[]{:S(2)}) collective-permute-start(f32[48,1024]{1,0:T(8,128)} %turn.4.refs_2_), channel_id=1, source_target_pairs={{0,8},{8,0},{16,24},{24,16},{1,9},{9,1},{17,25},{25,17},{2,10},{10... | collective-permute-start | bytes 589832 | tf_op jit(solution)/shard_map/ppermute | solution.py:25
  91.3 14.7 %collective-permute-start.16 = (f32[48,1024]{1,0:T(8,128)}, f32[48,1024]{1,0:T(8,128)S(1)}, u32[]{:S(2)}, u32[]{:S(2)}) collective-permute-start(f32[48,1024]{1,0:T(8,128)} %turn.4.refs_2_), channel_id=1, source_target_pairs={{0,16},{8,24},{16,0},{24,8},{1,17},{9,25},{17,1},{25,9},{2,18},{10... | collective-permute-start | bytes 589832 | tf_op jit(solution)/shard_map/ppermute | solution.py:25
  92.8 13.3 %collective-permute-start.17 = (f32[48,1024]{1,0:T(8,128)}, f32[48,1024]{1,0:T(8,128)S(1)}, u32[]{:S(2)}, u32[]{:S(2)}) collective-permute-start(f32[48,1024]{1,0:T(8,128)} %turn.4.refs_2_), channel_id=1, source_target_pairs={{0,24},{8,16},{16,8},{24,0},{1,25},{9,17},{17,9},{25,1},{2,26},{10... | collective-permute-start | bytes 589832 | tf_op jit(solution)/shard_map/ppermute | solution.py:25
  109.7 8.3 %collective-permute-start.23 = (f32[256,128]{1,0:T(8,128)S(1)}, f32[256,128]{1,0:T(8,128)S(1)}, u32[]{:S(2)}, u32[]{:S(2)}) collective-permute-start(f32[256,128]{1,0:T(8,128)S(1)} %get-tuple-element.12), channel_id=1, source_target_pairs={{0,6},{2,4},{4,2},{6,0},{1,7},{3,5},{5,3},{7,1},{8,14},{10,12},{12... | collective-permute-start | bytes 393224 | tf_op jit(solution)/shard_map/ppermute | solution.py:25
  112.0 10.6 %collective-permute-start.22 = (f32[256,128]{1,0:T(8,128)S(1)}, f32[256,128]{1,0:T(8,128)S(1)}, u32[]{:S(2)}, u32[]{:S(2)}) collective-permute-start(f32[256,128]{1,0:T(8,128)S(1)} %get-tuple-element.13), channel_id=1, source_target_pairs={{0,4},{2,6},{4,0},{6,2},{1,5},{3,7},{5,1},{7,3},{8,12},{10,14},{12... | collective-permute-start | bytes 393224 | tf_op jit(solution)/shard_map/ppermute | solution.py:25
  112.0 10.6 %collective-permute-start.21 = (f32[256,128]{1,0:T(8,128)S(1)}, f32[256,128]{1,0:T(8,128)S(1)}, u32[]{:S(2)}, u32[]{:S(2)}) collective-permute-start(f32[256,128]{1,0:T(8,128)S(1)} %get-tuple-element.11), channel_id=1, source_target_pairs={{0,2},{2,0},{4,6},{6,4},{1,3},{3,1},{5,7},{7,5},{8,10},{10,8},{12,... | collective-permute-start | bytes 393224 | tf_op jit(solution)/shard_map/ppermute | solution.py:25
  (13 other events, 142.8 us)

commit v2 on v0

v2 whole, which is shorter than its diff:
```python
import functools

import jax
import jax.numpy as jnp
from jax import lax
from jax.experimental import pallas as pl
from jax.experimental.pallas import tpu as pltpu
from jax.sharding import PartitionSpec as P

UNIT = 16
HALF = UNIT // 2
CHUNKS = (3, 3, 2)
VMEM = pl.BlockSpec(memory_space=pltpu.VMEM)
ANY = pl.BlockSpec(memory_space=pl.ANY)
PARAMS = pltpu.CompilerParams(vmem_limit_bytes=40 * 1024 * 1024)
COST = pl.CostEstimate(flops=1, bytes_accessed=1, transcendentals=0)
TOKEN = jax.ShapeDtypeStruct((8, 128), jnp.float32)


def reversed_bits(value, count):
    return sum(((value >> k) & 1) << (count - 1 - k) for k in range(count))


def bits_of(n):
    return n.bit_length() - 1


def exchange(x, axis, distance):
    n = lax.axis_size(axis)
    return lax.ppermute(x, axis, [(i, i ^ distance) for i in range(n)])


def project_kernel(n_mid, per_core, positions, spans, to_hbm, tensor, two_in, three_in, *refs):
    outs, (held, two_ref, three_ref, wide_s, two_s, three_s, sems, *results) = refs[: len(spans)], refs[len(spans) :]
    n_col = lax.axis_size("col")
    rank, n_two = two_ref.shape
    n_three = three_ref.shape[1]
    block = rank // n_mid
    pieces = [(s, p) for s in range(len(spans)) for p in range(len(positions))]

    copies, k = [], 0
    for s, p in pieces:
        core = lax.axis_index("col") ^ reversed_bits(n_col - 1 - positions[p], bits_of(n_col))
        first, count = spans[s]
        copies.append([])
        for at in range(first * UNIT, (first + count) * UNIT, UNIT):
            row = at // per_core * n_col * per_core + core * per_core + at % per_core
            rows = pl.ds(pl.multiple_of(row, UNIT), UNIT)
            copies[-1].append(pltpu.make_async_copy(tensor.at[rows], held.at[k], sems.at[k]))
            copies[-1][-1].start()
            k += 1
        if len(copies) == 1:
            factors = [
                pltpu.make_async_copy(two_in, two_ref, sems.at[sems.shape[0] - 2]),
                pltpu.make_async_copy(three_in, three_ref, sems.at[sems.shape[0] - 1]),
            ]
            for copy in factors:
                copy.start()
    for copy in factors:
        copy.wait()
    wide_s[...] = two_ref[...].astype(jnp.float32)
    blocks = []
    for position in range(n_mid):
        at = lax.axis_index("ba") ^ reversed_bits(n_mid - 1 - position, bits_of(n_mid))
        blocks.append(wide_s[pl.ds(pl.multiple_of(at * block, block), block), :])
    two_s[...] = jnp.concatenate(blocks, axis=0).astype(jnp.bfloat16)
    three = three_ref[...]
    zero = jnp.zeros_like(three)
    three_s[...] = jnp.concatenate(
        [jnp.concatenate([three, zero], axis=1), jnp.concatenate([zero, three], axis=1)], axis=0
    )
    k, flushes = 0, []
    for (s, p), arrivals in zip(pieces, copies):
        count = len(arrivals)
        for copy in arrivals:
            copy.wait()
        values = held[k : k + count]
        k += count
        pairs = jnp.concatenate([values[:, :HALF], values[:, HALF:]], axis=3)
        pairs = pairs.reshape(count * HALF * n_two, 2 * n_three)
        partial_value = lax.dot_general(
            pairs, three_s[...], (((1,), (1,)), ((), ())), preferred_element_type=jnp.float32
        ).astype(jnp.bfloat16)
        partial_value = partial_value.reshape(count * HALF, n_two, 2 * rank)
        wide = jnp.concatenate([partial_value[i] for i in range(count * HALF)], axis=1)
        product = jnp.dot(two_s[...], wide, preferred_element_type=jnp.float32)
        if to_hbm:
            results[s][p] = product
            at = k - count
            flushes.append(pltpu.make_async_copy(results[s].at[p], outs[s].at[p], sems.at[at]))
            flushes[-1].start()
        else:
            outs[s][p] = product
    for copy in flushes:
        copy.wait()


def project(tensor, two_t, three_t, positions, spans, n_mid, per_core, to_hbm):
    n_two, n_three = tensor.shape[1:]
    rank = two_t.shape[0]
    n_units = sum(len(positions) * count for _, count in spans)
    shapes = [(len(positions), rank, count * UNIT * rank) for _, count in spans]
    scratch = [
        pltpu.VMEM((n_units, UNIT, n_two, n_three), jnp.bfloat16),
        pltpu.VMEM((rank, n_two), jnp.bfloat16),
        pltpu.VMEM((rank, n_three), jnp.bfloat16),
        pltpu.VMEM((rank, n_two), jnp.float32),
        pltpu.VMEM((rank, n_two), jnp.bfloat16),
        pltpu.VMEM((2 * rank, 2 * n_three), jnp.bfloat16),
        pltpu.SemaphoreType.DMA((n_units + 2,)),
    ]
    if to_hbm:
        scratch += [pltpu.VMEM(shape, jnp.float32) for shape in shapes]
    return pl.pallas_call(
        functools.partial(project_kernel, n_mid, per_core, positions, spans, to_hbm),
        out_shape=tuple(jax.ShapeDtypeStruct(shape, jnp.float32) for shape in shapes),
        in_specs=[ANY] * 3,
        out_specs=[ANY if to_hbm else VMEM] * len(shapes),
        scratch_shapes=scratch,
        compiler_params=pltpu.CompilerParams(vmem_limit_bytes=(58 if to_hbm else 48) * 1024 * 1024),
        cost_estimate=COST,
        name="project",
    )(tensor, two_t, three_t)


def fold_kernel(keep, got, token, send_out, keep_out, token_out):
    half = keep.shape[0] // 2
    send_out[...] = keep[:half] + got[:half]
    keep_out[...] = keep[half:] + got[half:]
    token_out[...] = token[...]


def fold(keep, got, token):
    half = jax.ShapeDtypeStruct((keep.shape[0] // 2, *keep.shape[1:]), jnp.float32)
    return pl.pallas_call(
        fold_kernel,
        out_shape=(half, half, TOKEN),
        in_specs=[VMEM] * 3,
        out_specs=[VMEM] * 3,
        compiler_params=PARAMS,
        cost_estimate=COST,
        name="fold",
    )(keep, got, token)


def turn_kernel(keep, got, token, out_ref, token_out, turned):
    total = keep[...] + got[...]
    token_out[...] = token[...]
    block, width = total.shape
    lanes = out_ref.shape[1] // (block // 2)
    low = lax.broadcasted_iota(jnp.int32, (HALF, lanes), 1) < lanes // 2
    for unit in range(width // (HALF * lanes)):
        for p in range(HALF):
            at = (unit * HALF + p) * lanes
            for g in range(block // 8):
                turned[unit, pl.ds(g * 8 * HALF + p, 8, stride=HALF), :] = total[g * 8 : g * 8 + 8, at : at + lanes]
        for pair in range(block // 2):
            even = turned[unit, 2 * pair * HALF : (2 * pair + 1) * HALF, :]
            odd = turned[unit, (2 * pair + 1) * HALF : (2 * pair + 2) * HALF, :]
            columns = slice(pair * lanes, (pair + 1) * lanes)
            out_ref[unit * UNIT : unit * UNIT + HALF, columns] = jnp.where(low, even, pltpu.roll(odd, lanes // 2, 1))
            out_ref[unit * UNIT + HALF : (unit + 1) * UNIT, columns] = jnp.where(low, pltpu.roll(even, lanes // 2, 1), odd)


def turn(keep, got, token, rank):
    block, width = keep.shape
    return pl.pallas_call(
        turn_kernel,
        out_shape=(jax.ShapeDtypeStruct((width // rank, block * rank), jnp.float32), TOKEN),
        in_specs=[VMEM] * 3,
        out_specs=[VMEM] * 2,
        scratch_shapes=[pltpu.VMEM((width // rank // UNIT, block * HALF, 2 * rank), jnp.float32)],
        compiler_params=PARAMS,
        cost_estimate=COST,
        name="turn",
    )(keep, got, token)


def split(value):
    high = value.astype(jnp.bfloat16)
    return high, (value - high.astype(jnp.float32)).astype(jnp.bfloat16)


def gram_kernel(starts, n_aa, n_col, n_mid, per_core, *refs):
    place = [lax.axis_index(name) for name in ("col", "ba", "aa")]
    n_chunks = len(starts)
    rows_in = refs[: n_chunks * n_col]
    others_in = refs[n_chunks * n_col : n_chunks * (n_col + n_aa - 1)]
    outs = refs[n_chunks * (n_col + n_aa - 1) : n_chunks * (n_col + n_aa - 1) + n_mid]
    left, left_low, right, right_low = refs[n_chunks * (n_col + n_aa - 1) + n_mid :]
    for distance in range(n_col):
        core = place[0] ^ distance
        for k, start in enumerate(starts):
            ref = rows_in[k * n_col + distance]
            for unit in range(ref.shape[0] // UNIT):
                high, low = split(ref[unit * UNIT : (unit + 1) * UNIT, :])
                at = (start + unit) * UNIT
                row = (at // per_core) * n_col * per_core + core * per_core + at % per_core
                where = pl.ds(pl.multiple_of(row, UNIT), UNIT)
                left[where, :], left_low[where, :] = high, low
                if distance == 0:
                    right[0, at : at + UNIT, :], right_low[0, at : at + UNIT, :] = high, low
    for distance in range(1, n_aa):
        for k, start in enumerate(starts):
            ref = others_in[k * (n_aa - 1) + distance - 1]
            where = slice(start * UNIT, start * UNIT + ref.shape[0])
            right[distance, where, :], right_low[distance, where, :] = split(ref[...])
    scale = 1.0 / (n_mid * left.shape[1])
    share = n_mid // n_aa
    dot = functools.partial(
        lax.dot_general, dimension_numbers=(((1,), (1,)), ((), ())), preferred_element_type=jnp.float32
    )
    for distance in range(n_mid):
        goal = place[1] ^ distance
        block = (goal // share) ^ place[2]
        rows = pl.ds(pl.multiple_of((goal % share) * per_core, UNIT), per_core)
        high, low = right[block, rows, :], right_low[block, rows, :]
        value = dot(left[...], high) + (dot(left[...], low) + dot(left_low[...], high))
        outs[distance][...] = value * scale


def gram_terms(own, others, starts, n_aa, n_col, n_mid, per_core, local_rows):
    depth = own[0].shape[1]
    held = n_mid // n_aa * per_core
    return pl.pallas_call(
        functools.partial(gram_kernel, starts, n_aa, n_col, n_mid, per_core),
        out_shape=(jax.ShapeDtypeStruct((local_rows, per_core), jnp.float32),) * n_mid,
        in_specs=[VMEM] * (len(own) + len(others)),
        out_specs=[VMEM] * n_mid,
        scratch_shapes=[pltpu.VMEM((local_rows, depth), jnp.bfloat16)] * 2
        + [pltpu.VMEM((n_aa, held, depth), jnp.bfloat16)] * 2,
        compiler_params=PARAMS,
        name="gram_terms",
    )(*own, *others)


def body(tensor, factor_two, factor_three):
    n_aa, n_mid, n_col = (lax.axis_size(name) for name in ("aa", "ba", "col"))
    rank = factor_three.shape[1]
    local_rows = tensor.shape[0]
    per_core = local_rows * n_aa // (n_mid * n_col)
    units = local_rows // n_col // UNIT
    bounds = [0]
    for k in range(len(CHUNKS)):
        bounds.append(round(units * sum(CHUNKS[: k + 1]) / sum(CHUNKS)))
    spans = [(a, b - a) for a, b in zip(bounds, bounds[1:]) if b > a]
    n_chunks = len(spans)
    two_t, three_t = factor_two.T, factor_three.T
    token = jnp.zeros(TOKEN.shape, TOKEN.dtype)
    first_half, second_half = tuple(range(n_col // 2)), tuple(range(n_col // 2, n_col))

    sends = project(tensor, two_t, three_t, first_half, spans, n_mid, per_core, True)
    got = [exchange(send, "col", 1) for send in sends]
    keep = list(project(tensor, two_t, three_t, second_half, spans, n_mid, per_core, False))
    mine, own, others = [None] * n_chunks, [], []
    col_steps, mid_steps = bits_of(n_col), bits_of(n_mid)

    def over_col(k, token):
        for step in range(1, col_steps):
            send, keep[k], token = fold(keep[k], got[k], token)
            got[k] = exchange(send, "col", 1 << step)
        keep[k], got[k] = keep[k][0], got[k][0]
        return over_mid(k, 0, token)

    def over_mid(k, step, token):
        send, keep[k], token = fold(keep[k], got[k], token)
        got[k] = exchange(send, "ba", 1 << step)
        return token

    def finish(k, token):
        mine[k], token = turn(keep[k], got[k], token, rank)
        return token

    token = over_col(0, token)
    for k in range(1, n_chunks):
        if k >= 2:
            for step in range(1, mid_steps):
                token = over_mid(k - 2, step, token)
        token = over_col(k, token)
    for k in range(n_chunks):
        if k >= n_chunks - 2:
            for step in range(1, mid_steps):
                token = over_mid(k, step, token)
        if k >= 1:
            token = finish(k - 1, token)
    token = finish(n_chunks - 1, token)
    for k in range(n_chunks):
        own += [mine[k]] + [exchange(mine[k], "col", d) for d in range(1, n_col)]
        others += [exchange(mine[k], "aa", d) for d in range(1, n_aa)]

    starts = [first for first, _ in spans]
    sums = gram_terms(own, others, starts, n_aa, n_col, n_mid, per_core, local_rows)
    gram = sums[0]
    for d in range(1, n_mid):
        gram = gram + exchange(sums[d], "ba", d)
    return gram


def solution(mesh):
    return jax.shard_map(
        body,
        mesh=mesh,
        in_specs=(P("aa", "ba", "col"), P("ba", None), P("col", None)),
        out_specs=P("aa", ("ba", "col")),
        check_vma=False,
    )
```

time: 159 us -> 84.3 us (0.53)
  waiting for transfers between devices: 121 us -> 37.1 us
  starting transfers between devices: 0.08 us -> 32.7 us
  matrix products: 14.6 us -> 0 us
  Pallas kernels: 0 us -> 13.1 us
  between operations: 13.1 us -> 0.13 us
  local copies, waits for them, and re-layouts: 8.29 us -> 0.01 us
    reduce_scatter x2 -> x0, waiting for transfers between devices: 85.4 us -> none  [the longest x1 52.8 us: body(): lax.psum_scatter(product, ('ba', 'col'), scatter_dimension=0, tiled=True)]
    ppermute x0 -> x24, waiting for transfers between devices: none -> 37.1 us  [exchange(): return lax.ppermute(x, axis, [(i, i ^ distance) for i in range(n)])]
    all_gather x1 -> x0, waiting for transfers between devices: 35.1 us -> none  [body(): lax.all_gather(columns_here, 'aa', axis=1, tiled=True)]
    ppermute x0 -> x24, starting transfers between devices: none -> 32.7 us  [exchange(): return lax.ppermute(x, axis, [(i, i ^ distance) for i in range(n)])]
    dot_general x3 -> x0, matrix products: 14.6 us -> none  [the longest x1 6.39 us: body(): jnp.einsum('ijk,ks->jsi', tensor, factor_three, preferred_element_type=jn...]
    pallas_call x0 -> x12, Pallas kernels: none -> 13.1 us  [the longest x2 9.71 us: project(): pl.pallas_call(functools.partial(project_kernel, n_mid, per_core, positio...]
    reshape x1 -> x0, local copies, waits for them, and re-layouts: 4.87 us -> none  [body(): product = product.reshape(width * rank, local_rows)]
    convert_element_type x1 -> x0, local copies, waits for them, and re-layouts: 2.7 us -> none  [body(): partial_value = jnp.einsum('ijk,ks->jsi', tensor, factor_three, preferred...]
  transfers between devices with their start and end apart: 3 -> 24, of which waited for: 3 -> 10; matrix products, arithmetic and copies ran while one was open for 0% -> 0% of each run, Pallas kernels for 0% -> 7%
where the time goes in v2:
time: 84.3 us; the launch traced here: 83.7 us
  waiting for transfers between devices  37.1 us (44%)
  starting transfers between devices  32.7 us (39%)
  Pallas kernels  13.1 us (16%)
    ppermute x24, waiting for transfers between devices, exchange(): return lax.ppermute(x, axis, [(i, i ^ distance) for i in range(n)])  37.1 us
    ppermute x24, starting transfers between devices, exchange(): return lax.ppermute(x, axis, [(i, i ^ distance) for i in range(n)])  32.7 us
    pallas_call x2, Pallas kernels, project(): pl.pallas_call(functools.partial(project_kernel, n_mid, per_core, positio...  9.71 us
    pallas_call x1, Pallas kernels, gram_terms(): pl.pallas_call(functools.partial(gram_kernel, starts, n_aa, n_col, n_mid,...  2.15 us
  transfers between devices with their start and end apart: 24, of which 10 were waited for; matrix products, arithmetic and copies ran while one was open for 0% of the time, Pallas kernels for 7%

profile of v2, /device:TPU:0, one launch (start us, length us, event | category | flops | bytes accessed | tf_op | source)
XLA Modules:
  0.0 83.7 jit_solution(13674968743493945582)
XLA Ops:
  0.0 5.4 %project.3 = (f32[1,64,3072]{2,1,0:T(8,128)}, f32[1,64,3072]{2,1,0:T(8,128)}, f32[1,64,2048]{2,1,0:T(8,128)}) custom-call(bf16[256,128,128]{2,1,0:T(8,128)(2,1)} %tensor.3, bf16[64,128]{1,0:T(8,128)(2,1)} %bitcast.14, bf16[64,128]{1,0:T(8,128)(2,1)} %bitcast.16), custom_call_target="tpu_custom_call" | custom-call | flops 1 | bytes 1 | tf_op jit(solution)/shard_map/project/pallas_call | solution.py:114
  6.6 4.3 %project.2 = (f32[1,64,3072]{2,1,0:T(8,128)S(1)}, f32[1,64,3072]{2,1,0:T(8,128)S(1)}, f32[1,64,2048]{2,1,0:T(8,128)S(1)}) custom-call(bf16[256,128,128]{2,1,0:T(8,128)(2,1)} %tensor.3, bf16[64,128]{1,0:T(8,128)(2,1)S(1)} %bitcast.15, bf16[64,128]{1,0:T(8,128)(2,1)S(1)} %bitcast.17), custom_call_target="tpu_custom_call" | custom-call | flops 1 | bytes 1 | tf_op jit(solution)/shard_map/project/pallas_call | solution.py:114
  11.0 2.6 %collective-permute-start.1 = (f32[32,3072]{1,0:T(8,128)S(1)}, f32[32,3072]{1,0:T(8,128)S(1)}, u32[]{:S(2)}, u32[]{:S(2)}) collective-permute-start(f32[32,3072]{1,0:T(8,128)S(1)} %get-tuple-element.41), channel_id=1, source_target_pairs={{0,2},{2,0},{4,6},{6,4},{1,3},{3,1},{5,7},{7,5},{8,10},{10,8},{12,... | collective-permute-start | bytes 1179656 | tf_op jit(solution)/shard_map/ppermute | solution.py:30
  13.8 9.8 %collective-permute-done.1.got = f32[32,3072]{1,0:T(8,128)S(1)} collective-permute-done((f32[32,3072]{1,0:T(8,128)S(1)}, f32[32,3072]{1,0:T(8,128)S(1)}, u32[]{:S(2)}, u32[]{:S(2)}) %collective-permute-start.1) | collective-permute-done | bytes 393248 | tf_op jit(solution)/shard_map/ppermute | solution.py:30
  23.6 3.0 %collective-permute-start.3 = (f32[16,3072]{1,0:T(8,128)S(1)}, f32[16,3072]{1,0:T(8,128)S(1)}, u32[]{:S(2)}, u32[]{:S(2)}) collective-permute-start(f32[16,3072]{1,0:T(8,128)S(1)} %get-tuple-element.47), channel_id=1, source_target_pairs={{0,4},{2,6},{4,0},{6,2},{1,5},{3,7},{5,1},{7,3},{8,12},{10,14},{12... | collective-permute-start | bytes 589832 | tf_op jit(solution)/shard_map/ppermute | solution.py:30
  26.7 1.6 %collective-permute-start.8 = (f32[32,2048]{1,0:T(8,128)S(1)}, f32[32,2048]{1,0:T(8,128)S(1)}, u32[]{:S(2)}, u32[]{:S(2)}) collective-permute-start(f32[32,2048]{1,0:T(8,128)S(1)} %get-tuple-element.59), channel_id=1, source_target_pairs={{0,2},{2,0},{4,6},{6,4},{1,3},{3,1},{5,7},{7,5},{8,10},{10,8},{12,... | collective-permute-start | bytes 786440 | tf_op jit(solution)/shard_map/ppermute | solution.py:30
  28.3 7.9 %collective-permute-done.4.got = f32[32,3072]{1,0:T(8,128)S(1)} collective-permute-done((f32[32,3072]{1,0:T(8,128)S(1)}, f32[32,3072]{1,0:T(8,128)S(1)}, u32[]{:S(2)}, u32[]{:S(2)}) %collective-permute-start.4) | collective-permute-done | bytes 393248 | tf_op jit(solution)/shard_map/ppermute | solution.py:30
  36.2 2.1 %collective-permute-start.7 = (f32[16,3072]{1,0:T(8,128)S(1)}, f32[16,3072]{1,0:T(8,128)S(1)}, u32[]{:S(2)}, u32[]{:S(2)}) collective-permute-start(f32[16,3072]{1,0:T(8,128)S(1)} %get-tuple-element.57), channel_id=1, source_target_pairs={{0,4},{2,6},{4,0},{6,2},{1,5},{3,7},{5,1},{7,3},{8,12},{10,14},{12... | collective-permute-start | bytes 589832 | tf_op jit(solution)/shard_map/ppermute | solution.py:30
  38.5 2.5 %collective-permute-start.14 = (f32[48,1024]{1,0:T(8,128)S(1)}, f32[48,1024]{1,0:T(8,128)S(1)}, u32[]{:S(2)}, u32[]{:S(2)}) collective-permute-start(f32[48,1024]{1,0:T(8,128)S(1)} %get-tuple-element.55.refs_0_), channel_id=1, source_target_pairs={{0,24},{8,16},{16,8},{24,0},{1,25},{9,17},{17,9},{25,1},{2,26},{10... | collective-permute-start | bytes 589832 | tf_op jit(solution)/shard_map/ppermute | solution.py:30
  42.1 3.7 %collective-permute-done.8.got = f32[32,2048]{1,0:T(8,128)S(1)} collective-permute-done((f32[32,2048]{1,0:T(8,128)S(1)}, f32[32,2048]{1,0:T(8,128)S(1)}, u32[]{:S(2)}, u32[]{:S(2)}) %collective-permute-start.8) | collective-permute-done | bytes 262176 | tf_op jit(solution)/shard_map/ppermute | solution.py:30
  45.8 2.7 %collective-permute-start.10 = (f32[16,2048]{1,0:T(8,128)S(1)}, f32[16,2048]{1,0:T(8,128)S(1)}, u32[]{:S(2)}, u32[]{:S(2)}) collective-permute-start(f32[16,2048]{1,0:T(8,128)S(1)} %get-tuple-element.64), channel_id=1, source_target_pairs={{0,4},{2,6},{4,0},{6,2},{1,5},{3,7},{5,1},{7,3},{8,12},{10,14},{12... | collective-permute-start | bytes 393224 | tf_op jit(solution)/shard_map/ppermute | solution.py:30
  48.7 2.5 %collective-permute-start.17 = (f32[48,1024]{1,0:T(8,128)S(1)}, f32[48,1024]{1,0:T(8,128)S(1)}, u32[]{:S(2)}, u32[]{:S(2)}) collective-permute-start(f32[48,1024]{1,0:T(8,128)S(1)} %get-tuple-element.62.refs_2_), channel_id=1, source_target_pairs={{0,24},{8,16},{16,8},{24,0},{1,25},{9,17},{17,9},{25,1},{2,26},{10... | collective-permute-start | bytes 589832 | tf_op jit(solution)/shard_map/ppermute | solution.py:30
  52.2 3.3 %collective-permute-done.10.got = f32[16,2048]{1,0:T(8,128)S(1)} collective-permute-done((f32[16,2048]{1,0:T(8,128)S(1)}, f32[16,2048]{1,0:T(8,128)S(1)}, u32[]{:S(2)}, u32[]{:S(2)}) %collective-permute-start.10) | collective-permute-done | bytes 131104 | tf_op jit(solution)/shard_map/ppermute | solution.py:30
  56.1 2.6 %collective-permute-start.20 = (f32[32,1024]{1,0:T(8,128)S(1)}, f32[32,1024]{1,0:T(8,128)S(1)}, u32[]{:S(2)}, u32[]{:S(2)}) collective-permute-start(f32[32,1024]{1,0:T(8,128)S(1)} %get-tuple-element.66.refs_4_), channel_id=1, source_target_pairs={{0,24},{8,16},{16,8},{24,0},{1,25},{9,17},{17,9},{25,1},{2,26},{10... | collective-permute-start | bytes 393224 | tf_op jit(solution)/shard_map/ppermute | solution.py:30
  59.3 0.7 collective-permute-done.16.refs_10_
  60.0 1.5 %collective-permute-start.18 = (f32[32,1024]{1,0:T(8,128)S(1)}, f32[32,1024]{1,0:T(8,128)S(1)}, u32[]{:S(2)}, u32[]{:S(2)}) collective-permute-start(f32[32,1024]{1,0:T(8,128)S(1)} %get-tuple-element.66.refs_4_), channel_id=1, source_target_pairs={{0,8},{8,0},{16,24},{24,16},{1,9},{9,1},{17,25},{25,17},{2,10},{10... | collective-permute-start | bytes 393224 | tf_op jit(solution)/shard_map/ppermute | solution.py:30
  61.5 1.6 %collective-permute-done.20.refs_14_ = f32[32,1024]{1,0:T(8,128)S(1)} collective-permute-done((f32[32,1024]{1,0:T(8,128)S(1)}, f32[32,1024]{1,0:T(8,128)S(1)}, u32[]{:S(2)}, u32[]{:S(2)}) %collective-permute-start.20) | collective-permute-done | bytes 131104 | tf_op jit(solution)/shard_map/ppermute | solution.py:30
  63.1 2.7 %collective-permute-done.19.refs_13_ = f32[32,1024]{1,0:T(8,128)S(1)} collective-permute-done((f32[32,1024]{1,0:T(8,128)S(1)}, f32[32,1024]{1,0:T(8,128)S(1)}, u32[]{:S(2)}, u32[]{:S(2)}) %collective-permute-start.19) | collective-permute-done | bytes 131104 | tf_op jit(solution)/shard_map/ppermute | solution.py:30
  66.0 2.1 %gram_terms.1 = (f32[256,128]{1,0:T(8,128)S(1)}, f32[256,128]{1,0:T(8,128)S(1)}, f32[256,128]{1,0:T(8,128)S(1)}, f32[256,128]{1,0:T(8,128)S(1)}) custom-call(f32[48,1024]{1,0:T(8,128)S(1)} %get-tuple-element.55.refs_0_, f32[48,1024]{1,0:T(8,128)S(1)} %collective-permute-done.6.refs_1_, f32[48,1024]{1,0:T(8,128)S(1)} %get-tuple-element.62.refs_2_, ...), custom_call_target="tpu_custom_call" | custom-call | tf_op jit(solution)/shard_map/gram_terms/pallas_call | solution.py:225
  68.2 5.2 %collective-permute-start.21 = (f32[256,128]{1,0:T(8,128)S(1)}, f32[256,128]{1,0:T(8,128)S(1)}, u32[]{:S(2)}, u32[]{:S(2)}) collective-permute-start(f32[256,128]{1,0:T(8,128)S(1)} %get-tuple-element.68), channel_id=1, source_target_pairs={{0,2},{2,0},{4,6},{6,4},{1,3},{3,1},{5,7},{7,5},{8,10},{10,8},{12,... | collective-permute-start | bytes 393224 | tf_op jit(solution)/shard_map/ppermute | solution.py:30
  73.4 2.4 %collective-permute-start.23 = (f32[256,128]{1,0:T(8,128)S(1)}, f32[256,128]{1,0:T(8,128)S(1)}, u32[]{:S(2)}, u32[]{:S(2)}) collective-permute-start(f32[256,128]{1,0:T(8,128)S(1)} %get-tuple-element.70), channel_id=1, source_target_pairs={{0,6},{2,4},{4,2},{6,0},{1,7},{3,5},{5,3},{7,1},{8,14},{10,12},{12... | collective-permute-start | bytes 393224 | tf_op jit(solution)/shard_map/ppermute | solution.py:30
  75.8 2.0 %collective-permute-done.21 = f32[256,128]{1,0:T(8,128)S(1)} collective-permute-done((f32[256,128]{1,0:T(8,128)S(1)}, f32[256,128]{1,0:T(8,128)S(1)}, u32[]{:S(2)}, u32[]{:S(2)}) %collective-permute-start.21) | collective-permute-done | bytes 131104 | tf_op jit(solution)/shard_map/ppermute | solution.py:30
  77.8 5.2 %collective-permute-done.22 = f32[256,128]{1,0:T(8,128)S(1)} collective-permute-done((f32[256,128]{1,0:T(8,128)S(1)}, f32[256,128]{1,0:T(8,128)S(1)}, u32[]{:S(2)}, u32[]{:S(2)}) %collective-permute-start.22) | collective-permute-done | bytes 131104 | tf_op jit(solution)/shard_map/ppermute | solution.py:30
  83.0 0.7 add_add_fusion
  (42 shorter events, 5.4 us)
Async XLA Ops:
  5.4 5.5 %collective-permute-start = (f32[1,64,3072]{2,1,0:T(8,128)}, f32[1,64,3072]{2,1,0:T(8,128)S(1)}, u32[]{:S(2)}, u32[]{:S(2)}) collective-permute-start(f32[1,64,3072]{2,1,0:T(8,128)} %get-tuple-element.39), channel_id=1, source_target_pairs={{0,1},{1,0},{2,3},{3,2},{4,5},{5,4},{6,7},{7,6},{8,9},{9,8},{10,11... | collective-permute-start | bytes 2359304 | tf_op jit(solution)/shard_map/ppermute | solution.py:30
  6.1 7.5 %collective-permute-start.2 = (f32[1,64,3072]{2,1,0:T(8,128)}, f32[1,64,3072]{2,1,0:T(8,128)S(1)}, u32[]{:S(2)}, u32[]{:S(2)}) collective-permute-start(f32[1,64,3072]{2,1,0:T(8,128)} %get-tuple-element.43), channel_id=1, source_target_pairs={{0,1},{1,0},{2,3},{3,2},{4,5},{5,4},{6,7},{7,6},{8,9},{9,8},{10,11... | collective-permute-start | bytes 2359304 | tf_op jit(solution)/shard_map/ppermute | solution.py:30
  6.2 20.5 %collective-permute-start.5 = (f32[1,64,2048]{2,1,0:T(8,128)}, f32[1,64,2048]{2,1,0:T(8,128)S(1)}, u32[]{:S(2)}, u32[]{:S(2)}) collective-permute-start(f32[1,64,2048]{2,1,0:T(8,128)} %get-tuple-element.51), channel_id=1, source_target_pairs={{0,1},{1,0},{2,3},{3,2},{4,5},{5,4},{6,7},{7,6},{8,9},{9,8},{10,11... | collective-permute-start | bytes 1572872 | tf_op jit(solution)/shard_map/ppermute | solution.py:30
  11.0 12.5 %collective-permute-start.1 = (f32[32,3072]{1,0:T(8,128)S(1)}, f32[32,3072]{1,0:T(8,128)S(1)}, u32[]{:S(2)}, u32[]{:S(2)}) collective-permute-start(f32[32,3072]{1,0:T(8,128)S(1)} %get-tuple-element.41), channel_id=1, source_target_pairs={{0,2},{2,0},{4,6},{6,4},{1,3},{3,1},{5,7},{7,5},{8,10},{10,8},{12,... | collective-permute-start | bytes 1179656 | tf_op jit(solution)/shard_map/ppermute | solution.py:30
  13.7 22.5 %collective-permute-start.4 = (f32[32,3072]{1,0:T(8,128)S(1)}, f32[32,3072]{1,0:T(8,128)S(1)}, u32[]{:S(2)}, u32[]{:S(2)}) collective-permute-start(f32[32,3072]{1,0:T(8,128)S(1)} %get-tuple-element.49), channel_id=1, source_target_pairs={{0,2},{2,0},{4,6},{6,4},{1,3},{3,1},{5,7},{7,5},{8,10},{10,8},{12,... | collective-permute-start | bytes 1179656 | tf_op jit(solution)/shard_map/ppermute | solution.py:30
  23.6 14.8 %collective-permute-start.3 = (f32[16,3072]{1,0:T(8,128)S(1)}, f32[16,3072]{1,0:T(8,128)S(1)}, u32[]{:S(2)}, u32[]{:S(2)}) collective-permute-start(f32[16,3072]{1,0:T(8,128)S(1)} %get-tuple-element.47), channel_id=1, source_target_pairs={{0,4},{2,6},{4,0},{6,2},{1,5},{3,7},{5,1},{7,3},{8,12},{10,14},{12... | collective-permute-start | bytes 589832 | tf_op jit(solution)/shard_map/ppermute | solution.py:30
  26.7 19.1 %collective-permute-start.8 = (f32[32,2048]{1,0:T(8,128)S(1)}, f32[32,2048]{1,0:T(8,128)S(1)}, u32[]{:S(2)}, u32[]{:S(2)}) collective-permute-start(f32[32,2048]{1,0:T(8,128)S(1)} %get-tuple-element.59), channel_id=1, source_target_pairs={{0,2},{2,0},{4,6},{6,4},{1,3},{3,1},{5,7},{7,5},{8,10},{10,8},{12,... | collective-permute-start | bytes 786440 | tf_op jit(solution)/shard_map/ppermute | solution.py:30
  36.2 9.6 %collective-permute-start.7 = (f32[16,3072]{1,0:T(8,128)S(1)}, f32[16,3072]{1,0:T(8,128)S(1)}, u32[]{:S(2)}, u32[]{:S(2)}) collective-permute-start(f32[16,3072]{1,0:T(8,128)S(1)} %get-tuple-element.57), channel_id=1, source_target_pairs={{0,4},{2,6},{4,0},{6,2},{1,5},{3,7},{5,1},{7,3},{8,12},{10,14},{12... | collective-permute-start | bytes 589832 | tf_op jit(solution)/shard_map/ppermute | solution.py:30
  38.5 10.2 %collective-permute-start.14 = (f32[48,1024]{1,0:T(8,128)S(1)}, f32[48,1024]{1,0:T(8,128)S(1)}, u32[]{:S(2)}, u32[]{:S(2)}) collective-permute-start(f32[48,1024]{1,0:T(8,128)S(1)} %get-tuple-element.55.refs_0_), channel_id=1, source_target_pairs={{0,24},{8,16},{16,8},{24,0},{1,25},{9,17},{17,9},{25,1},{2,26},{10... | collective-permute-start | bytes 589832 | tf_op jit(solution)/shard_map/ppermute | solution.py:30
  41.0 10.2 %collective-permute-start.13 = (f32[48,1024]{1,0:T(8,128)S(1)}, f32[48,1024]{1,0:T(8,128)S(1)}, u32[]{:S(2)}, u32[]{:S(2)}) collective-permute-start(f32[48,1024]{1,0:T(8,128)S(1)} %get-tuple-element.55.refs_0_), channel_id=1, source_target_pairs={{0,16},{8,24},{16,0},{24,8},{1,17},{9,25},{17,1},{25,9},{2,18},{10... | collective-permute-start | bytes 589832 | tf_op jit(solution)/shard_map/ppermute | solution.py:30
  41.5 10.2 %collective-permute-start.12 = (f32[48,1024]{1,0:T(8,128)S(1)}, f32[48,1024]{1,0:T(8,128)S(1)}, u32[]{:S(2)}, u32[]{:S(2)}) collective-permute-start(f32[48,1024]{1,0:T(8,128)S(1)} %get-tuple-element.55.refs_0_), channel_id=1, source_target_pairs={{0,8},{8,0},{16,24},{24,16},{1,9},{9,1},{17,25},{25,17},{2,10},{10... | collective-permute-start | bytes 589832 | tf_op jit(solution)/shard_map/ppermute | solution.py:30
  45.8 10.4 %collective-permute-start.6 = (f32[48,1024]{1,0:T(8,128)S(1)}, f32[48,1024]{1,0:T(8,128)S(1)}, u32[]{:S(2)}, u32[]{:S(2)}) collective-permute-start(f32[48,1024]{1,0:T(8,128)S(1)} %get-tuple-element.55.refs_0_), channel_id=1, source_target_pairs={{0,1},{1,0},{2,3},{3,2},{4,5},{5,4},{6,7},{7,6},{8,9},{9,8},{10,11... | collective-permute-start | bytes 589832 | tf_op jit(solution)/shard_map/ppermute | solution.py:30
  45.8 9.7 %collective-permute-start.10 = (f32[16,2048]{1,0:T(8,128)S(1)}, f32[16,2048]{1,0:T(8,128)S(1)}, u32[]{:S(2)}, u32[]{:S(2)}) collective-permute-start(f32[16,2048]{1,0:T(8,128)S(1)} %get-tuple-element.64), channel_id=1, source_target_pairs={{0,4},{2,6},{4,0},{6,2},{1,5},{3,7},{5,1},{7,3},{8,12},{10,14},{12... | collective-permute-start | bytes 393224 | tf_op jit(solution)/shard_map/ppermute | solution.py:30
  48.7 10.1 %collective-permute-start.17 = (f32[48,1024]{1,0:T(8,128)S(1)}, f32[48,1024]{1,0:T(8,128)S(1)}, u32[]{:S(2)}, u32[]{:S(2)}) collective-permute-start(f32[48,1024]{1,0:T(8,128)S(1)} %get-tuple-element.62.refs_2_), channel_id=1, source_target_pairs={{0,24},{8,16},{16,8},{24,0},{1,25},{9,17},{17,9},{25,1},{2,26},{10... | collective-permute-start | bytes 589832 | tf_op jit(solution)/shard_map/ppermute | solution.py:30
  51.2 8.8 %collective-permute-start.16 = (f32[48,1024]{1,0:T(8,128)S(1)}, f32[48,1024]{1,0:T(8,128)S(1)}, u32[]{:S(2)}, u32[]{:S(2)}) collective-permute-start(f32[48,1024]{1,0:T(8,128)S(1)} %get-tuple-element.62.refs_2_), channel_id=1, source_target_pairs={{0,16},{8,24},{16,0},{24,8},{1,17},{9,25},{17,1},{25,9},{2,18},{10... | collective-permute-start | bytes 589832 | tf_op jit(solution)/shard_map/ppermute | solution.py:30
  51.7 9.8 %collective-permute-start.15 = (f32[48,1024]{1,0:T(8,128)S(1)}, f32[48,1024]{1,0:T(8,128)S(1)}, u32[]{:S(2)}, u32[]{:S(2)}) collective-permute-start(f32[48,1024]{1,0:T(8,128)S(1)} %get-tuple-element.62.refs_2_), channel_id=1, source_target_pairs={{0,8},{8,0},{16,24},{24,16},{1,9},{9,1},{17,25},{25,17},{2,10},{10... | collective-permute-start | bytes 589832 | tf_op jit(solution)/shard_map/ppermute | solution.py:30
  55.5 6.0 %collective-permute-start.9 = (f32[48,1024]{1,0:T(8,128)S(1)}, f32[48,1024]{1,0:T(8,128)S(1)}, u32[]{:S(2)}, u32[]{:S(2)}) collective-permute-start(f32[48,1024]{1,0:T(8,128)S(1)} %get-tuple-element.62.refs_2_), channel_id=1, source_target_pairs={{0,1},{1,0},{2,3},{3,2},{4,5},{5,4},{6,7},{7,6},{8,9},{9,8},{10,11... | collective-permute-start | bytes 589832 | tf_op jit(solution)/shard_map/ppermute | solution.py:30
  56.1 6.9 %collective-permute-start.20 = (f32[32,1024]{1,0:T(8,128)S(1)}, f32[32,1024]{1,0:T(8,128)S(1)}, u32[]{:S(2)}, u32[]{:S(2)}) collective-permute-start(f32[32,1024]{1,0:T(8,128)S(1)} %get-tuple-element.66.refs_4_), channel_id=1, source_target_pairs={{0,24},{8,16},{16,8},{24,0},{1,25},{9,17},{17,9},{25,1},{2,26},{10... | collective-permute-start | bytes 393224 | tf_op jit(solution)/shard_map/ppermute | solution.py:30
  58.8 7.0 %collective-permute-start.19 = (f32[32,1024]{1,0:T(8,128)S(1)}, f32[32,1024]{1,0:T(8,128)S(1)}, u32[]{:S(2)}, u32[]{:S(2)}) collective-permute-start(f32[32,1024]{1,0:T(8,128)S(1)} %get-tuple-element.66.refs_4_), channel_id=1, source_target_pairs={{0,16},{8,24},{16,0},{24,8},{1,17},{9,25},{17,1},{25,9},{2,18},{10... | collective-permute-start | bytes 393224 | tf_op jit(solution)/shard_map/ppermute | solution.py:30
  60.0 6.0 %collective-permute-start.18 = (f32[32,1024]{1,0:T(8,128)S(1)}, f32[32,1024]{1,0:T(8,128)S(1)}, u32[]{:S(2)}, u32[]{:S(2)}) collective-permute-start(f32[32,1024]{1,0:T(8,128)S(1)} %get-tuple-element.66.refs_4_), channel_id=1, source_target_pairs={{0,8},{8,0},{16,24},{24,16},{1,9},{9,1},{17,25},{25,17},{2,10},{10... | collective-permute-start | bytes 393224 | tf_op jit(solution)/shard_map/ppermute | solution.py:30
  61.5 4.5 %collective-permute-start.11 = (f32[32,1024]{1,0:T(8,128)S(1)}, f32[32,1024]{1,0:T(8,128)S(1)}, u32[]{:S(2)}, u32[]{:S(2)}) collective-permute-start(f32[32,1024]{1,0:T(8,128)S(1)} %get-tuple-element.66.refs_4_), channel_id=1, source_target_pairs={{0,1},{1,0},{2,3},{3,2},{4,5},{5,4},{6,7},{7,6},{8,9},{9,8},{10,11... | collective-permute-start | bytes 393224 | tf_op jit(solution)/shard_map/ppermute | solution.py:30
  68.2 9.6 %collective-permute-start.21 = (f32[256,128]{1,0:T(8,128)S(1)}, f32[256,128]{1,0:T(8,128)S(1)}, u32[]{:S(2)}, u32[]{:S(2)}) collective-permute-start(f32[256,128]{1,0:T(8,128)S(1)} %get-tuple-element.68), channel_id=1, source_target_pairs={{0,2},{2,0},{4,6},{6,4},{1,3},{3,1},{5,7},{7,5},{8,10},{10,8},{12,... | collective-permute-start | bytes 393224 | tf_op jit(solution)/shard_map/ppermute | solution.py:30
  73.4 9.6 %collective-permute-start.22 = (f32[256,128]{1,0:T(8,128)S(1)}, f32[256,128]{1,0:T(8,128)S(1)}, u32[]{:S(2)}, u32[]{:S(2)}) collective-permute-start(f32[256,128]{1,0:T(8,128)S(1)} %get-tuple-element.69), channel_id=1, source_target_pairs={{0,4},{2,6},{4,0},{6,2},{1,5},{3,7},{5,1},{7,3},{8,12},{10,14},{12... | collective-permute-start | bytes 393224 | tf_op jit(solution)/shard_map/ppermute | solution.py:30
  73.4 9.6 %collective-permute-start.23 = (f32[256,128]{1,0:T(8,128)S(1)}, f32[256,128]{1,0:T(8,128)S(1)}, u32[]{:S(2)}, u32[]{:S(2)}) collective-permute-start(f32[256,128]{1,0:T(8,128)S(1)} %get-tuple-element.70), channel_id=1, source_target_pairs={{0,6},{2,4},{4,2},{6,0},{1,7},{3,5},{5,3},{7,1},{8,14},{10,12},{12... | collective-permute-start | bytes 393224 | tf_op jit(solution)/shard_map/ppermute | solution.py:30
  (2 other events, 13.2 us)

commit v3 on v2

--- a/solution.py
+++ b/solution.py
@@ -10,6 +10,10 @@
 UNIT = 16
 HALF = UNIT // 2
 CHUNKS = (3, 3, 2)
+ORDER = (
+    (("first", 0), ("first", 1), ("later", 0), ("first", 2), ("later", 1)),
+    (("finish", 0), ("later", 2), ("finish", 1), ("take", 0), ("finish", 2), ("take", 1), ("take", 2)),
+)
 VMEM = pl.BlockSpec(memory_space=pltpu.VMEM)
 ANY = pl.BlockSpec(memory_space=pl.ANY)
 PARAMS = pltpu.CompilerParams(vmem_limit_bytes=40 * 1024 * 1024)
@@ -31,6 +35,7 @@
 
 
 def project_kernel(n_mid, per_core, positions, spans, to_hbm, tensor, two_in, three_in, *refs):
+    refs = refs if to_hbm else refs[1:]
     outs, (held, two_ref, three_ref, wide_s, two_s, three_s, sems, *results) = refs[: len(spans)], refs[len(spans) :]
     n_col = lax.axis_size("col")
     rank, n_two = two_ref.shape
@@ -95,7 +100,7 @@
         copy.wait()
 
 
-def project(tensor, two_t, three_t, positions, spans, n_mid, per_core, to_hbm):
+def project(tensor, two_t, three_t, token, positions, spans, n_mid, per_core, to_hbm):
     n_two, n_three = tensor.shape[1:]
     rank = two_t.shape[0]
     n_units = sum(len(positions) * count for _, count in spans)
@@ -114,16 +119,17 @@
     return pl.pallas_call(
         functools.partial(project_kernel, n_mid, per_core, positions, spans, to_hbm),
         out_shape=tuple(jax.ShapeDtypeStruct(shape, jnp.float32) for shape in shapes),
-        in_specs=[ANY] * 3,
+        in_specs=[ANY] * 3 + [VMEM] * (not to_hbm),
         out_specs=[ANY if to_hbm else VMEM] * len(shapes),
         scratch_shapes=scratch,
         compiler_params=pltpu.CompilerParams(vmem_limit_bytes=(58 if to_hbm else 48) * 1024 * 1024),
         cost_estimate=COST,
         name="project",
-    )(tensor, two_t, three_t)
-
-
-def fold_kernel(keep, got, token, send_out, keep_out, token_out):
+    )(tensor, two_t, three_t, *(() if to_hbm else (token,)))
+
+
+def fold_kernel(*refs):
+    (keep, got, token), (send_out, keep_out, token_out) = refs[:3], refs[3:]
     half = keep.shape[0] // 2
     send_out[...] = keep[:half] + got[:half]
     keep_out[...] = keep[half:] + got[half:]
@@ -143,8 +149,35 @@
     )(keep, got, token)
 
 
-def turn_kernel(keep, got, token, out_ref, token_out, turned):
-    total = keep[...] + got[...]
+def deal_kernel(block, keep, got, token, *refs):
+    *outs, token_out = refs
+    at = 0
+    for out in outs:
+        out[...] = keep[at : at + out.shape[0]] + got[at : at + out.shape[0]]
+        at += out.shape[0]
+    token_out[...] = token[...]
+
+
+def deal(keep, got, token, block):
+    blocks, width = keep.shape[0] // block, keep.shape[1]
+    half = (blocks + 1) // 2
+    sizes = [half - 1, 1, half - 1] + ([1] if blocks % 2 == 0 else [])
+    shapes = [jax.ShapeDtypeStruct((size * block, width), jnp.float32) for size in sizes if size]
+    *outs, token = pl.pallas_call(
+        functools.partial(deal_kernel, block),
+        out_shape=(*shapes, TOKEN),
+        in_specs=[VMEM] * 3,
+        out_specs=[VMEM] * (len(shapes) + 1),
+        compiler_params=PARAMS,
+        cost_estimate=COST,
+        name="deal",
+    )(keep, got, token)
+    return [outs.pop(0) if size else None for size in sizes], token
+
+
+def turn_kernel(n_terms, *refs):
+    terms, (token, out_ref, token_out, turned) = refs[:n_terms], refs[n_terms:]
+    total = sum((term[...] for term in terms[1:]), terms[0][...])
     token_out[...] = token[...]
     block, width = total.shape
     lanes = out_ref.shape[1] // (block // 2)
@@ -162,18 +195,18 @@
             out_ref[unit * UNIT + HALF : (unit + 1) * UNIT, columns] = jnp.where(low, pltpu.roll(even, lanes // 2, 1), odd)
 
 
-def turn(keep, got, token, rank):
-    block, width = keep.shape
+def turn(terms, token, rank):
+    block, width = terms[0].shape
     return pl.pallas_call(
-        turn_kernel,
+        functools.partial(turn_kernel, len(terms)),
         out_shape=(jax.ShapeDtypeStruct((width // rank, block * rank), jnp.float32), TOKEN),
-        in_specs=[VMEM] * 3,
+        in_specs=[VMEM] * (len(terms) + 1),
         out_specs=[VMEM] * 2,
         scratch_shapes=[pltpu.VMEM((width // rank // UNIT, block * HALF, 2 * rank), jnp.float32)],
         compiler_params=PARAMS,
         cost_estimate=COST,
         name="turn",
-    )(keep, got, token)
+    )(*terms, token)
 
 
 def split(value):
@@ -181,30 +214,28 @@
     return high, (value - high.astype(jnp.float32)).astype(jnp.bfloat16)
 
 
-def gram_kernel(starts, n_aa, n_col, n_mid, per_core, *refs):
+def absorb_kernel(first, start, n_aa, n_col, n_mid, per_core, last, token, *refs):
     place = [lax.axis_index(name) for name in ("col", "ba", "aa")]
-    n_chunks = len(starts)
-    rows_in = refs[: n_chunks * n_col]
-    others_in = refs[n_chunks * n_col : n_chunks * (n_col + n_aa - 1)]
-    outs = refs[n_chunks * (n_col + n_aa - 1) : n_chunks * (n_col + n_aa - 1) + n_mid]
-    left, left_low, right, right_low = refs[n_chunks * (n_col + n_aa - 1) + n_mid :]
+    rows_in, others_in = refs[:n_col], refs[n_col : n_col + n_aa - 1]
+    refs = refs[n_col + n_aa - 1 + (0 if first else 4) :]
+    left, left_low, right, right_low, token_out, *outs = refs
+    token_out[...] = token[...]
+    count = rows_in[0].shape[0] // UNIT
     for distance in range(n_col):
         core = place[0] ^ distance
-        for k, start in enumerate(starts):
-            ref = rows_in[k * n_col + distance]
-            for unit in range(ref.shape[0] // UNIT):
-                high, low = split(ref[unit * UNIT : (unit + 1) * UNIT, :])
-                at = (start + unit) * UNIT
-                row = (at // per_core) * n_col * per_core + core * per_core + at % per_core
-                where = pl.ds(pl.multiple_of(row, UNIT), UNIT)
-                left[where, :], left_low[where, :] = high, low
-                if distance == 0:
-                    right[0, at : at + UNIT, :], right_low[0, at : at + UNIT, :] = high, low
+        for unit in range(count):
+            high, low = split(rows_in[distance][unit * UNIT : (unit + 1) * UNIT, :])
+            at = (start + unit) * UNIT
+            row = (at // per_core) * n_col * per_core + core * per_core + at % per_core
+            where = pl.ds(pl.multiple_of(row, UNIT), UNIT)
+            left[where, :], left_low[where, :] = high, low
+            if distance == 0:
+                right[0, at : at + UNIT, :], right_low[0, at : at + UNIT, :] = high, low
     for distance in range(1, n_aa):
-        for k, start in enumerate(starts):
-            ref = others_in[k * (n_aa - 1) + distance - 1]
-            where = slice(start * UNIT, start * UNIT + ref.shape[0])
-            right[distance, where, :], right_low[distance, where, :] = split(ref[...])
+        where = slice(start * UNIT, (start + count) * UNIT)
+        right[distance, where, :], right_low[distance, where, :] = split(others_in[distance - 1][...])
+    if not last:
+        return
     scale = 1.0 / (n_mid * left.shape[1])
     share = n_mid // n_aa
     dot = functools.partial(
@@ -219,19 +250,23 @@
         outs[distance][...] = value * scale
 
 
-def gram_terms(own, others, starts, n_aa, n_col, n_mid, per_core, local_rows):
-    depth = own[0].shape[1]
-    held = n_mid // n_aa * per_core
-    return pl.pallas_call(
-        functools.partial(gram_kernel, starts, n_aa, n_col, n_mid, per_core),
-        out_shape=(jax.ShapeDtypeStruct((local_rows, per_core), jnp.float32),) * n_mid,
-        in_specs=[VMEM] * (len(own) + len(others)),
-        out_specs=[VMEM] * n_mid,
-        scratch_shapes=[pltpu.VMEM((local_rows, depth), jnp.bfloat16)] * 2
-        + [pltpu.VMEM((n_aa, held, depth), jnp.bfloat16)] * 2,
+def absorb(token, rows, others, held, start, n_aa, n_col, n_mid, per_core, local_rows, last):
+    depth = rows[0].shape[1]
+    shapes = [jax.ShapeDtypeStruct((local_rows, depth), jnp.bfloat16)] * 2
+    shapes += [jax.ShapeDtypeStruct((n_aa, n_mid // n_aa * per_core, depth), jnp.bfloat16)] * 2
+    shapes += [TOKEN] + [jax.ShapeDtypeStruct((local_rows, per_core), jnp.float32)] * (n_mid if last else 0)
+    n_in = 1 + len(rows) + len(others)
+    outs = pl.pallas_call(
+        functools.partial(absorb_kernel, not held, start, n_aa, n_col, n_mid, per_core, last),
+        out_shape=tuple(shapes),
+        in_specs=[VMEM] * (n_in + len(held)),
+        out_specs=[VMEM] * len(shapes),
+        input_output_aliases={n_in + i: i for i in range(len(held))},
         compiler_params=PARAMS,
-        name="gram_terms",
-    )(*own, *others)
+        cost_estimate=COST,
+        name="gram" if last else "absorb",
+    )(token, *rows, *others, *held)
+    return outs[:4], outs[4], outs[5:]
 
 
 def body(tensor, factor_two, factor_three):
@@ -245,51 +280,59 @@
         bounds.append(round(units * sum(CHUNKS[: k + 1]) / sum(CHUNKS)))
     spans = [(a, b - a) for a, b in zip(bounds, bounds[1:]) if b > a]
     n_chunks = len(spans)
+    block = rank // n_mid
     two_t, three_t = factor_two.T, factor_three.T
     token = jnp.zeros(TOKEN.shape, TOKEN.dtype)
     first_half, second_half = tuple(range(n_col // 2)), tuple(range(n_col // 2, n_col))
 
-    sends = project(tensor, two_t, three_t, first_half, spans, n_mid, per_core, True)
+    sends = project(tensor, two_t, three_t, token, first_half, spans, n_mid, per_core, True)
     got = [exchange(send, "col", 1) for send in sends]
-    keep = list(project(tensor, two_t, three_t, second_half, spans, n_mid, per_core, False))
-    mine, own, others = [None] * n_chunks, [], []
+    keep = list(project(tensor, two_t, three_t, token, second_half, spans[:1], n_mid, per_core, False))
     col_steps, mid_steps = bits_of(n_col), bits_of(n_mid)
-
-    def over_col(k, token):
+    finals, gathered = [[] for _ in spans], [None] * n_chunks
+    held = ()
+
+    def first_step(k, token):
         for step in range(1, col_steps):
             send, keep[k], token = fold(keep[k], got[k], token)
             got[k] = exchange(send, "col", 1 << step)
-        keep[k], got[k] = keep[k][0], got[k][0]
-        return over_mid(k, 0, token)
-
-    def over_mid(k, step, token):
-        send, keep[k], token = fold(keep[k], got[k], token)
-        got[k] = exchange(send, "ba", 1 << step)
+        (onward, final, keep[k], mine), token = deal(keep[k][0], got[k][0], token, block)
+        got[k] = exchange(onward, "ba", 1)
+        if k == 0 and spans[1:]:
+            keep.extend(project(tensor, two_t, three_t, token, second_half, spans[1:], n_mid, per_core, False))
+        finals[k] += [mine, exchange(final, "ba", 1)]
         return token
 
+    def later_steps(k, token):
+        for step in range(1, mid_steps):
+            (onward, final, keep[k]), token = deal(keep[k], got[k], token, block)
+            if onward is not None:
+                got[k] = exchange(onward, "ba", 1 << step)
+            finals[k].append(exchange(final, "ba", 1 << step))
+        return token
+
     def finish(k, token):
-        mine[k], token = turn(keep[k], got[k], token, rank)
+        mine, token = turn(finals[k], token, rank)
+        rows = [mine] + [exchange(mine, "col", d) for d in range(1, n_col)]
+        gathered[k] = rows, [exchange(mine, "aa", d) for d in range(1, n_aa)]
         return token
 
-    token = over_col(0, token)
-    for k in range(1, n_chunks):
-        if k >= 2:
-            for step in range(1, mid_steps):
-                token = over_mid(k - 2, step, token)
-        token = over_col(k, token)
-    for k in range(n_chunks):
-        if k >= n_chunks - 2:
-            for step in range(1, mid_steps):
-                token = over_mid(k, step, token)
-        if k >= 1:
-            token = finish(k - 1, token)
-    token = finish(n_chunks - 1, token)
-    for k in range(n_chunks):
-        own += [mine[k]] + [exchange(mine[k], "col", d) for d in range(1, n_col)]
-        others += [exchange(mine[k], "aa", d) for d in range(1, n_aa)]
-
-    starts = [first for first, _ in spans]
-    sums = gram_terms(own, others, starts, n_aa, n_col, n_mid, per_core, local_rows)
+    def take(k, token, held):
+        last = k == n_chunks - 1
+        return absorb(token, *gathered[k], held, spans[k][0], n_aa, n_col, n_mid, per_core, local_rows, last)
+
+    for order in ORDER:
+        for name, k in order:
+            if k >= n_chunks:
+                continue
+            if name == "first":
+                token = first_step(k, token)
+            elif name == "later":
+                token = later_steps(k, token)
+            elif name == "finish":
+                token = finish(k, token)
+            else:
+                held, token, sums = take(k, token, held)
     gram = sums[0]
     for d in range(1, n_mid):
         gram = gram + exchange(sums[d], "ba", d)

time: 84.3 us -> 79.8 us (0.947)
  waiting for transfers between devices: 37.1 us -> 31.1 us
  Pallas kernels: 13.1 us -> 14.3 us
    ppermute x24 -> x27, waiting for transfers between devices: 37.1 us -> 31.1 us  [exchange(): return lax.ppermute(x, axis, [(i, i ^ distance) for i in range(n)])]
    pallas_call x2 -> x3, Pallas kernels: 9.71 us -> 11 us  [project(): pl.pallas_call(functools.partial(project_kernel, n_mid, per_core, positio...]
    ppermute x24 -> x27, starting transfers between devices: 32.7 us -> 33.5 us  [exchange(): return lax.ppermute(x, axis, [(i, i ^ distance) for i in range(n)])]
    pallas_call x10 -> x12, Pallas kernels: 3.38 us -> 3.21 us  [the longest x3 2.5 us: absorb(): pl.pallas_call(functools.partial(absorb_kernel, not held, start, n_aa, n_...]
  transfers between devices with their start and end apart: 24 -> 27, of which waited for: 10 -> 11; matrix products, arithmetic and copies ran while one was open for 0% -> 0% of each run, Pallas kernels for 7% -> 8%
where the time goes in v3:
time: 79.8 us; the launch traced here: 79.6 us
  starting transfers between devices  33.5 us (42%)
  waiting for transfers between devices  31.1 us (39%)
  Pallas kernels  14.3 us (18%)
    ppermute x27, starting transfers between devices, exchange(): return lax.ppermute(x, axis, [(i, i ^ distance) for i in range(n)])  33.5 us
    ppermute x27, waiting for transfers between devices, exchange(): return lax.ppermute(x, axis, [(i, i ^ distance) for i in range(n)])  31.1 us
    pallas_call x3, Pallas kernels, project(): pl.pallas_call(functools.partial(project_kernel, n_mid, per_core, positio...  11 us
    pallas_call x3, Pallas kernels, absorb(): pl.pallas_call(functools.partial(absorb_kernel, not held, start, n_aa, n_...  2.5 us
  transfers between devices with their start and end apart: 27, of which 11 were waited for; matrix products, arithmetic and copies ran while one was open for 0% of the time, Pallas kernels for 8%

profile of v3, /device:TPU:0, one launch (start us, length us, event | category | flops | bytes accessed | tf_op | source)
XLA Modules:
  0.0 79.6 jit_solution(9012477273006066291)
XLA Ops:
  0.0 5.4 %project.4 = (f32[1,64,3072]{2,1,0:T(8,128)}, f32[1,64,3072]{2,1,0:T(8,128)}, f32[1,64,2048]{2,1,0:T(8,128)}) custom-call(bf16[256,128,128]{2,1,0:T(8,128)(2,1)} %tensor.5, bf16[64,128]{1,0:T(8,128)(2,1)} %bitcast.14, bf16[64,128]{1,0:T(8,128)(2,1)} %bitcast.17), custom_call_target="tpu_custom_call" | custom-call | flops 1 | bytes 1 | tf_op jit(solution)/shard_map/project/pallas_call | solution.py:119
  6.6 2.3 %project.3 = f32[1,64,3072]{2,1,0:T(8,128)S(1)} custom-call(bf16[256,128,128]{2,1,0:T(8,128)(2,1)} %tensor.5, bf16[64,128]{1,0:T(8,128)(2,1)S(1)} %bitcast.15, bf16[64,128]{1,0:T(8,128)(2,1)S(1)} %bitcast.18, f32[8,128]{1,0:T(8,128)S(1)} %broadcast_in_dim.3.refs_0_.token), custom_call_target="tpu_custom_call" | custom-call | flops 1 | bytes 1 | tf_op jit(solution)/shard_map/project/pallas_call | solution.py:119
  9.0 2.6 %collective-permute-start.2 = (f32[16,3072]{1,0:T(8,128)S(1)}, f32[16,3072]{1,0:T(8,128)S(1)}, u32[]{:S(2)}, u32[]{:S(2)}) collective-permute-start(f32[16,3072]{1,0:T(8,128)S(1)} %get-tuple-element.56), channel_id=1, source_target_pairs={{0,2},{2,0},{4,6},{6,4},{1,3},{3,1},{5,7},{7,5},{8,10},{10,8},{12,... | collective-permute-start | bytes 589832 | tf_op jit(solution)/shard_map/ppermute | solution.py:34
  11.6 3.4 %project.5 = (f32[1,64,3072]{2,1,0:T(8,128)S(1)}, f32[1,64,2048]{2,1,0:T(8,128)S(1)}) custom-call(bf16[256,128,128]{2,1,0:T(8,128)(2,1)} %tensor.5, bf16[64,128]{1,0:T(8,128)(2,1)S(1)} %bitcast.16, bf16[64,128]{1,0:T(8,128)(2,1)S(1)} %bitcast.19, f32[8,128]{1,0:T(8,128)S(1)} %get-tuple-element.52.refs_0_.token), custom_call_target="tpu_custom_call" | custom-call | flops 1 | bytes 1 | tf_op jit(solution)/shard_map/project/pallas_call | solution.py:119
  15.1 2.0 %collective-permute-start.6 = (f32[16,3072]{1,0:T(8,128)S(1)}, f32[16,3072]{1,0:T(8,128)S(1)}, u32[]{:S(2)}, u32[]{:S(2)}) collective-permute-start(f32[16,3072]{1,0:T(8,128)S(1)} %get-tuple-element.66), channel_id=1, source_target_pairs={{0,2},{2,0},{4,6},{6,4},{1,3},{3,1},{5,7},{7,5},{8,10},{10,8},{12,... | collective-permute-start | bytes 589832 | tf_op jit(solution)/shard_map/ppermute | solution.py:34
  17.2 2.8 %collective-permute-start.7 = (f32[16,3072]{1,0:T(8,128)S(1)}, f32[16,3072]{1,0:T(8,128)S(1)}, u32[]{:S(2)}, u32[]{:S(2)}) collective-permute-start(f32[16,3072]{1,0:T(8,128)S(1)} %get-tuple-element.67), channel_id=1, source_target_pairs={{0,4},{2,6},{4,0},{6,2},{1,5},{3,7},{5,1},{7,3},{8,12},{10,14},{12... | collective-permute-start | bytes 589832 | tf_op jit(solution)/shard_map/ppermute | solution.py:34
  19.9 2.0 %collective-permute-start.10 = (f32[16,3072]{1,0:T(8,128)S(1)}, f32[16,3072]{1,0:T(8,128)S(1)}, u32[]{:S(2)}, u32[]{:S(2)}) collective-permute-start(f32[16,3072]{1,0:T(8,128)S(1)} %get-tuple-element.75), channel_id=1, source_target_pairs={{0,2},{2,0},{4,6},{6,4},{1,3},{3,1},{5,7},{7,5},{8,10},{10,8},{12,... | collective-permute-start | bytes 589832 | tf_op jit(solution)/shard_map/ppermute | solution.py:34
  22.0 5.0 %collective-permute-done.8.got = f32[16,3072]{1,0:T(8,128)S(1)} collective-permute-done((f32[16,3072]{1,0:T(8,128)S(1)}, f32[16,3072]{1,0:T(8,128)S(1)}, u32[]{:S(2)}, u32[]{:S(2)}) %collective-permute-start.8) | collective-permute-done | bytes 196640 | tf_op jit(solution)/shard_map/ppermute | solution.py:34
  27.9 2.5 %collective-permute-start.5 = (f32[16,2048]{1,0:T(8,128)S(1)}, f32[16,2048]{1,0:T(8,128)S(1)}, u32[]{:S(2)}, u32[]{:S(2)}) collective-permute-start(f32[16,2048]{1,0:T(8,128)S(1)} %get-tuple-element.64), channel_id=1, source_target_pairs={{0,2},{2,0},{4,6},{6,4},{1,3},{3,1},{5,7},{7,5},{8,10},{10,8},{12,... | collective-permute-start | bytes 393224 | tf_op jit(solution)/shard_map/ppermute | solution.py:34
  30.4 1.0 %collective-permute-done.6.refs_1_ = f32[16,3072]{1,0:T(8,128)S(1)} collective-permute-done((f32[16,3072]{1,0:T(8,128)S(1)}, f32[16,3072]{1,0:T(8,128)S(1)}, u32[]{:S(2)}, u32[]{:S(2)}) %collective-permute-start.6) | collective-permute-done | bytes 196640 | tf_op jit(solution)/shard_map/ppermute | solution.py:34
  31.5 2.5 %collective-permute-start.15 = (f32[48,1024]{1,0:T(8,128)S(1)}, f32[48,1024]{1,0:T(8,128)S(1)}, u32[]{:S(2)}, u32[]{:S(2)}) collective-permute-start(f32[48,1024]{1,0:T(8,128)S(1)} %get-tuple-element.79.refs_0_), channel_id=1, source_target_pairs={{0,24},{8,16},{16,8},{24,0},{1,25},{9,17},{17,9},{25,1},{2,26},{10... | collective-permute-start | bytes 589832 | tf_op jit(solution)/shard_map/ppermute | solution.py:34
  34.5 5.2 %collective-permute-done.10.refs_1_ = f32[16,3072]{1,0:T(8,128)S(1)} collective-permute-done((f32[16,3072]{1,0:T(8,128)S(1)}, f32[16,3072]{1,0:T(8,128)S(1)}, u32[]{:S(2)}, u32[]{:S(2)}) %collective-permute-start.10) | collective-permute-done | bytes 196640 | tf_op jit(solution)/shard_map/ppermute | solution.py:34
  39.7 1.5 %collective-permute-start.13 = (f32[48,1024]{1,0:T(8,128)S(1)}, f32[48,1024]{1,0:T(8,128)S(1)}, u32[]{:S(2)}, u32[]{:S(2)}) collective-permute-start(f32[48,1024]{1,0:T(8,128)S(1)} %get-tuple-element.79.refs_0_), channel_id=1, source_target_pairs={{0,8},{8,0},{16,24},{24,16},{1,9},{9,1},{17,25},{25,17},{2,10},{10... | collective-permute-start | bytes 589832 | tf_op jit(solution)/shard_map/ppermute | solution.py:34
  42.9 3.8 %collective-permute-done.4.refs_1_ = f32[16,2048]{1,0:T(8,128)S(1)} collective-permute-done((f32[16,2048]{1,0:T(8,128)S(1)}, f32[16,2048]{1,0:T(8,128)S(1)}, u32[]{:S(2)}, u32[]{:S(2)}) %collective-permute-start.4) | collective-permute-done | bytes 131104 | tf_op jit(solution)/shard_map/ppermute | solution.py:34
  46.7 2.4 %collective-permute-start.19 = (f32[48,1024]{1,0:T(8,128)S(1)}, f32[48,1024]{1,0:T(8,128)S(1)}, u32[]{:S(2)}, u32[]{:S(2)}) collective-permute-start(f32[48,1024]{1,0:T(8,128)S(1)} %get-tuple-element.82.refs_0_), channel_id=1, source_target_pairs={{0,24},{8,16},{16,8},{24,0},{1,25},{9,17},{17,9},{25,1},{2,26},{10... | collective-permute-start | bytes 589832 | tf_op jit(solution)/shard_map/ppermute | solution.py:34
  50.2 2.6 %collective-permute-start.9 = (f32[16,2048]{1,0:T(8,128)S(1)}, f32[16,2048]{1,0:T(8,128)S(1)}, u32[]{:S(2)}, u32[]{:S(2)}) collective-permute-start(f32[16,2048]{1,0:T(8,128)S(1)} %get-tuple-element.73), channel_id=1, source_target_pairs={{0,4},{2,6},{4,0},{6,2},{1,5},{3,7},{5,1},{7,3},{8,12},{10,14},{12... | collective-permute-start | bytes 393224 | tf_op jit(solution)/shard_map/ppermute | solution.py:34
  53.0 4.5 %collective-permute-done.9.refs_2_ = f32[16,2048]{1,0:T(8,128)S(1)} collective-permute-done((f32[16,2048]{1,0:T(8,128)S(1)}, f32[16,2048]{1,0:T(8,128)S(1)}, u32[]{:S(2)}, u32[]{:S(2)}) %collective-permute-start.9) | collective-permute-done | bytes 131104 | tf_op jit(solution)/shard_map/ppermute | solution.py:34
  57.6 2.5 %collective-permute-start.23 = (f32[32,1024]{1,0:T(8,128)S(1)}, f32[32,1024]{1,0:T(8,128)S(1)}, u32[]{:S(2)}, u32[]{:S(2)}) collective-permute-start(f32[32,1024]{1,0:T(8,128)S(1)} %get-tuple-element.88.refs_0_), channel_id=1, source_target_pairs={{0,24},{8,16},{16,8},{24,0},{1,25},{9,17},{17,9},{25,1},{2,26},{10... | collective-permute-start | bytes 393224 | tf_op jit(solution)/shard_map/ppermute | solution.py:34
  61.3 2.2 %collective-permute-done.23.refs_4_ = f32[32,1024]{1,0:T(8,128)S(1)} collective-permute-done((f32[32,1024]{1,0:T(8,128)S(1)}, f32[32,1024]{1,0:T(8,128)S(1)}, u32[]{:S(2)}, u32[]{:S(2)}) %collective-permute-start.23) | collective-permute-done | bytes 131104 | tf_op jit(solution)/shard_map/ppermute | solution.py:34
  63.5 1.5 %collective-permute-done.22.refs_3_ = f32[32,1024]{1,0:T(8,128)S(1)} collective-permute-done((f32[32,1024]{1,0:T(8,128)S(1)}, f32[32,1024]{1,0:T(8,128)S(1)}, u32[]{:S(2)}, u32[]{:S(2)}) %collective-permute-start.22) | collective-permute-done | bytes 131104 | tf_op jit(solution)/shard_map/ppermute | solution.py:34
  65.6 2.2 %gram.1 = (bf16[256,1024]{1,0:T(8,128)(2,1)S(1)}, bf16[256,1024]{1,0:T(8,128)(2,1)S(1)}, bf16[4,128,1024]{2,1,0:T(8,128)(2,1)S(1)}, bf16[4,128,1024]{2,1,0:T(8,1...) custom-call(f32[8,128]{1,0:T(8,128)S(1)} %get-tuple-element.87.token, ...), custom_call_target="tpu_custom_call", output_to_operand_aliasing={{0}: (6, {}), {1}: (7, {}), {2}: (8, {}), {3}: (9, {})} | custom-call | flops 1 | bytes 1 | tf_op jit(solution)/shard_map/gram/pallas_call | solution.py:259
  68.1 3.4 %collective-permute-start.25 = (f32[256,128]{1,0:T(8,128)S(1)}, f32[256,128]{1,0:T(8,128)S(1)}, u32[]{:S(2)}, u32[]{:S(2)}) collective-permute-start(f32[256,128]{1,0:T(8,128)S(1)} %get-tuple-element.95), channel_id=1, source_target_pairs={{0,4},{2,6},{4,0},{6,2},{1,5},{3,7},{5,1},{7,3},{8,12},{10,14},{12... | collective-permute-start | bytes 393224 | tf_op jit(solution)/shard_map/ppermute | solution.py:34
  72.2 2.0 %collective-permute-done.24 = f32[256,128]{1,0:T(8,128)S(1)} collective-permute-done((f32[256,128]{1,0:T(8,128)S(1)}, f32[256,128]{1,0:T(8,128)S(1)}, u32[]{:S(2)}, u32[]{:S(2)}) %collective-permute-start.24) | collective-permute-done | bytes 131104 | tf_op jit(solution)/shard_map/ppermute | solution.py:34
  74.2 4.7 %collective-permute-done.25 = f32[256,128]{1,0:T(8,128)S(1)} collective-permute-done((f32[256,128]{1,0:T(8,128)S(1)}, f32[256,128]{1,0:T(8,128)S(1)}, u32[]{:S(2)}, u32[]{:S(2)}) %collective-permute-start.25) | collective-permute-done | bytes 131104 | tf_op jit(solution)/shard_map/ppermute | solution.py:34
  (51 shorter events, 9.4 us)
Async XLA Ops:
  6.1 8.8 %collective-permute-start.3 = (f32[1,64,3072]{2,1,0:T(8,128)}, f32[1,64,3072]{2,1,0:T(8,128)S(1)}, u32[]{:S(2)}, u32[]{:S(2)}) collective-permute-start(f32[1,64,3072]{2,1,0:T(8,128)} %get-tuple-element.58), channel_id=1, source_target_pairs={{0,1},{1,0},{2,3},{3,2},{4,5},{5,4},{6,7},{7,6},{8,9},{9,8},{10,11... | collective-permute-start | bytes 2359304 | tf_op jit(solution)/shard_map/ppermute | solution.py:34
  6.2 15.8 %collective-permute-start.1 = (f32[1,64,2048]{2,1,0:T(8,128)}, f32[1,64,2048]{2,1,0:T(8,128)S(1)}, u32[]{:S(2)}, u32[]{:S(2)}) collective-permute-start(f32[1,64,2048]{2,1,0:T(8,128)} %get-tuple-element.54), channel_id=1, source_target_pairs={{0,1},{1,0},{2,3},{3,2},{4,5},{5,4},{6,7},{7,6},{8,9},{9,8},{10,11... | collective-permute-start | bytes 1572872 | tf_op jit(solution)/shard_map/ppermute | solution.py:34
  9.0 8.1 %collective-permute-start.2 = (f32[16,3072]{1,0:T(8,128)S(1)}, f32[16,3072]{1,0:T(8,128)S(1)}, u32[]{:S(2)}, u32[]{:S(2)}) collective-permute-start(f32[16,3072]{1,0:T(8,128)S(1)} %get-tuple-element.56), channel_id=1, source_target_pairs={{0,2},{2,0},{4,6},{6,4},{1,3},{3,1},{5,7},{7,5},{8,10},{10,8},{12,... | collective-permute-start | bytes 589832 | tf_op jit(solution)/shard_map/ppermute | solution.py:34
  15.0 12.0 %collective-permute-start.8 = (f32[16,3072]{1,0:T(8,128)S(1)}, f32[16,3072]{1,0:T(8,128)S(1)}, u32[]{:S(2)}, u32[]{:S(2)}) collective-permute-start(f32[16,3072]{1,0:T(8,128)S(1)} %get-tuple-element.69), channel_id=1, source_target_pairs={{0,2},{2,0},{4,6},{6,4},{1,3},{3,1},{5,7},{7,5},{8,10},{10,8},{12,... | collective-permute-start | bytes 589832 | tf_op jit(solution)/shard_map/ppermute | solution.py:34
  15.1 16.3 %collective-permute-start.6 = (f32[16,3072]{1,0:T(8,128)S(1)}, f32[16,3072]{1,0:T(8,128)S(1)}, u32[]{:S(2)}, u32[]{:S(2)}) collective-permute-start(f32[16,3072]{1,0:T(8,128)S(1)} %get-tuple-element.66), channel_id=1, source_target_pairs={{0,2},{2,0},{4,6},{6,4},{1,3},{3,1},{5,7},{7,5},{8,10},{10,8},{12,... | collective-permute-start | bytes 589832 | tf_op jit(solution)/shard_map/ppermute | solution.py:34
  17.2 14.2 %collective-permute-start.7 = (f32[16,3072]{1,0:T(8,128)S(1)}, f32[16,3072]{1,0:T(8,128)S(1)}, u32[]{:S(2)}, u32[]{:S(2)}) collective-permute-start(f32[16,3072]{1,0:T(8,128)S(1)} %get-tuple-element.67), channel_id=1, source_target_pairs={{0,4},{2,6},{4,0},{6,2},{1,5},{3,7},{5,1},{7,3},{8,12},{10,14},{12... | collective-permute-start | bytes 589832 | tf_op jit(solution)/shard_map/ppermute | solution.py:34
  19.9 19.8 %collective-permute-start.10 = (f32[16,3072]{1,0:T(8,128)S(1)}, f32[16,3072]{1,0:T(8,128)S(1)}, u32[]{:S(2)}, u32[]{:S(2)}) collective-permute-start(f32[16,3072]{1,0:T(8,128)S(1)} %get-tuple-element.75), channel_id=1, source_target_pairs={{0,2},{2,0},{4,6},{6,4},{1,3},{3,1},{5,7},{7,5},{8,10},{10,8},{12,... | collective-permute-start | bytes 589832 | tf_op jit(solution)/shard_map/ppermute | solution.py:34
  27.1 15.6 %collective-permute-start.11 = (f32[16,3072]{1,0:T(8,128)S(1)}, f32[16,3072]{1,0:T(8,128)S(1)}, u32[]{:S(2)}, u32[]{:S(2)}) collective-permute-start(f32[16,3072]{1,0:T(8,128)S(1)} %get-tuple-element.76), channel_id=1, source_target_pairs={{0,4},{2,6},{4,0},{6,2},{1,5},{3,7},{5,1},{7,3},{8,12},{10,14},{12... | collective-permute-start | bytes 589832 | tf_op jit(solution)/shard_map/ppermute | solution.py:34
  27.9 13.8 %collective-permute-start.5 = (f32[16,2048]{1,0:T(8,128)S(1)}, f32[16,2048]{1,0:T(8,128)S(1)}, u32[]{:S(2)}, u32[]{:S(2)}) collective-permute-start(f32[16,2048]{1,0:T(8,128)S(1)} %get-tuple-element.64), channel_id=1, source_target_pairs={{0,2},{2,0},{4,6},{6,4},{1,3},{3,1},{5,7},{7,5},{8,10},{10,8},{12,... | collective-permute-start | bytes 393224 | tf_op jit(solution)/shard_map/ppermute | solution.py:34
  31.5 17.6 %collective-permute-start.15 = (f32[48,1024]{1,0:T(8,128)S(1)}, f32[48,1024]{1,0:T(8,128)S(1)}, u32[]{:S(2)}, u32[]{:S(2)}) collective-permute-start(f32[48,1024]{1,0:T(8,128)S(1)} %get-tuple-element.79.refs_0_), channel_id=1, source_target_pairs={{0,24},{8,16},{16,8},{24,0},{1,25},{9,17},{17,9},{25,1},{2,26},{10... | collective-permute-start | bytes 589832 | tf_op jit(solution)/shard_map/ppermute | solution.py:34
  34.0 15.6 %collective-permute-start.14 = (f32[48,1024]{1,0:T(8,128)S(1)}, f32[48,1024]{1,0:T(8,128)S(1)}, u32[]{:S(2)}, u32[]{:S(2)}) collective-permute-start(f32[48,1024]{1,0:T(8,128)S(1)} %get-tuple-element.79.refs_0_), channel_id=1, source_target_pairs={{0,16},{8,24},{16,0},{24,8},{1,17},{9,25},{17,1},{25,9},{2,18},{10... | collective-permute-start | bytes 589832 | tf_op jit(solution)/shard_map/ppermute | solution.py:34
  39.7 10.5 %collective-permute-start.13 = (f32[48,1024]{1,0:T(8,128)S(1)}, f32[48,1024]{1,0:T(8,128)S(1)}, u32[]{:S(2)}, u32[]{:S(2)}) collective-permute-start(f32[48,1024]{1,0:T(8,128)S(1)} %get-tuple-element.79.refs_0_), channel_id=1, source_target_pairs={{0,8},{8,0},{16,24},{24,16},{1,9},{9,1},{17,25},{25,17},{2,10},{10... | collective-permute-start | bytes 589832 | tf_op jit(solution)/shard_map/ppermute | solution.py:34
  42.7 10.1 %collective-permute-start.12 = (f32[48,1024]{1,0:T(8,128)S(1)}, f32[48,1024]{1,0:T(8,128)S(1)}, u32[]{:S(2)}, u32[]{:S(2)}) collective-permute-start(f32[48,1024]{1,0:T(8,128)S(1)} %get-tuple-element.79.refs_0_), channel_id=1, source_target_pairs={{0,1},{1,0},{2,3},{3,2},{4,5},{5,4},{6,7},{7,6},{8,9},{9,8},{10,11... | collective-permute-start | bytes 589832 | tf_op jit(solution)/shard_map/ppermute | solution.py:34
  46.7 13.4 %collective-permute-start.19 = (f32[48,1024]{1,0:T(8,128)S(1)}, f32[48,1024]{1,0:T(8,128)S(1)}, u32[]{:S(2)}, u32[]{:S(2)}) collective-permute-start(f32[48,1024]{1,0:T(8,128)S(1)} %get-tuple-element.82.refs_0_), channel_id=1, source_target_pairs={{0,24},{8,16},{16,8},{24,0},{1,25},{9,17},{17,9},{25,1},{2,26},{10... | collective-permute-start | bytes 589832 | tf_op jit(solution)/shard_map/ppermute | solution.py:34
  49.1 11.5 %collective-permute-start.18 = (f32[48,1024]{1,0:T(8,128)S(1)}, f32[48,1024]{1,0:T(8,128)S(1)}, u32[]{:S(2)}, u32[]{:S(2)}) collective-permute-start(f32[48,1024]{1,0:T(8,128)S(1)} %get-tuple-element.82.refs_0_), channel_id=1, source_target_pairs={{0,16},{8,24},{16,0},{24,8},{1,17},{9,25},{17,1},{25,9},{2,18},{10... | collective-permute-start | bytes 589832 | tf_op jit(solution)/shard_map/ppermute | solution.py:34
  49.7 11.5 %collective-permute-start.17 = (f32[48,1024]{1,0:T(8,128)S(1)}, f32[48,1024]{1,0:T(8,128)S(1)}, u32[]{:S(2)}, u32[]{:S(2)}) collective-permute-start(f32[48,1024]{1,0:T(8,128)S(1)} %get-tuple-element.82.refs_0_), channel_id=1, source_target_pairs={{0,8},{8,0},{16,24},{24,16},{1,9},{9,1},{17,25},{25,17},{2,10},{10... | collective-permute-start | bytes 589832 | tf_op jit(solution)/shard_map/ppermute | solution.py:34
  50.2 7.3 %collective-permute-start.9 = (f32[16,2048]{1,0:T(8,128)S(1)}, f32[16,2048]{1,0:T(8,128)S(1)}, u32[]{:S(2)}, u32[]{:S(2)}) collective-permute-start(f32[16,2048]{1,0:T(8,128)S(1)} %get-tuple-element.73), channel_id=1, source_target_pairs={{0,4},{2,6},{4,0},{6,2},{1,5},{3,7},{5,1},{7,3},{8,12},{10,14},{12... | collective-permute-start | bytes 393224 | tf_op jit(solution)/shard_map/ppermute | solution.py:34
  52.8 8.3 %collective-permute-start.16 = (f32[48,1024]{1,0:T(8,128)S(1)}, f32[48,1024]{1,0:T(8,128)S(1)}, u32[]{:S(2)}, u32[]{:S(2)}) collective-permute-start(f32[48,1024]{1,0:T(8,128)S(1)} %get-tuple-element.82.refs_0_), channel_id=1, source_target_pairs={{0,1},{1,0},{2,3},{3,2},{4,5},{5,4},{6,7},{7,6},{8,9},{9,8},{10,11... | collective-permute-start | bytes 589832 | tf_op jit(solution)/shard_map/ppermute | solution.py:34
  57.6 5.9 %collective-permute-start.23 = (f32[32,1024]{1,0:T(8,128)S(1)}, f32[32,1024]{1,0:T(8,128)S(1)}, u32[]{:S(2)}, u32[]{:S(2)}) collective-permute-start(f32[32,1024]{1,0:T(8,128)S(1)} %get-tuple-element.88.refs_0_), channel_id=1, source_target_pairs={{0,24},{8,16},{16,8},{24,0},{1,25},{9,17},{17,9},{25,1},{2,26},{10... | collective-permute-start | bytes 393224 | tf_op jit(solution)/shard_map/ppermute | solution.py:34
  60.1 5.0 %collective-permute-start.22 = (f32[32,1024]{1,0:T(8,128)S(1)}, f32[32,1024]{1,0:T(8,128)S(1)}, u32[]{:S(2)}, u32[]{:S(2)}) collective-permute-start(f32[32,1024]{1,0:T(8,128)S(1)} %get-tuple-element.88.refs_0_), channel_id=1, source_target_pairs={{0,16},{8,24},{16,0},{24,8},{1,17},{9,25},{17,1},{25,9},{2,18},{10... | collective-permute-start | bytes 393224 | tf_op jit(solution)/shard_map/ppermute | solution.py:34
  60.6 5.0 %collective-permute-start.21 = (f32[32,1024]{1,0:T(8,128)S(1)}, f32[32,1024]{1,0:T(8,128)S(1)}, u32[]{:S(2)}, u32[]{:S(2)}) collective-permute-start(f32[32,1024]{1,0:T(8,128)S(1)} %get-tuple-element.88.refs_0_), channel_id=1, source_target_pairs={{0,8},{8,0},{16,24},{24,16},{1,9},{9,1},{17,25},{25,17},{2,10},{10... | collective-permute-start | bytes 393224 | tf_op jit(solution)/shard_map/ppermute | solution.py:34
  67.8 6.4 %collective-permute-start.24 = (f32[256,128]{1,0:T(8,128)S(1)}, f32[256,128]{1,0:T(8,128)S(1)}, u32[]{:S(2)}, u32[]{:S(2)}) collective-permute-start(f32[256,128]{1,0:T(8,128)S(1)} %get-tuple-element.94), channel_id=1, source_target_pairs={{0,2},{2,0},{4,6},{6,4},{1,3},{3,1},{5,7},{7,5},{8,10},{10,8},{12,... | collective-permute-start | bytes 393224 | tf_op jit(solution)/shard_map/ppermute | solution.py:34
  68.1 10.9 %collective-permute-start.25 = (f32[256,128]{1,0:T(8,128)S(1)}, f32[256,128]{1,0:T(8,128)S(1)}, u32[]{:S(2)}, u32[]{:S(2)}) collective-permute-start(f32[256,128]{1,0:T(8,128)S(1)} %get-tuple-element.95), channel_id=1, source_target_pairs={{0,4},{2,6},{4,0},{6,2},{1,5},{3,7},{5,1},{7,3},{8,12},{10,14},{12... | collective-permute-start | bytes 393224 | tf_op jit(solution)/shard_map/ppermute | solution.py:34
  71.5 7.5 %collective-permute-start.26 = (f32[256,128]{1,0:T(8,128)S(1)}, f32[256,128]{1,0:T(8,128)S(1)}, u32[]{:S(2)}, u32[]{:S(2)}) collective-permute-start(f32[256,128]{1,0:T(8,128)S(1)} %get-tuple-element.96), channel_id=1, source_target_pairs={{0,6},{2,4},{4,2},{6,0},{1,7},{3,5},{5,3},{7,1},{8,14},{10,12},{12... | collective-permute-start | bytes 393224 | tf_op jit(solution)/shard_map/ppermute | solution.py:34
  (5 other events, 26.1 us)

commit v4 on v3

--- a/solution.py
+++ b/solution.py
@@ -14,6 +14,11 @@
     (("first", 0), ("first", 1), ("later", 0), ("first", 2), ("later", 1)),
     (("finish", 0), ("later", 2), ("finish", 1), ("take", 0), ("finish", 2), ("take", 1), ("take", 2)),
 )
+CORE = {0: (0,), 1: (1,), 2: (2,)}
+WHOLE = ()
+LATE = ()
+SOON = (1,)
+SUMS = (2, 3, 1)
 VMEM = pl.BlockSpec(memory_space=pltpu.VMEM)
 ANY = pl.BlockSpec(memory_space=pl.ANY)
 PARAMS = pltpu.CompilerParams(vmem_limit_bytes=40 * 1024 * 1024)
@@ -149,8 +154,10 @@
     )(keep, got, token)
 
 
-def deal_kernel(block, keep, got, token, *refs):
-    *outs, token_out = refs
+def deal_kernel(block, n_through, n_after, keep, got, token, *refs):
+    through, (*outs, token_out) = refs[:n_through], refs[n_through + n_after :]
+    if through:
+        outs.pop()[...] = through[0][...]
     at = 0
     for out in outs:
         out[...] = keep[at : at + out.shape[0]] + got[at : at + out.shape[0]]
@@ -158,27 +165,41 @@
     token_out[...] = token[...]
 
 
-def deal(keep, got, token, block):
+def deal(keep, got, token, after, block, through=()):
     blocks, width = keep.shape[0] // block, keep.shape[1]
     half = (blocks + 1) // 2
     sizes = [half - 1, 1, half - 1] + ([1] if blocks % 2 == 0 else [])
     shapes = [jax.ShapeDtypeStruct((size * block, width), jnp.float32) for size in sizes if size]
+    shapes += [jax.ShapeDtypeStruct(t.shape, t.dtype) for t in through]
     *outs, token = pl.pallas_call(
-        functools.partial(deal_kernel, block),
+        functools.partial(deal_kernel, block, len(through), len(after)),
         out_shape=(*shapes, TOKEN),
-        in_specs=[VMEM] * 3,
+        in_specs=[VMEM] * (3 + len(through) + len(after)),
         out_specs=[VMEM] * (len(shapes) + 1),
         compiler_params=PARAMS,
         cost_estimate=COST,
         name="deal",
-    )(keep, got, token)
-    return [outs.pop(0) if size else None for size in sizes], token
-
-
-def turn_kernel(n_terms, *refs):
-    terms, (token, out_ref, token_out, turned) = refs[:n_terms], refs[n_terms:]
+    )(keep, got, token, *through, *after)
+    return [outs.pop(0) if size else None for size in sizes], token, outs
+
+
+def turn_kernel(n_terms, n_earlier, copied, n_after, *refs):
+    refs = refs[n_after:]
+    terms, earlier, (token, out_ref, token_out, *joined, turned) = refs[:n_terms], refs[n_terms : n_terms + n_earlier], refs[n_terms + n_earlier :]
     total = sum((term[...] for term in terms[1:]), terms[0][...])
+    turn_rows(total, out_ref, turned)
+    if copied:
+        copies = joined.pop()
+        for k in range(copies.shape[0]):
+            copies[k] = out_ref[...]
+    row = 0
+    for ref in (*earlier, out_ref) if joined else ():
+        joined[0][row : row + ref.shape[0], :] = ref[...]
+        row += ref.shape[0]
     token_out[...] = token[...]
+
+
+def turn_rows(total, out_ref, turned):
     block, width = total.shape
     lanes = out_ref.shape[1] // (block // 2)
     low = lax.broadcasted_iota(jnp.int32, (HALF, lanes), 1) < lanes // 2
@@ -195,18 +216,24 @@
             out_ref[unit * UNIT + HALF : (unit + 1) * UNIT, columns] = jnp.where(low, pltpu.roll(even, lanes // 2, 1), odd)
 
 
-def turn(terms, token, rank):
+def turn(terms, earlier, copies, token, after, rank):
     block, width = terms[0].shape
+    shapes = [jax.ShapeDtypeStruct((width // rank, block * rank), jnp.float32), TOKEN]
+    if earlier:
+        rows = width // rank + sum(e.shape[0] for e in earlier)
+        shapes.append(jax.ShapeDtypeStruct((rows, block * rank), jnp.float32))
+    if copies:
+        shapes.append(jax.ShapeDtypeStruct((copies, width // rank, block * rank), jnp.float32))
     return pl.pallas_call(
-        functools.partial(turn_kernel, len(terms)),
-        out_shape=(jax.ShapeDtypeStruct((width // rank, block * rank), jnp.float32), TOKEN),
-        in_specs=[VMEM] * (len(terms) + 1),
-        out_specs=[VMEM] * 2,
+        functools.partial(turn_kernel, len(terms), len(earlier), copies > 0, len(after)),
+        out_shape=tuple(shapes),
+        in_specs=[VMEM] * (len(terms) + len(earlier) + len(after) + 1),
+        out_specs=[VMEM] * len(shapes),
         scratch_shapes=[pltpu.VMEM((width // rank // UNIT, block * HALF, 2 * rank), jnp.float32)],
         compiler_params=PARAMS,
         cost_estimate=COST,
         name="turn",
-    )(*terms, token)
+    )(*after, *terms, *earlier, token)
 
 
 def split(value):
@@ -214,26 +241,36 @@
     return high, (value - high.astype(jnp.float32)).astype(jnp.bfloat16)
 
 
-def absorb_kernel(first, start, n_aa, n_col, n_mid, per_core, last, token, *refs):
+def absorb_kernel(first, start, rows_start, n_others, n_aa, n_col, n_mid, per_core, last, n_after, token, mine, *refs):
+    refs = refs[n_after:]
     place = [lax.axis_index(name) for name in ("col", "ba", "aa")]
-    rows_in, others_in = refs[:n_col], refs[n_col : n_col + n_aa - 1]
-    refs = refs[n_col + n_aa - 1 + (0 if first else 4) :]
+    n_rows = 0 if rows_start is None else n_col - 1
+    rows_in, others_in = refs[:n_rows], refs[n_rows : n_others + n_rows]
+    refs = refs[n_others + n_rows + (0 if first else 4) :]
     left, left_low, right, right_low, token_out, *outs = refs
     token_out[...] = token[...]
-    count = rows_in[0].shape[0] // UNIT
-    for distance in range(n_col):
-        core = place[0] ^ distance
-        for unit in range(count):
-            high, low = split(rows_in[distance][unit * UNIT : (unit + 1) * UNIT, :])
-            at = (start + unit) * UNIT
-            row = (at // per_core) * n_col * per_core + core * per_core + at % per_core
-            where = pl.ds(pl.multiple_of(row, UNIT), UNIT)
-            left[where, :], left_low[where, :] = high, low
-            if distance == 0:
-                right[0, at : at + UNIT, :], right_low[0, at : at + UNIT, :] = high, low
-    for distance in range(1, n_aa):
+    count = mine.shape[0] // UNIT
+
+    def put_left(unit, core, high, low):
+        at = unit * UNIT
+        row = (at // per_core) * n_col * per_core + core * per_core + at % per_core
+        where = pl.ds(pl.multiple_of(row, UNIT), UNIT)
+        left[where, :], left_low[where, :] = high, low
+
+    for unit in range(count):
+        high, low = split(mine[unit * UNIT : (unit + 1) * UNIT, :])
+        put_left(start + unit, place[0], high, low)
+        where = slice((start + unit) * UNIT, (start + unit + 1) * UNIT)
+        right[0, where, :], right_low[0, where, :] = high, low
+    for i, distance in enumerate(range(1, n_aa)):
         where = slice(start * UNIT, (start + count) * UNIT)
-        right[distance, where, :], right_low[distance, where, :] = split(others_in[distance - 1][...])
+        right[distance, where, :], right_low[distance, where, :] = split(
+            others_in[0][place[2] ^ distance] if n_others == 1 else others_in[i][...]
+        )
+    for distance in range(1, n_rows + 1):
+        ref = rows_in[distance - 1]
+        for unit in range(ref.shape[0] // UNIT):
+            put_left(rows_start + unit, place[0] ^ distance, *split(ref[unit * UNIT : (unit + 1) * UNIT, :]))
     if not last:
         return
     scale = 1.0 / (n_mid * left.shape[1])
@@ -250,14 +287,14 @@
         outs[distance][...] = value * scale
 
 
-def absorb(token, rows, others, held, start, n_aa, n_col, n_mid, per_core, local_rows, last):
-    depth = rows[0].shape[1]
+def absorb(token, after, mine, others, rows, held, start, rows_start, n_aa, n_col, n_mid, per_core, local_rows, last):
+    depth = mine.shape[1]
     shapes = [jax.ShapeDtypeStruct((local_rows, depth), jnp.bfloat16)] * 2
     shapes += [jax.ShapeDtypeStruct((n_aa, n_mid // n_aa * per_core, depth), jnp.bfloat16)] * 2
     shapes += [TOKEN] + [jax.ShapeDtypeStruct((local_rows, per_core), jnp.float32)] * (n_mid if last else 0)
-    n_in = 1 + len(rows) + len(others)
+    n_in = 2 + len(after) + len(others) + len(rows)
     outs = pl.pallas_call(
-        functools.partial(absorb_kernel, not held, start, n_aa, n_col, n_mid, per_core, last),
+        functools.partial(absorb_kernel, not held, start, rows_start, len(others), n_aa, n_col, n_mid, per_core, last, len(after)),
         out_shape=tuple(shapes),
         in_specs=[VMEM] * (n_in + len(held)),
         out_specs=[VMEM] * len(shapes),
@@ -265,7 +302,7 @@
         compiler_params=PARAMS,
         cost_estimate=COST,
         name="gram" if last else "absorb",
-    )(token, *rows, *others, *held)
+    )(token, mine, *after, *rows, *others, *held)
     return outs[:4], outs[4], outs[5:]
 
 
@@ -290,36 +327,65 @@
     keep = list(project(tensor, two_t, three_t, token, second_half, spans[:1], n_mid, per_core, False))
     col_steps, mid_steps = bits_of(n_col), bits_of(n_mid)
     finals, gathered = [[] for _ in spans], [None] * n_chunks
-    held = ()
+    held, mine, rows, shared, waiting, after = (), {}, {}, set(), {}, []
+
+    def take_after():
+        taken = list(after)
+        after.clear()
+        return taken
 
     def first_step(k, token):
         for step in range(1, col_steps):
             send, keep[k], token = fold(keep[k], got[k], token)
             got[k] = exchange(send, "col", 1 << step)
-        (onward, final, keep[k], mine), token = deal(keep[k][0], got[k][0], token, block)
+        (onward, final, keep[k], own), token, _ = deal(keep[k][0], got[k][0], token, take_after(), block)
         got[k] = exchange(onward, "ba", 1)
         if k == 0 and spans[1:]:
             keep.extend(project(tensor, two_t, three_t, token, second_half, spans[1:], n_mid, per_core, False))
-        finals[k] += [mine, exchange(final, "ba", 1)]
+        finals[k].append(own)
+        if k in LATE:
+            waiting[k] = [final]
+        else:
+            finals[k].append(exchange(final, "ba", 1))
         return token
 
     def later_steps(k, token):
         for step in range(1, mid_steps):
-            (onward, final, keep[k]), token = deal(keep[k], got[k], token, block)
+            (onward, final, keep[k]), token, late = deal(keep[k], got[k], token, take_after(), block, waiting.pop(k, []))
+            finals[k] += [exchange(block_late, "ba", 1) for block_late in late]
             if onward is not None:
                 got[k] = exchange(onward, "ba", 1 << step)
             finals[k].append(exchange(final, "ba", 1 << step))
         return token
 
     def finish(k, token):
-        mine, token = turn(finals[k], token, rank)
-        rows = [mine] + [exchange(mine, "col", d) for d in range(1, n_col)]
-        gathered[k] = rows, [exchange(mine, "aa", d) for d in range(1, n_aa)]
+        last = k == n_chunks - 1
+        sent = [c for c in CORE.get(k, ()) if c < k] if k < max(CORE) else []
+        sent = [c for c in range(k) if c not in shared] if last else sent
+        copies = n_aa if k in WHOLE else 0
+        out, token, *joined = turn(finals[k], [mine[c] for c in sent], copies, token, take_after(), rank)
+        mine[k] = out
+        def gather():
+            if copies:
+                gathered[k] = [lax.all_to_all(joined.pop(), "aa", 0, 0, tiled=True)]
+            else:
+                gathered[k] = [exchange(out, "aa", d) for d in range(1, n_aa)]
+
+        source = joined[0] if sent else out
+        if last or k in CORE.get(k, ()):
+            shared.update(sent + [k])
+            rows[k] = [exchange(source, "col", d) for d in range(1, n_col)], spans[min(sent + [k])][0]
+            if k in SOON:
+                after.extend(rows[k][0])
+        gather()
         return token
 
     def take(k, token, held):
         last = k == n_chunks - 1
-        return absorb(token, *gathered[k], held, spans[k][0], n_aa, n_col, n_mid, per_core, local_rows, last)
+        others, (came, rows_start) = gathered[k], rows.get(k, ([], None))
+        return absorb(
+            token, take_after(), mine[k], others, came, held, spans[k][0], rows_start, n_aa, n_col, n_mid, per_core, local_rows, last
+        )
 
     for order in ORDER:
         for name, k in order:
@@ -334,7 +400,7 @@
             else:
                 held, token, sums = take(k, token, held)
     gram = sums[0]
-    for d in range(1, n_mid):
+    for d in SUMS if n_mid == 4 else range(1, n_mid):
         gram = gram + exchange(sums[d], "ba", d)
     return gram
 

time: 79.8 us -> 77.1 us (0.966)
  waiting for transfers between devices: 31.1 us -> 26.7 us
  starting transfers between devices: 33.5 us -> 35.1 us
    ppermute x27, waiting for transfers between devices: 31.1 us -> 26.7 us  [exchange(): return lax.ppermute(x, axis, [(i, i ^ distance) for i in range(n)])]
    ppermute x27, starting transfers between devices: 33.5 us -> 35.1 us  [exchange(): return lax.ppermute(x, axis, [(i, i ^ distance) for i in range(n)])]
  transfers between devices with their start and end apart: 27 -> 27, of which waited for: 11 -> 10; matrix products, arithmetic and copies ran while one was open for 0% -> 0% of each run, Pallas kernels for 8% -> 9%
where the time goes in v4:
time: 77.1 us; the launch traced here: 76.9 us
  starting transfers between devices  35.1 us (46%)
  waiting for transfers between devices  26.7 us (35%)
  Pallas kernels  14.2 us (18%)
    ppermute x27, starting transfers between devices, exchange(): return lax.ppermute(x, axis, [(i, i ^ distance) for i in range(n)])  35.1 us
    ppermute x27, waiting for transfers between devices, exchange(): return lax.ppermute(x, axis, [(i, i ^ distance) for i in range(n)])  26.7 us
    pallas_call x3, Pallas kernels, project(): pl.pallas_call(functools.partial(project_kernel, n_mid, per_core, positio...  11 us
    pallas_call x3, Pallas kernels, absorb(): pl.pallas_call(functools.partial(absorb_kernel, not held, start, rows_sta...  2.5 us
  transfers between devices with their start and end apart: 27, of which 10 were waited for; matrix products, arithmetic and copies ran while one was open for 0% of the time, Pallas kernels for 9%

profile of v4, /device:TPU:0, one launch (start us, length us, event | category | flops | bytes accessed | tf_op | source)
XLA Modules:
  0.0 76.9 jit_solution(5061755498819160658)
XLA Ops:
  0.0 5.4 %project.4 = (f32[1,64,3072]{2,1,0:T(8,128)}, f32[1,64,3072]{2,1,0:T(8,128)}, f32[1,64,2048]{2,1,0:T(8,128)}) custom-call(bf16[256,128,128]{2,1,0:T(8,128)(2,1)} %tensor.5, bf16[64,128]{1,0:T(8,128)(2,1)} %bitcast.14, bf16[64,128]{1,0:T(8,128)(2,1)} %bitcast.17), custom_call_target="tpu_custom_call" | custom-call | flops 1 | bytes 1 | tf_op jit(solution)/shard_map/project/pallas_call | solution.py:124
  6.6 2.3 %project.3 = f32[1,64,3072]{2,1,0:T(8,128)S(1)} custom-call(bf16[256,128,128]{2,1,0:T(8,128)(2,1)} %tensor.5, bf16[64,128]{1,0:T(8,128)(2,1)S(1)} %bitcast.15, bf16[64,128]{1,0:T(8,128)(2,1)S(1)} %bitcast.18, f32[8,128]{1,0:T(8,128)S(1)} %broadcast_in_dim.3.refs_0_.token), custom_call_target="tpu_custom_call" | custom-call | flops 1 | bytes 1 | tf_op jit(solution)/shard_map/project/pallas_call | solution.py:124
  9.0 2.6 %collective-permute-start.2 = (f32[16,3072]{1,0:T(8,128)S(1)}, f32[16,3072]{1,0:T(8,128)S(1)}, u32[]{:S(2)}, u32[]{:S(2)}) collective-permute-start(f32[16,3072]{1,0:T(8,128)S(1)} %get-tuple-element.56), channel_id=1, source_target_pairs={{0,2},{2,0},{4,6},{6,4},{1,3},{3,1},{5,7},{7,5},{8,10},{10,8},{12,... | collective-permute-start | bytes 589832 | tf_op jit(solution)/shard_map/ppermute | solution.py:39
  11.6 3.4 %project.5 = (f32[1,64,3072]{2,1,0:T(8,128)S(1)}, f32[1,64,2048]{2,1,0:T(8,128)S(1)}) custom-call(bf16[256,128,128]{2,1,0:T(8,128)(2,1)} %tensor.5, bf16[64,128]{1,0:T(8,128)(2,1)S(1)} %bitcast.16, bf16[64,128]{1,0:T(8,128)(2,1)S(1)} %bitcast.19, f32[8,128]{1,0:T(8,128)S(1)} %get-tuple-element.52.refs_0_.token), custom_call_target="tpu_custom_call" | custom-call | flops 1 | bytes 1 | tf_op jit(solution)/shard_map/project/pallas_call | solution.py:124
  15.1 2.0 %collective-permute-start.6 = (f32[16,3072]{1,0:T(8,128)S(1)}, f32[16,3072]{1,0:T(8,128)S(1)}, u32[]{:S(2)}, u32[]{:S(2)}) collective-permute-start(f32[16,3072]{1,0:T(8,128)S(1)} %get-tuple-element.66), channel_id=1, source_target_pairs={{0,2},{2,0},{4,6},{6,4},{1,3},{3,1},{5,7},{7,5},{8,10},{10,8},{12,... | collective-permute-start | bytes 589832 | tf_op jit(solution)/shard_map/ppermute | solution.py:39
  17.2 2.8 %collective-permute-start.7 = (f32[16,3072]{1,0:T(8,128)S(1)}, f32[16,3072]{1,0:T(8,128)S(1)}, u32[]{:S(2)}, u32[]{:S(2)}) collective-permute-start(f32[16,3072]{1,0:T(8,128)S(1)} %get-tuple-element.67), channel_id=1, source_target_pairs={{0,4},{2,6},{4,0},{6,2},{1,5},{3,7},{5,1},{7,3},{8,12},{10,14},{12... | collective-permute-start | bytes 589832 | tf_op jit(solution)/shard_map/ppermute | solution.py:39
  19.9 2.0 %collective-permute-start.10 = (f32[16,3072]{1,0:T(8,128)S(1)}, f32[16,3072]{1,0:T(8,128)S(1)}, u32[]{:S(2)}, u32[]{:S(2)}) collective-permute-start(f32[16,3072]{1,0:T(8,128)S(1)} %get-tuple-element.75), channel_id=1, source_target_pairs={{0,2},{2,0},{4,6},{6,4},{1,3},{3,1},{5,7},{7,5},{8,10},{10,8},{12,... | collective-permute-start | bytes 589832 | tf_op jit(solution)/shard_map/ppermute | solution.py:39
  22.0 5.0 %collective-permute-done.8.got = f32[16,3072]{1,0:T(8,128)S(1)} collective-permute-done((f32[16,3072]{1,0:T(8,128)S(1)}, f32[16,3072]{1,0:T(8,128)S(1)}, u32[]{:S(2)}, u32[]{:S(2)}) %collective-permute-start.8) | collective-permute-done | bytes 196640 | tf_op jit(solution)/shard_map/ppermute | solution.py:39
  27.9 2.5 %collective-permute-start.5 = (f32[16,2048]{1,0:T(8,128)S(1)}, f32[16,2048]{1,0:T(8,128)S(1)}, u32[]{:S(2)}, u32[]{:S(2)}) collective-permute-start(f32[16,2048]{1,0:T(8,128)S(1)} %get-tuple-element.64), channel_id=1, source_target_pairs={{0,2},{2,0},{4,6},{6,4},{1,3},{3,1},{5,7},{7,5},{8,10},{10,8},{12,... | collective-permute-start | bytes 393224 | tf_op jit(solution)/shard_map/ppermute | solution.py:39
  30.4 1.0 %collective-permute-done.6.refs_1_ = f32[16,3072]{1,0:T(8,128)S(1)} collective-permute-done((f32[16,3072]{1,0:T(8,128)S(1)}, f32[16,3072]{1,0:T(8,128)S(1)}, u32[]{:S(2)}, u32[]{:S(2)}) %collective-permute-start.6) | collective-permute-done | bytes 196640 | tf_op jit(solution)/shard_map/ppermute | solution.py:39
  31.5 2.5 %collective-permute-start.16 = (f32[48,1024]{1,0:T(8,128)S(1)}, f32[48,1024]{1,0:T(8,128)S(1)}, u32[]{:S(2)}, u32[]{:S(2)}) collective-permute-start(f32[48,1024]{1,0:T(8,128)S(1)} %get-tuple-element.79.mine), channel_id=1, source_target_pairs={{0,24},{8,16},{16,8},{24,0},{1,25},{9,17},{17,9},{25,1},{2,26},{10... | collective-permute-start | bytes 589832 | tf_op jit(solution)/shard_map/ppermute | solution.py:39
  34.5 5.2 %collective-permute-done.10.refs_1_ = f32[16,3072]{1,0:T(8,128)S(1)} collective-permute-done((f32[16,3072]{1,0:T(8,128)S(1)}, f32[16,3072]{1,0:T(8,128)S(1)}, u32[]{:S(2)}, u32[]{:S(2)}) %collective-permute-start.10) | collective-permute-done | bytes 196640 | tf_op jit(solution)/shard_map/ppermute | solution.py:39
  39.7 1.5 %collective-permute-start.14 = (f32[48,1024]{1,0:T(8,128)S(1)}, f32[48,1024]{1,0:T(8,128)S(1)}, u32[]{:S(2)}, u32[]{:S(2)}) collective-permute-start(f32[48,1024]{1,0:T(8,128)S(1)} %get-tuple-element.79.mine), channel_id=1, source_target_pairs={{0,8},{8,0},{16,24},{24,16},{1,9},{9,1},{17,25},{25,17},{2,10},{10... | collective-permute-start | bytes 589832 | tf_op jit(solution)/shard_map/ppermute | solution.py:39
  42.5 2.4 %collective-permute-start.19 = (f32[48,1024]{1,0:T(8,128)S(1)}, f32[48,1024]{1,0:T(8,128)S(1)}, u32[]{:S(2)}, u32[]{:S(2)}) collective-permute-start(f32[48,1024]{1,0:T(8,128)S(1)} %get-tuple-element.80.mine), channel_id=1, source_target_pairs={{0,24},{8,16},{16,8},{24,0},{1,25},{9,17},{17,9},{25,1},{2,26},{10... | collective-permute-start | bytes 589832 | tf_op jit(solution)/shard_map/ppermute | solution.py:39
  46.4 3.4 %collective-permute-start.9 = (f32[16,2048]{1,0:T(8,128)S(1)}, f32[16,2048]{1,0:T(8,128)S(1)}, u32[]{:S(2)}, u32[]{:S(2)}) collective-permute-start(f32[16,2048]{1,0:T(8,128)S(1)} %get-tuple-element.73), channel_id=1, source_target_pairs={{0,4},{2,6},{4,0},{6,2},{1,5},{3,7},{5,1},{7,3},{8,12},{10,14},{12... | collective-permute-start | bytes 393224 | tf_op jit(solution)/shard_map/ppermute | solution.py:39
  49.8 1.6 %collective-permute-start.17 = (f32[48,1024]{1,0:T(8,128)S(1)}, f32[48,1024]{1,0:T(8,128)S(1)}, u32[]{:S(2)}, u32[]{:S(2)}) collective-permute-start(f32[48,1024]{1,0:T(8,128)S(1)} %get-tuple-element.80.mine), channel_id=1, source_target_pairs={{0,8},{8,0},{16,24},{24,16},{1,9},{9,1},{17,25},{25,17},{2,10},{10... | collective-permute-start | bytes 589832 | tf_op jit(solution)/shard_map/ppermute | solution.py:39
  52.3 3.1 %collective-permute-done.9.refs_2_ = f32[16,2048]{1,0:T(8,128)S(1)} collective-permute-done((f32[16,2048]{1,0:T(8,128)S(1)}, f32[16,2048]{1,0:T(8,128)S(1)}, u32[]{:S(2)}, u32[]{:S(2)}) %collective-permute-start.9) | collective-permute-done | bytes 131104 | tf_op jit(solution)/shard_map/ppermute | solution.py:39
  55.5 1.7 %collective-permute-start.23 = (f32[32,1024]{1,0:T(8,128)S(1)}, f32[32,1024]{1,0:T(8,128)S(1)}, u32[]{:S(2)}, u32[]{:S(2)}) collective-permute-start(f32[32,1024]{1,0:T(8,128)S(1)} %get-tuple-element.88.mine), channel_id=1, source_target_pairs={{0,24},{8,16},{16,8},{24,0},{1,25},{9,17},{17,9},{25,1},{2,26},{10... | collective-permute-start | bytes 393224 | tf_op jit(solution)/shard_map/ppermute | solution.py:39
  57.2 1.2 %collective-permute-start.22 = (f32[32,1024]{1,0:T(8,128)S(1)}, f32[32,1024]{1,0:T(8,128)S(1)}, u32[]{:S(2)}, u32[]{:S(2)}) collective-permute-start(f32[32,1024]{1,0:T(8,128)S(1)} %get-tuple-element.88.mine), channel_id=1, source_target_pairs={{0,16},{8,24},{16,0},{24,8},{1,17},{9,25},{17,1},{25,9},{2,18},{10... | collective-permute-start | bytes 393224 | tf_op jit(solution)/shard_map/ppermute | solution.py:39
  59.2 2.3 %collective-permute-done.23.refs_3_ = f32[32,1024]{1,0:T(8,128)S(1)} collective-permute-done((f32[32,1024]{1,0:T(8,128)S(1)}, f32[32,1024]{1,0:T(8,128)S(1)}, u32[]{:S(2)}, u32[]{:S(2)}) %collective-permute-start.23) | collective-permute-done | bytes 131104 | tf_op jit(solution)/shard_map/ppermute | solution.py:39
  61.5 1.3 %collective-permute-done.22.refs_2_ = f32[32,1024]{1,0:T(8,128)S(1)} collective-permute-done((f32[32,1024]{1,0:T(8,128)S(1)}, f32[32,1024]{1,0:T(8,128)S(1)}, u32[]{:S(2)}, u32[]{:S(2)}) %collective-permute-start.22) | collective-permute-done | bytes 131104 | tf_op jit(solution)/shard_map/ppermute | solution.py:39
  63.3 2.2 %gram.1 = (bf16[256,1024]{1,0:T(8,128)(2,1)S(1)}, bf16[256,1024]{1,0:T(8,128)(2,1)S(1)}, bf16[4,128,1024]{2,1,0:T(8,128)(2,1)S(1)}, bf16[4,128,1024]{2,1,0:T(8,1...) custom-call(f32[8,128]{1,0:T(8,128)S(1)} %get-tuple-element.87.token, ...), custom_call_target="tpu_custom_call", output_to_operand_aliasing={{0}: (6, {}), {1}: (7, {}), {2}: (8, {}), {3}: (9, {})} | custom-call | flops 1 | bytes 1 | tf_op jit(solution)/shard_map/gram/pallas_call | solution.py:296
  66.2 2.5 %collective-permute-start.25 = (f32[256,128]{1,0:T(8,128)S(1)}, f32[256,128]{1,0:T(8,128)S(1)}, u32[]{:S(2)}, u32[]{:S(2)}) collective-permute-start(f32[256,128]{1,0:T(8,128)S(1)} %get-tuple-element.95), channel_id=1, source_target_pairs={{0,6},{2,4},{4,2},{6,0},{1,7},{3,5},{5,3},{7,1},{8,14},{10,12},{12... | collective-permute-start | bytes 393224 | tf_op jit(solution)/shard_map/ppermute | solution.py:39
  69.3 7.0 %collective-permute-done.24 = f32[256,128]{1,0:T(8,128)S(1)} collective-permute-done((f32[256,128]{1,0:T(8,128)S(1)}, f32[256,128]{1,0:T(8,128)S(1)}, u32[]{:S(2)}, u32[]{:S(2)}) %collective-permute-start.24) | collective-permute-done | bytes 131104 | tf_op jit(solution)/shard_map/ppermute | solution.py:39
  (51 shorter events, 10.1 us)
Async XLA Ops:
  6.1 8.8 %collective-permute-start.3 = (f32[1,64,3072]{2,1,0:T(8,128)}, f32[1,64,3072]{2,1,0:T(8,128)S(1)}, u32[]{:S(2)}, u32[]{:S(2)}) collective-permute-start(f32[1,64,3072]{2,1,0:T(8,128)} %get-tuple-element.58), channel_id=1, source_target_pairs={{0,1},{1,0},{2,3},{3,2},{4,5},{5,4},{6,7},{7,6},{8,9},{9,8},{10,11... | collective-permute-start | bytes 2359304 | tf_op jit(solution)/shard_map/ppermute | solution.py:39
  6.2 15.8 %collective-permute-start.1 = (f32[1,64,2048]{2,1,0:T(8,128)}, f32[1,64,2048]{2,1,0:T(8,128)S(1)}, u32[]{:S(2)}, u32[]{:S(2)}) collective-permute-start(f32[1,64,2048]{2,1,0:T(8,128)} %get-tuple-element.54), channel_id=1, source_target_pairs={{0,1},{1,0},{2,3},{3,2},{4,5},{5,4},{6,7},{7,6},{8,9},{9,8},{10,11... | collective-permute-start | bytes 1572872 | tf_op jit(solution)/shard_map/ppermute | solution.py:39
  9.0 8.1 %collective-permute-start.2 = (f32[16,3072]{1,0:T(8,128)S(1)}, f32[16,3072]{1,0:T(8,128)S(1)}, u32[]{:S(2)}, u32[]{:S(2)}) collective-permute-start(f32[16,3072]{1,0:T(8,128)S(1)} %get-tuple-element.56), channel_id=1, source_target_pairs={{0,2},{2,0},{4,6},{6,4},{1,3},{3,1},{5,7},{7,5},{8,10},{10,8},{12,... | collective-permute-start | bytes 589832 | tf_op jit(solution)/shard_map/ppermute | solution.py:39
  15.0 12.0 %collective-permute-start.8 = (f32[16,3072]{1,0:T(8,128)S(1)}, f32[16,3072]{1,0:T(8,128)S(1)}, u32[]{:S(2)}, u32[]{:S(2)}) collective-permute-start(f32[16,3072]{1,0:T(8,128)S(1)} %get-tuple-element.69), channel_id=1, source_target_pairs={{0,2},{2,0},{4,6},{6,4},{1,3},{3,1},{5,7},{7,5},{8,10},{10,8},{12,... | collective-permute-start | bytes 589832 | tf_op jit(solution)/shard_map/ppermute | solution.py:39
  15.1 16.3 %collective-permute-start.6 = (f32[16,3072]{1,0:T(8,128)S(1)}, f32[16,3072]{1,0:T(8,128)S(1)}, u32[]{:S(2)}, u32[]{:S(2)}) collective-permute-start(f32[16,3072]{1,0:T(8,128)S(1)} %get-tuple-element.66), channel_id=1, source_target_pairs={{0,2},{2,0},{4,6},{6,4},{1,3},{3,1},{5,7},{7,5},{8,10},{10,8},{12,... | collective-permute-start | bytes 589832 | tf_op jit(solution)/shard_map/ppermute | solution.py:39
  17.2 14.2 %collective-permute-start.7 = (f32[16,3072]{1,0:T(8,128)S(1)}, f32[16,3072]{1,0:T(8,128)S(1)}, u32[]{:S(2)}, u32[]{:S(2)}) collective-permute-start(f32[16,3072]{1,0:T(8,128)S(1)} %get-tuple-element.67), channel_id=1, source_target_pairs={{0,4},{2,6},{4,0},{6,2},{1,5},{3,7},{5,1},{7,3},{8,12},{10,14},{12... | collective-permute-start | bytes 589832 | tf_op jit(solution)/shard_map/ppermute | solution.py:39
  19.9 19.8 %collective-permute-start.10 = (f32[16,3072]{1,0:T(8,128)S(1)}, f32[16,3072]{1,0:T(8,128)S(1)}, u32[]{:S(2)}, u32[]{:S(2)}) collective-permute-start(f32[16,3072]{1,0:T(8,128)S(1)} %get-tuple-element.75), channel_id=1, source_target_pairs={{0,2},{2,0},{4,6},{6,4},{1,3},{3,1},{5,7},{7,5},{8,10},{10,8},{12,... | collective-permute-start | bytes 589832 | tf_op jit(solution)/shard_map/ppermute | solution.py:39
  27.1 14.7 %collective-permute-start.11 = (f32[16,3072]{1,0:T(8,128)S(1)}, f32[16,3072]{1,0:T(8,128)S(1)}, u32[]{:S(2)}, u32[]{:S(2)}) collective-permute-start(f32[16,3072]{1,0:T(8,128)S(1)} %get-tuple-element.76), channel_id=1, source_target_pairs={{0,4},{2,6},{4,0},{6,2},{1,5},{3,7},{5,1},{7,3},{8,12},{10,14},{12... | collective-permute-start | bytes 589832 | tf_op jit(solution)/shard_map/ppermute | solution.py:39
  27.9 13.8 %collective-permute-start.5 = (f32[16,2048]{1,0:T(8,128)S(1)}, f32[16,2048]{1,0:T(8,128)S(1)}, u32[]{:S(2)}, u32[]{:S(2)}) collective-permute-start(f32[16,2048]{1,0:T(8,128)S(1)} %get-tuple-element.64), channel_id=1, source_target_pairs={{0,2},{2,0},{4,6},{6,4},{1,3},{3,1},{5,7},{7,5},{8,10},{10,8},{12,... | collective-permute-start | bytes 393224 | tf_op jit(solution)/shard_map/ppermute | solution.py:39
  31.5 11.0 %collective-permute-start.16 = (f32[48,1024]{1,0:T(8,128)S(1)}, f32[48,1024]{1,0:T(8,128)S(1)}, u32[]{:S(2)}, u32[]{:S(2)}) collective-permute-start(f32[48,1024]{1,0:T(8,128)S(1)} %get-tuple-element.79.mine), channel_id=1, source_target_pairs={{0,24},{8,16},{16,8},{24,0},{1,25},{9,17},{17,9},{25,1},{2,26},{10... | collective-permute-start | bytes 589832 | tf_op jit(solution)/shard_map/ppermute | solution.py:39
  34.0 10.9 %collective-permute-start.15 = (f32[48,1024]{1,0:T(8,128)S(1)}, f32[48,1024]{1,0:T(8,128)S(1)}, u32[]{:S(2)}, u32[]{:S(2)}) collective-permute-start(f32[48,1024]{1,0:T(8,128)S(1)} %get-tuple-element.79.mine), channel_id=1, source_target_pairs={{0,16},{8,24},{16,0},{24,8},{1,17},{9,25},{17,1},{25,9},{2,18},{10... | collective-permute-start | bytes 589832 | tf_op jit(solution)/shard_map/ppermute | solution.py:39
  39.7 5.7 %collective-permute-start.14 = (f32[48,1024]{1,0:T(8,128)S(1)}, f32[48,1024]{1,0:T(8,128)S(1)}, u32[]{:S(2)}, u32[]{:S(2)}) collective-permute-start(f32[48,1024]{1,0:T(8,128)S(1)} %get-tuple-element.79.mine), channel_id=1, source_target_pairs={{0,8},{8,0},{16,24},{24,16},{1,9},{9,1},{17,25},{25,17},{2,10},{10... | collective-permute-start | bytes 589832 | tf_op jit(solution)/shard_map/ppermute | solution.py:39
  41.9 7.9 %collective-permute-start.12 = (f32[48,1024]{1,0:T(8,128)S(1)}, f32[48,1024]{1,0:T(8,128)S(1)}, u32[]{:S(2)}, u32[]{:S(2)}) collective-permute-start(f32[48,1024]{1,0:T(8,128)S(1)} %get-tuple-element.80.mine), channel_id=1, source_target_pairs={{0,1},{1,0},{2,3},{3,2},{4,5},{5,4},{6,7},{7,6},{8,9},{9,8},{10,11... | collective-permute-start | bytes 589832 | tf_op jit(solution)/shard_map/ppermute | solution.py:39
  42.5 15.9 %collective-permute-start.19 = (f32[48,1024]{1,0:T(8,128)S(1)}, f32[48,1024]{1,0:T(8,128)S(1)}, u32[]{:S(2)}, u32[]{:S(2)}) collective-permute-start(f32[48,1024]{1,0:T(8,128)S(1)} %get-tuple-element.80.mine), channel_id=1, source_target_pairs={{0,24},{8,16},{16,8},{24,0},{1,25},{9,17},{17,9},{25,1},{2,26},{10... | collective-permute-start | bytes 589832 | tf_op jit(solution)/shard_map/ppermute | solution.py:39
  44.9 14.1 %collective-permute-start.18 = (f32[48,1024]{1,0:T(8,128)S(1)}, f32[48,1024]{1,0:T(8,128)S(1)}, u32[]{:S(2)}, u32[]{:S(2)}) collective-permute-start(f32[48,1024]{1,0:T(8,128)S(1)} %get-tuple-element.80.mine), channel_id=1, source_target_pairs={{0,16},{8,24},{16,0},{24,8},{1,17},{9,25},{17,1},{25,9},{2,18},{10... | collective-permute-start | bytes 589832 | tf_op jit(solution)/shard_map/ppermute | solution.py:39
  45.4 6.8 %collective-permute-start.4 = (f32[16,2048]{1,0:T(8,128)S(1)}, f32[16,2048]{1,0:T(8,128)S(1)}, u32[]{:S(2)}, u32[]{:S(2)}) collective-permute-start(f32[16,2048]{1,0:T(8,128)S(1)} %get-tuple-element.62), channel_id=1, source_target_pairs={{0,2},{2,0},{4,6},{6,4},{1,3},{3,1},{5,7},{7,5},{8,10},{10,8},{12,... | collective-permute-start | bytes 393224 | tf_op jit(solution)/shard_map/ppermute | solution.py:39
  46.4 8.9 %collective-permute-start.9 = (f32[16,2048]{1,0:T(8,128)S(1)}, f32[16,2048]{1,0:T(8,128)S(1)}, u32[]{:S(2)}, u32[]{:S(2)}) collective-permute-start(f32[16,2048]{1,0:T(8,128)S(1)} %get-tuple-element.73), channel_id=1, source_target_pairs={{0,4},{2,6},{4,0},{6,2},{1,5},{3,7},{5,1},{7,3},{8,12},{10,14},{12... | collective-permute-start | bytes 393224 | tf_op jit(solution)/shard_map/ppermute | solution.py:39
  49.8 9.2 %collective-permute-start.17 = (f32[48,1024]{1,0:T(8,128)S(1)}, f32[48,1024]{1,0:T(8,128)S(1)}, u32[]{:S(2)}, u32[]{:S(2)}) collective-permute-start(f32[48,1024]{1,0:T(8,128)S(1)} %get-tuple-element.80.mine), channel_id=1, source_target_pairs={{0,8},{8,0},{16,24},{24,16},{1,9},{9,1},{17,25},{25,17},{2,10},{10... | collective-permute-start | bytes 589832 | tf_op jit(solution)/shard_map/ppermute | solution.py:39
  55.5 6.0 %collective-permute-start.23 = (f32[32,1024]{1,0:T(8,128)S(1)}, f32[32,1024]{1,0:T(8,128)S(1)}, u32[]{:S(2)}, u32[]{:S(2)}) collective-permute-start(f32[32,1024]{1,0:T(8,128)S(1)} %get-tuple-element.88.mine), channel_id=1, source_target_pairs={{0,24},{8,16},{16,8},{24,0},{1,25},{9,17},{17,9},{25,1},{2,26},{10... | collective-permute-start | bytes 393224 | tf_op jit(solution)/shard_map/ppermute | solution.py:39
  57.2 5.7 %collective-permute-start.22 = (f32[32,1024]{1,0:T(8,128)S(1)}, f32[32,1024]{1,0:T(8,128)S(1)}, u32[]{:S(2)}, u32[]{:S(2)}) collective-permute-start(f32[32,1024]{1,0:T(8,128)S(1)} %get-tuple-element.88.mine), channel_id=1, source_target_pairs={{0,16},{8,24},{16,0},{24,8},{1,17},{9,25},{17,1},{25,9},{2,18},{10... | collective-permute-start | bytes 393224 | tf_op jit(solution)/shard_map/ppermute | solution.py:39
  58.4 5.0 %collective-permute-start.21 = (f32[32,1024]{1,0:T(8,128)S(1)}, f32[32,1024]{1,0:T(8,128)S(1)}, u32[]{:S(2)}, u32[]{:S(2)}) collective-permute-start(f32[32,1024]{1,0:T(8,128)S(1)} %get-tuple-element.88.mine), channel_id=1, source_target_pairs={{0,8},{8,0},{16,24},{24,16},{1,9},{9,1},{17,25},{25,17},{2,10},{10... | collective-permute-start | bytes 393224 | tf_op jit(solution)/shard_map/ppermute | solution.py:39
  65.6 10.7 %collective-permute-start.24 = (f32[256,128]{1,0:T(8,128)S(1)}, f32[256,128]{1,0:T(8,128)S(1)}, u32[]{:S(2)}, u32[]{:S(2)}) collective-permute-start(f32[256,128]{1,0:T(8,128)S(1)} %get-tuple-element.94), channel_id=1, source_target_pairs={{0,4},{2,6},{4,0},{6,2},{1,5},{3,7},{5,1},{7,3},{8,12},{10,14},{12... | collective-permute-start | bytes 393224 | tf_op jit(solution)/shard_map/ppermute | solution.py:39
  66.2 10.0 %collective-permute-start.25 = (f32[256,128]{1,0:T(8,128)S(1)}, f32[256,128]{1,0:T(8,128)S(1)}, u32[]{:S(2)}, u32[]{:S(2)}) collective-permute-start(f32[256,128]{1,0:T(8,128)S(1)} %get-tuple-element.95), channel_id=1, source_target_pairs={{0,6},{2,4},{4,2},{6,0},{1,7},{3,5},{5,3},{7,1},{8,14},{10,12},{12... | collective-permute-start | bytes 393224 | tf_op jit(solution)/shard_map/ppermute | solution.py:39
  68.7 7.6 %collective-permute-start.26 = (f32[256,128]{1,0:T(8,128)S(1)}, f32[256,128]{1,0:T(8,128)S(1)}, u32[]{:S(2)}, u32[]{:S(2)}) collective-permute-start(f32[256,128]{1,0:T(8,128)S(1)} %get-tuple-element.96), channel_id=1, source_target_pairs={{0,2},{2,0},{4,6},{6,4},{1,3},{3,1},{5,7},{7,5},{8,10},{10,8},{12,... | collective-permute-start | bytes 393224 | tf_op jit(solution)/shard_map/ppermute | solution.py:39
  (5 other events, 25.7 us)

commit v5 on v4

--- a/solution.py
+++ b/solution.py
@@ -283,7 +283,8 @@
         block = (goal // share) ^ place[2]
         rows = pl.ds(pl.multiple_of((goal % share) * per_core, UNIT), per_core)
         high, low = right[block, rows, :], right_low[block, rows, :]
-        value = dot(left[...], high) + (dot(left[...], low) + dot(left_low[...], high))
+        both = dot(left[...], jnp.concatenate([high, low], axis=0))
+        value = both[:, :per_core] + (both[:, per_core:] + dot(left_low[...], high))
         outs[distance][...] = value * scale
 
 

time: 77.1 us -> 76.7 us (level)
  no operation moved by 1% of the time
where the time goes in v5:
time: 76.7 us; the launch traced here: 76.5 us
  starting transfers between devices  35.1 us (46%)
  waiting for transfers between devices  26.7 us (35%)
  Pallas kernels  13.8 us (18%)
    ppermute x27, starting transfers between devices, exchange(): return lax.ppermute(x, axis, [(i, i ^ distance) for i in range(n)])  35.1 us
    ppermute x27, waiting for transfers between devices, exchange(): return lax.ppermute(x, axis, [(i, i ^ distance) for i in range(n)])  26.7 us
    pallas_call x3, Pallas kernels, project(): pl.pallas_call(functools.partial(project_kernel, n_mid, per_core, positio...  11 us
    pallas_call x3, Pallas kernels, absorb(): pl.pallas_call(functools.partial(absorb_kernel, not held, start, rows_sta...  2.07 us
  transfers between devices with their start and end apart: 27, of which 10 were waited for; matrix products, arithmetic and copies ran while one was open for 0% of the time, Pallas kernels for 9%

profile of v5, /device:TPU:0, one launch (start us, length us, event | category | flops | bytes accessed | tf_op | source)
XLA Modules:
  0.0 76.5 jit_solution(5087063838989399680)
XLA Ops:
  0.0 5.4 %project.4 = (f32[1,64,3072]{2,1,0:T(8,128)}, f32[1,64,3072]{2,1,0:T(8,128)}, f32[1,64,2048]{2,1,0:T(8,128)}) custom-call(bf16[256,128,128]{2,1,0:T(8,128)(2,1)} %tensor.5, bf16[64,128]{1,0:T(8,128)(2,1)} %bitcast.14, bf16[64,128]{1,0:T(8,128)(2,1)} %bitcast.17), custom_call_target="tpu_custom_call" | custom-call | flops 1 | bytes 1 | tf_op jit(solution)/shard_map/project/pallas_call | solution.py:124
  6.6 2.3 %project.3 = f32[1,64,3072]{2,1,0:T(8,128)S(1)} custom-call(bf16[256,128,128]{2,1,0:T(8,128)(2,1)} %tensor.5, bf16[64,128]{1,0:T(8,128)(2,1)S(1)} %bitcast.15, bf16[64,128]{1,0:T(8,128)(2,1)S(1)} %bitcast.18, f32[8,128]{1,0:T(8,128)S(1)} %broadcast_in_dim.3.refs_0_.token), custom_call_target="tpu_custom_call" | custom-call | flops 1 | bytes 1 | tf_op jit(solution)/shard_map/project/pallas_call | solution.py:124
  9.0 2.6 %collective-permute-start.2 = (f32[16,3072]{1,0:T(8,128)S(1)}, f32[16,3072]{1,0:T(8,128)S(1)}, u32[]{:S(2)}, u32[]{:S(2)}) collective-permute-start(f32[16,3072]{1,0:T(8,128)S(1)} %get-tuple-element.56), channel_id=1, source_target_pairs={{0,2},{2,0},{4,6},{6,4},{1,3},{3,1},{5,7},{7,5},{8,10},{10,8},{12,... | collective-permute-start | bytes 589832 | tf_op jit(solution)/shard_map/ppermute | solution.py:39
  11.6 3.4 %project.5 = (f32[1,64,3072]{2,1,0:T(8,128)S(1)}, f32[1,64,2048]{2,1,0:T(8,128)S(1)}) custom-call(bf16[256,128,128]{2,1,0:T(8,128)(2,1)} %tensor.5, bf16[64,128]{1,0:T(8,128)(2,1)S(1)} %bitcast.16, bf16[64,128]{1,0:T(8,128)(2,1)S(1)} %bitcast.19, f32[8,128]{1,0:T(8,128)S(1)} %get-tuple-element.52.refs_0_.token), custom_call_target="tpu_custom_call" | custom-call | flops 1 | bytes 1 | tf_op jit(solution)/shard_map/project/pallas_call | solution.py:124
  15.1 2.0 %collective-permute-start.6 = (f32[16,3072]{1,0:T(8,128)S(1)}, f32[16,3072]{1,0:T(8,128)S(1)}, u32[]{:S(2)}, u32[]{:S(2)}) collective-permute-start(f32[16,3072]{1,0:T(8,128)S(1)} %get-tuple-element.66), channel_id=1, source_target_pairs={{0,2},{2,0},{4,6},{6,4},{1,3},{3,1},{5,7},{7,5},{8,10},{10,8},{12,... | collective-permute-start | bytes 589832 | tf_op jit(solution)/shard_map/ppermute | solution.py:39
  17.2 2.8 %collective-permute-start.7 = (f32[16,3072]{1,0:T(8,128)S(1)}, f32[16,3072]{1,0:T(8,128)S(1)}, u32[]{:S(2)}, u32[]{:S(2)}) collective-permute-start(f32[16,3072]{1,0:T(8,128)S(1)} %get-tuple-element.67), channel_id=1, source_target_pairs={{0,4},{2,6},{4,0},{6,2},{1,5},{3,7},{5,1},{7,3},{8,12},{10,14},{12... | collective-permute-start | bytes 589832 | tf_op jit(solution)/shard_map/ppermute | solution.py:39
  19.9 2.0 %collective-permute-start.10 = (f32[16,3072]{1,0:T(8,128)S(1)}, f32[16,3072]{1,0:T(8,128)S(1)}, u32[]{:S(2)}, u32[]{:S(2)}) collective-permute-start(f32[16,3072]{1,0:T(8,128)S(1)} %get-tuple-element.75), channel_id=1, source_target_pairs={{0,2},{2,0},{4,6},{6,4},{1,3},{3,1},{5,7},{7,5},{8,10},{10,8},{12,... | collective-permute-start | bytes 589832 | tf_op jit(solution)/shard_map/ppermute | solution.py:39
  22.0 5.0 %collective-permute-done.8.got = f32[16,3072]{1,0:T(8,128)S(1)} collective-permute-done((f32[16,3072]{1,0:T(8,128)S(1)}, f32[16,3072]{1,0:T(8,128)S(1)}, u32[]{:S(2)}, u32[]{:S(2)}) %collective-permute-start.8) | collective-permute-done | bytes 196640 | tf_op jit(solution)/shard_map/ppermute | solution.py:39
  27.9 2.5 %collective-permute-start.5 = (f32[16,2048]{1,0:T(8,128)S(1)}, f32[16,2048]{1,0:T(8,128)S(1)}, u32[]{:S(2)}, u32[]{:S(2)}) collective-permute-start(f32[16,2048]{1,0:T(8,128)S(1)} %get-tuple-element.64), channel_id=1, source_target_pairs={{0,2},{2,0},{4,6},{6,4},{1,3},{3,1},{5,7},{7,5},{8,10},{10,8},{12,... | collective-permute-start | bytes 393224 | tf_op jit(solution)/shard_map/ppermute | solution.py:39
  30.4 1.0 %collective-permute-done.6.refs_1_ = f32[16,3072]{1,0:T(8,128)S(1)} collective-permute-done((f32[16,3072]{1,0:T(8,128)S(1)}, f32[16,3072]{1,0:T(8,128)S(1)}, u32[]{:S(2)}, u32[]{:S(2)}) %collective-permute-start.6) | collective-permute-done | bytes 196640 | tf_op jit(solution)/shard_map/ppermute | solution.py:39
  31.5 2.5 %collective-permute-start.16 = (f32[48,1024]{1,0:T(8,128)S(1)}, f32[48,1024]{1,0:T(8,128)S(1)}, u32[]{:S(2)}, u32[]{:S(2)}) collective-permute-start(f32[48,1024]{1,0:T(8,128)S(1)} %get-tuple-element.79.mine), channel_id=1, source_target_pairs={{0,24},{8,16},{16,8},{24,0},{1,25},{9,17},{17,9},{25,1},{2,26},{10... | collective-permute-start | bytes 589832 | tf_op jit(solution)/shard_map/ppermute | solution.py:39
  34.5 5.2 %collective-permute-done.10.refs_1_ = f32[16,3072]{1,0:T(8,128)S(1)} collective-permute-done((f32[16,3072]{1,0:T(8,128)S(1)}, f32[16,3072]{1,0:T(8,128)S(1)}, u32[]{:S(2)}, u32[]{:S(2)}) %collective-permute-start.10) | collective-permute-done | bytes 196640 | tf_op jit(solution)/shard_map/ppermute | solution.py:39
  39.7 1.5 %collective-permute-start.14 = (f32[48,1024]{1,0:T(8,128)S(1)}, f32[48,1024]{1,0:T(8,128)S(1)}, u32[]{:S(2)}, u32[]{:S(2)}) collective-permute-start(f32[48,1024]{1,0:T(8,128)S(1)} %get-tuple-element.79.mine), channel_id=1, source_target_pairs={{0,8},{8,0},{16,24},{24,16},{1,9},{9,1},{17,25},{25,17},{2,10},{10... | collective-permute-start | bytes 589832 | tf_op jit(solution)/shard_map/ppermute | solution.py:39
  42.5 2.4 %collective-permute-start.19 = (f32[48,1024]{1,0:T(8,128)S(1)}, f32[48,1024]{1,0:T(8,128)S(1)}, u32[]{:S(2)}, u32[]{:S(2)}) collective-permute-start(f32[48,1024]{1,0:T(8,128)S(1)} %get-tuple-element.80.mine), channel_id=1, source_target_pairs={{0,24},{8,16},{16,8},{24,0},{1,25},{9,17},{17,9},{25,1},{2,26},{10... | collective-permute-start | bytes 589832 | tf_op jit(solution)/shard_map/ppermute | solution.py:39
  46.4 3.4 %collective-permute-start.9 = (f32[16,2048]{1,0:T(8,128)S(1)}, f32[16,2048]{1,0:T(8,128)S(1)}, u32[]{:S(2)}, u32[]{:S(2)}) collective-permute-start(f32[16,2048]{1,0:T(8,128)S(1)} %get-tuple-element.73), channel_id=1, source_target_pairs={{0,4},{2,6},{4,0},{6,2},{1,5},{3,7},{5,1},{7,3},{8,12},{10,14},{12... | collective-permute-start | bytes 393224 | tf_op jit(solution)/shard_map/ppermute | solution.py:39
  49.8 1.6 %collective-permute-start.17 = (f32[48,1024]{1,0:T(8,128)S(1)}, f32[48,1024]{1,0:T(8,128)S(1)}, u32[]{:S(2)}, u32[]{:S(2)}) collective-permute-start(f32[48,1024]{1,0:T(8,128)S(1)} %get-tuple-element.80.mine), channel_id=1, source_target_pairs={{0,8},{8,0},{16,24},{24,16},{1,9},{9,1},{17,25},{25,17},{2,10},{10... | collective-permute-start | bytes 589832 | tf_op jit(solution)/shard_map/ppermute | solution.py:39
  52.3 3.1 %collective-permute-done.9.refs_2_ = f32[16,2048]{1,0:T(8,128)S(1)} collective-permute-done((f32[16,2048]{1,0:T(8,128)S(1)}, f32[16,2048]{1,0:T(8,128)S(1)}, u32[]{:S(2)}, u32[]{:S(2)}) %collective-permute-start.9) | collective-permute-done | bytes 131104 | tf_op jit(solution)/shard_map/ppermute | solution.py:39
  55.5 1.7 %collective-permute-start.23 = (f32[32,1024]{1,0:T(8,128)S(1)}, f32[32,1024]{1,0:T(8,128)S(1)}, u32[]{:S(2)}, u32[]{:S(2)}) collective-permute-start(f32[32,1024]{1,0:T(8,128)S(1)} %get-tuple-element.88.mine), channel_id=1, source_target_pairs={{0,24},{8,16},{16,8},{24,0},{1,25},{9,17},{17,9},{25,1},{2,26},{10... | collective-permute-start | bytes 393224 | tf_op jit(solution)/shard_map/ppermute | solution.py:39
  57.2 1.2 %collective-permute-start.22 = (f32[32,1024]{1,0:T(8,128)S(1)}, f32[32,1024]{1,0:T(8,128)S(1)}, u32[]{:S(2)}, u32[]{:S(2)}) collective-permute-start(f32[32,1024]{1,0:T(8,128)S(1)} %get-tuple-element.88.mine), channel_id=1, source_target_pairs={{0,16},{8,24},{16,0},{24,8},{1,17},{9,25},{17,1},{25,9},{2,18},{10... | collective-permute-start | bytes 393224 | tf_op jit(solution)/shard_map/ppermute | solution.py:39
  59.2 2.3 %collective-permute-done.23.refs_3_ = f32[32,1024]{1,0:T(8,128)S(1)} collective-permute-done((f32[32,1024]{1,0:T(8,128)S(1)}, f32[32,1024]{1,0:T(8,128)S(1)}, u32[]{:S(2)}, u32[]{:S(2)}) %collective-permute-start.23) | collective-permute-done | bytes 131104 | tf_op jit(solution)/shard_map/ppermute | solution.py:39
  61.5 1.3 %collective-permute-done.22.refs_2_ = f32[32,1024]{1,0:T(8,128)S(1)} collective-permute-done((f32[32,1024]{1,0:T(8,128)S(1)}, f32[32,1024]{1,0:T(8,128)S(1)}, u32[]{:S(2)}, u32[]{:S(2)}) %collective-permute-start.22) | collective-permute-done | bytes 131104 | tf_op jit(solution)/shard_map/ppermute | solution.py:39
  63.3 1.8 %gram.1 = (bf16[256,1024]{1,0:T(8,128)(2,1)S(1)}, bf16[256,1024]{1,0:T(8,128)(2,1)S(1)}, bf16[4,128,1024]{2,1,0:T(8,128)(2,1)S(1)}, bf16[4,128,1024]{2,1,0:T(8,1...) custom-call(f32[8,128]{1,0:T(8,128)S(1)} %get-tuple-element.87.token, ...), custom_call_target="tpu_custom_call", output_to_operand_aliasing={{0}: (6, {}), {1}: (7, {}), {2}: (8, {}), {3}: (9, {})} | custom-call | flops 1 | bytes 1 | tf_op jit(solution)/shard_map/gram/pallas_call | solution.py:297
  65.8 2.5 %collective-permute-start.25 = (f32[256,128]{1,0:T(8,128)S(1)}, f32[256,128]{1,0:T(8,128)S(1)}, u32[]{:S(2)}, u32[]{:S(2)}) collective-permute-start(f32[256,128]{1,0:T(8,128)S(1)} %get-tuple-element.95), channel_id=1, source_target_pairs={{0,6},{2,4},{4,2},{6,0},{1,7},{3,5},{5,3},{7,1},{8,14},{10,12},{12... | collective-permute-start | bytes 393224 | tf_op jit(solution)/shard_map/ppermute | solution.py:39
  68.8 7.0 %collective-permute-done.24 = f32[256,128]{1,0:T(8,128)S(1)} collective-permute-done((f32[256,128]{1,0:T(8,128)S(1)}, f32[256,128]{1,0:T(8,128)S(1)}, u32[]{:S(2)}, u32[]{:S(2)}) %collective-permute-start.24) | collective-permute-done | bytes 131104 | tf_op jit(solution)/shard_map/ppermute | solution.py:39
  (51 shorter events, 10.1 us)
Async XLA Ops:
  6.1 8.8 %collective-permute-start.3 = (f32[1,64,3072]{2,1,0:T(8,128)}, f32[1,64,3072]{2,1,0:T(8,128)S(1)}, u32[]{:S(2)}, u32[]{:S(2)}) collective-permute-start(f32[1,64,3072]{2,1,0:T(8,128)} %get-tuple-element.58), channel_id=1, source_target_pairs={{0,1},{1,0},{2,3},{3,2},{4,5},{5,4},{6,7},{7,6},{8,9},{9,8},{10,11... | collective-permute-start | bytes 2359304 | tf_op jit(solution)/shard_map/ppermute | solution.py:39
  6.2 15.8 %collective-permute-start.1 = (f32[1,64,2048]{2,1,0:T(8,128)}, f32[1,64,2048]{2,1,0:T(8,128)S(1)}, u32[]{:S(2)}, u32[]{:S(2)}) collective-permute-start(f32[1,64,2048]{2,1,0:T(8,128)} %get-tuple-element.54), channel_id=1, source_target_pairs={{0,1},{1,0},{2,3},{3,2},{4,5},{5,4},{6,7},{7,6},{8,9},{9,8},{10,11... | collective-permute-start | bytes 1572872 | tf_op jit(solution)/shard_map/ppermute | solution.py:39
  9.0 8.1 %collective-permute-start.2 = (f32[16,3072]{1,0:T(8,128)S(1)}, f32[16,3072]{1,0:T(8,128)S(1)}, u32[]{:S(2)}, u32[]{:S(2)}) collective-permute-start(f32[16,3072]{1,0:T(8,128)S(1)} %get-tuple-element.56), channel_id=1, source_target_pairs={{0,2},{2,0},{4,6},{6,4},{1,3},{3,1},{5,7},{7,5},{8,10},{10,8},{12,... | collective-permute-start | bytes 589832 | tf_op jit(solution)/shard_map/ppermute | solution.py:39
  15.0 12.0 %collective-permute-start.8 = (f32[16,3072]{1,0:T(8,128)S(1)}, f32[16,3072]{1,0:T(8,128)S(1)}, u32[]{:S(2)}, u32[]{:S(2)}) collective-permute-start(f32[16,3072]{1,0:T(8,128)S(1)} %get-tuple-element.69), channel_id=1, source_target_pairs={{0,2},{2,0},{4,6},{6,4},{1,3},{3,1},{5,7},{7,5},{8,10},{10,8},{12,... | collective-permute-start | bytes 589832 | tf_op jit(solution)/shard_map/ppermute | solution.py:39
  15.1 16.3 %collective-permute-start.6 = (f32[16,3072]{1,0:T(8,128)S(1)}, f32[16,3072]{1,0:T(8,128)S(1)}, u32[]{:S(2)}, u32[]{:S(2)}) collective-permute-start(f32[16,3072]{1,0:T(8,128)S(1)} %get-tuple-element.66), channel_id=1, source_target_pairs={{0,2},{2,0},{4,6},{6,4},{1,3},{3,1},{5,7},{7,5},{8,10},{10,8},{12,... | collective-permute-start | bytes 589832 | tf_op jit(solution)/shard_map/ppermute | solution.py:39
  17.2 14.2 %collective-permute-start.7 = (f32[16,3072]{1,0:T(8,128)S(1)}, f32[16,3072]{1,0:T(8,128)S(1)}, u32[]{:S(2)}, u32[]{:S(2)}) collective-permute-start(f32[16,3072]{1,0:T(8,128)S(1)} %get-tuple-element.67), channel_id=1, source_target_pairs={{0,4},{2,6},{4,0},{6,2},{1,5},{3,7},{5,1},{7,3},{8,12},{10,14},{12... | collective-permute-start | bytes 589832 | tf_op jit(solution)/shard_map/ppermute | solution.py:39
  19.9 19.8 %collective-permute-start.10 = (f32[16,3072]{1,0:T(8,128)S(1)}, f32[16,3072]{1,0:T(8,128)S(1)}, u32[]{:S(2)}, u32[]{:S(2)}) collective-permute-start(f32[16,3072]{1,0:T(8,128)S(1)} %get-tuple-element.75), channel_id=1, source_target_pairs={{0,2},{2,0},{4,6},{6,4},{1,3},{3,1},{5,7},{7,5},{8,10},{10,8},{12,... | collective-permute-start | bytes 589832 | tf_op jit(solution)/shard_map/ppermute | solution.py:39
  27.1 14.7 %collective-permute-start.11 = (f32[16,3072]{1,0:T(8,128)S(1)}, f32[16,3072]{1,0:T(8,128)S(1)}, u32[]{:S(2)}, u32[]{:S(2)}) collective-permute-start(f32[16,3072]{1,0:T(8,128)S(1)} %get-tuple-element.76), channel_id=1, source_target_pairs={{0,4},{2,6},{4,0},{6,2},{1,5},{3,7},{5,1},{7,3},{8,12},{10,14},{12... | collective-permute-start | bytes 589832 | tf_op jit(solution)/shard_map/ppermute | solution.py:39
  27.9 13.8 %collective-permute-start.5 = (f32[16,2048]{1,0:T(8,128)S(1)}, f32[16,2048]{1,0:T(8,128)S(1)}, u32[]{:S(2)}, u32[]{:S(2)}) collective-permute-start(f32[16,2048]{1,0:T(8,128)S(1)} %get-tuple-element.64), channel_id=1, source_target_pairs={{0,2},{2,0},{4,6},{6,4},{1,3},{3,1},{5,7},{7,5},{8,10},{10,8},{12,... | collective-permute-start | bytes 393224 | tf_op jit(solution)/shard_map/ppermute | solution.py:39
  31.5 11.0 %collective-permute-start.16 = (f32[48,1024]{1,0:T(8,128)S(1)}, f32[48,1024]{1,0:T(8,128)S(1)}, u32[]{:S(2)}, u32[]{:S(2)}) collective-permute-start(f32[48,1024]{1,0:T(8,128)S(1)} %get-tuple-element.79.mine), channel_id=1, source_target_pairs={{0,24},{8,16},{16,8},{24,0},{1,25},{9,17},{17,9},{25,1},{2,26},{10... | collective-permute-start | bytes 589832 | tf_op jit(solution)/shard_map/ppermute | solution.py:39
  34.0 10.9 %collective-permute-start.15 = (f32[48,1024]{1,0:T(8,128)S(1)}, f32[48,1024]{1,0:T(8,128)S(1)}, u32[]{:S(2)}, u32[]{:S(2)}) collective-permute-start(f32[48,1024]{1,0:T(8,128)S(1)} %get-tuple-element.79.mine), channel_id=1, source_target_pairs={{0,16},{8,24},{16,0},{24,8},{1,17},{9,25},{17,1},{25,9},{2,18},{10... | collective-permute-start | bytes 589832 | tf_op jit(solution)/shard_map/ppermute | solution.py:39
  39.7 5.7 %collective-permute-start.14 = (f32[48,1024]{1,0:T(8,128)S(1)}, f32[48,1024]{1,0:T(8,128)S(1)}, u32[]{:S(2)}, u32[]{:S(2)}) collective-permute-start(f32[48,1024]{1,0:T(8,128)S(1)} %get-tuple-element.79.mine), channel_id=1, source_target_pairs={{0,8},{8,0},{16,24},{24,16},{1,9},{9,1},{17,25},{25,17},{2,10},{10... | collective-permute-start | bytes 589832 | tf_op jit(solution)/shard_map/ppermute | solution.py:39
  41.9 7.9 %collective-permute-start.12 = (f32[48,1024]{1,0:T(8,128)S(1)}, f32[48,1024]{1,0:T(8,128)S(1)}, u32[]{:S(2)}, u32[]{:S(2)}) collective-permute-start(f32[48,1024]{1,0:T(8,128)S(1)} %get-tuple-element.80.mine), channel_id=1, source_target_pairs={{0,1},{1,0},{2,3},{3,2},{4,5},{5,4},{6,7},{7,6},{8,9},{9,8},{10,11... | collective-permute-start | bytes 589832 | tf_op jit(solution)/shard_map/ppermute | solution.py:39
  42.5 15.9 %collective-permute-start.19 = (f32[48,1024]{1,0:T(8,128)S(1)}, f32[48,1024]{1,0:T(8,128)S(1)}, u32[]{:S(2)}, u32[]{:S(2)}) collective-permute-start(f32[48,1024]{1,0:T(8,128)S(1)} %get-tuple-element.80.mine), channel_id=1, source_target_pairs={{0,24},{8,16},{16,8},{24,0},{1,25},{9,17},{17,9},{25,1},{2,26},{10... | collective-permute-start | bytes 589832 | tf_op jit(solution)/shard_map/ppermute | solution.py:39
  44.9 14.1 %collective-permute-start.18 = (f32[48,1024]{1,0:T(8,128)S(1)}, f32[48,1024]{1,0:T(8,128)S(1)}, u32[]{:S(2)}, u32[]{:S(2)}) collective-permute-start(f32[48,1024]{1,0:T(8,128)S(1)} %get-tuple-element.80.mine), channel_id=1, source_target_pairs={{0,16},{8,24},{16,0},{24,8},{1,17},{9,25},{17,1},{25,9},{2,18},{10... | collective-permute-start | bytes 589832 | tf_op jit(solution)/shard_map/ppermute | solution.py:39
  45.4 6.8 %collective-permute-start.4 = (f32[16,2048]{1,0:T(8,128)S(1)}, f32[16,2048]{1,0:T(8,128)S(1)}, u32[]{:S(2)}, u32[]{:S(2)}) collective-permute-start(f32[16,2048]{1,0:T(8,128)S(1)} %get-tuple-element.62), channel_id=1, source_target_pairs={{0,2},{2,0},{4,6},{6,4},{1,3},{3,1},{5,7},{7,5},{8,10},{10,8},{12,... | collective-permute-start | bytes 393224 | tf_op jit(solution)/shard_map/ppermute | solution.py:39
  46.4 8.9 %collective-permute-start.9 = (f32[16,2048]{1,0:T(8,128)S(1)}, f32[16,2048]{1,0:T(8,128)S(1)}, u32[]{:S(2)}, u32[]{:S(2)}) collective-permute-start(f32[16,2048]{1,0:T(8,128)S(1)} %get-tuple-element.73), channel_id=1, source_target_pairs={{0,4},{2,6},{4,0},{6,2},{1,5},{3,7},{5,1},{7,3},{8,12},{10,14},{12... | collective-permute-start | bytes 393224 | tf_op jit(solution)/shard_map/ppermute | solution.py:39
  49.8 9.2 %collective-permute-start.17 = (f32[48,1024]{1,0:T(8,128)S(1)}, f32[48,1024]{1,0:T(8,128)S(1)}, u32[]{:S(2)}, u32[]{:S(2)}) collective-permute-start(f32[48,1024]{1,0:T(8,128)S(1)} %get-tuple-element.80.mine), channel_id=1, source_target_pairs={{0,8},{8,0},{16,24},{24,16},{1,9},{9,1},{17,25},{25,17},{2,10},{10... | collective-permute-start | bytes 589832 | tf_op jit(solution)/shard_map/ppermute | solution.py:39
  55.5 6.0 %collective-permute-start.23 = (f32[32,1024]{1,0:T(8,128)S(1)}, f32[32,1024]{1,0:T(8,128)S(1)}, u32[]{:S(2)}, u32[]{:S(2)}) collective-permute-start(f32[32,1024]{1,0:T(8,128)S(1)} %get-tuple-element.88.mine), channel_id=1, source_target_pairs={{0,24},{8,16},{16,8},{24,0},{1,25},{9,17},{17,9},{25,1},{2,26},{10... | collective-permute-start | bytes 393224 | tf_op jit(solution)/shard_map/ppermute | solution.py:39
  57.2 5.7 %collective-permute-start.22 = (f32[32,1024]{1,0:T(8,128)S(1)}, f32[32,1024]{1,0:T(8,128)S(1)}, u32[]{:S(2)}, u32[]{:S(2)}) collective-permute-start(f32[32,1024]{1,0:T(8,128)S(1)} %get-tuple-element.88.mine), channel_id=1, source_target_pairs={{0,16},{8,24},{16,0},{24,8},{1,17},{9,25},{17,1},{25,9},{2,18},{10... | collective-permute-start | bytes 393224 | tf_op jit(solution)/shard_map/ppermute | solution.py:39
  58.4 5.0 %collective-permute-start.21 = (f32[32,1024]{1,0:T(8,128)S(1)}, f32[32,1024]{1,0:T(8,128)S(1)}, u32[]{:S(2)}, u32[]{:S(2)}) collective-permute-start(f32[32,1024]{1,0:T(8,128)S(1)} %get-tuple-element.88.mine), channel_id=1, source_target_pairs={{0,8},{8,0},{16,24},{24,16},{1,9},{9,1},{17,25},{25,17},{2,10},{10... | collective-permute-start | bytes 393224 | tf_op jit(solution)/shard_map/ppermute | solution.py:39
  65.1 10.7 %collective-permute-start.24 = (f32[256,128]{1,0:T(8,128)S(1)}, f32[256,128]{1,0:T(8,128)S(1)}, u32[]{:S(2)}, u32[]{:S(2)}) collective-permute-start(f32[256,128]{1,0:T(8,128)S(1)} %get-tuple-element.94), channel_id=1, source_target_pairs={{0,4},{2,6},{4,0},{6,2},{1,5},{3,7},{5,1},{7,3},{8,12},{10,14},{12... | collective-permute-start | bytes 393224 | tf_op jit(solution)/shard_map/ppermute | solution.py:39
  65.8 10.0 %collective-permute-start.25 = (f32[256,128]{1,0:T(8,128)S(1)}, f32[256,128]{1,0:T(8,128)S(1)}, u32[]{:S(2)}, u32[]{:S(2)}) collective-permute-start(f32[256,128]{1,0:T(8,128)S(1)} %get-tuple-element.95), channel_id=1, source_target_pairs={{0,6},{2,4},{4,2},{6,0},{1,7},{3,5},{5,3},{7,1},{8,14},{10,12},{12... | collective-permute-start | bytes 393224 | tf_op jit(solution)/shard_map/ppermute | solution.py:39
  68.3 7.6 %collective-permute-start.26 = (f32[256,128]{1,0:T(8,128)S(1)}, f32[256,128]{1,0:T(8,128)S(1)}, u32[]{:S(2)}, u32[]{:S(2)}) collective-permute-start(f32[256,128]{1,0:T(8,128)S(1)} %get-tuple-element.96), channel_id=1, source_target_pairs={{0,2},{2,0},{4,6},{6,4},{1,3},{3,1},{5,7},{7,5},{8,10},{10,8},{12,... | collective-permute-start | bytes 393224 | tf_op jit(solution)/shard_map/ppermute | solution.py:39
  (5 other events, 25.7 us)
